TPU v7x, 128 devices: a whole 4x4x4 slice. The times are simulated.
128 devices in a mesh: role: 2 (over core), rows: 16 (over z, y), heads: 4 (over x).
Axes of the slice: x: 4, y: 4, z: 4, core: 2. Of those that a mesh axis runs over, the one named last changes fastest.
Arguments:
- queries: bfloat16 [512, 2, 4, 1024], P('rows', 'role', 'heads'), may hold values from -9 to 9
- k_cache: bfloat16 [512, 4, 512, 128], P('rows', 'heads'), may hold values from -6 to 6
- value_cache: bfloat16 [512, 4, 512, 128], P('rows', 'heads'), may hold values from -6 to 6
- new_token_key: bfloat16 [512, 4, 128], P('rows', 'heads'), may hold values from -6 to 6
- new_token_value: bfloat16 [512, 4, 128], P('rows', 'heads'), may hold values from -6 to 6
- lengths: int32 [512], P('rows'), may hold values from 2 to 512, as said below
- output_weight: bfloat16 [2, 4, 1024, 4096], P('role', 'heads'), may hold values from -0.5 to 0.5
- residual: bfloat16 [512, 4096], P('rows'), may hold values from -60 to 60
- norm_gain: float32 [4096], replicated, may hold values from 0.5 to 2
- routes: int32 [512, 8], P('rows'), may hold values from 0 to 63, all different within a row; in each aligned block of 32 rows (0 to 31, 32 to 63, ...) at most 8 rows name the same one
- route_scores: float32 [512, 8], P('rows'), may hold values from 0.05 to 1
- w_gate: bfloat16 [64, 4096, 1024], P(('role', 'rows'), None, 'heads'), may hold values from -0.09375 to 0.09375
- w_up: bfloat16 [64, 4096, 1024], P(('role', 'rows'), None, 'heads'), may hold values from -0.09375 to 0.09375
- w_down: bfloat16 [64, 1024, 4096], P(('role', 'rows'), 'heads'), may hold values from -0.1875 to 0.1875
Outputs:
- final: bfloat16 [512, 4096], P('rows', ('role', 'heads'))
Inputs may be any that keep to these rules, and one draw needn't show every extreme that they name: `lengths`: at least one row holds 512 cached positions. `routes`: each row names 8 different experts; the 32 rows of one index of rows name no expert more than 8 times, a bound that some block reaches.
All inputs are finite; a program needn't handle non-finite values.
Results may differ from a plain program's by a relative error of at most 0.015.
Values may be sent and summed in bfloat16 or wider, within the bound.
No kernel may reach another device: no remote copies, remote signals or barrier semaphores. Data moves between devices by JAX's collectives and lax.ppermute only.
A program may use at most 128 MiB of HBM per device.

v0:
```python
import math

import jax
import jax.numpy as jnp
from jax import lax
from jax.sharding import PartitionSpec as P


def per_device(
    queries,
    k_cache,
    value_cache,
    new_token_key,
    new_token_value,
    lengths,
    output_weight,
    residual,
    norm_gain,
    routes,
    route_scores,
    w_gate,
    w_up,
    w_down,
):
    rows_here = queries.shape[0]
    head_size = k_cache.shape[3]
    cache_len = k_cache.shape[2]
    per_group = queries.shape[3] // head_size
    root = math.sqrt(head_size)
    query_vectors = queries[:, 0, 0].reshape(rows_here, per_group, head_size)
    key_rows = k_cache[:, 0]
    value_rows = value_cache[:, 0]
    scores = (
        jnp.einsum("rqd,rld->rql", query_vectors, key_rows, preferred_element_type=jnp.float32)
        / root
    )
    fresh = (
        jnp.einsum(
            "rqd,rd->rq", query_vectors, new_token_key[:, 0], preferred_element_type=jnp.float32
        )
        / root
    )
    valid = lax.broadcasted_iota(jnp.int32, (rows_here, cache_len), 1) < lengths[:, None]
    scores = jnp.where(valid[:, None, :], scores, -jnp.inf)
    top = jnp.maximum(jnp.max(scores, axis=-1), fresh)
    expo = jnp.exp(scores - top[..., None])
    expo_new = jnp.exp(fresh - top)
    denom = jnp.sum(expo, axis=-1) + expo_new
    probs = (expo / denom[..., None]).astype(jnp.bfloat16)
    probs_new = (expo_new / denom).astype(jnp.bfloat16)
    attention_result = jnp.einsum(
        "rql,rld->rqd", probs, value_rows, preferred_element_type=jnp.float32
    )
    attention_result = (
        attention_result
        + probs_new.astype(jnp.float32)[..., None]
        * new_token_value[:, 0].astype(jnp.float32)[:, None, :]
    )
    attention_result = attention_result.astype(jnp.bfloat16).reshape(
        rows_here, per_group * head_size
    )
    partial_out = jnp.dot(attention_result, output_weight[0, 0], preferred_element_type=jnp.float32)
    width = residual.shape[1]
    roles = lax.axis_size("role")
    heads_count = lax.axis_size("heads")
    piece = width // (roles * heads_count)
    head_place = lax.axis_index("heads")
    place = lax.axis_index("role") * heads_count + head_place
    total = lax.psum(partial_out.astype(jnp.bfloat16), ("role", "heads")).astype(jnp.float32)
    hidden = residual.astype(jnp.float32) + total
    meansq = jnp.mean(hidden * hidden, axis=1, keepdims=True)
    normed = (hidden * lax.rsqrt(meansq + 1e-06) * norm_gain).astype(jnp.bfloat16)
    hidden_part = lax.dynamic_slice_in_dim(hidden, place * piece, piece, 1)
    top_k = routes.shape[1]
    per_dev = w_gate.shape[0]
    shards = lax.axis_size("rows")
    experts = per_dev * shards * roles
    capacity = max(2, 2 * rows_here * top_k // experts)
    slots = shards * per_dev * capacity
    picks = rows_here * top_k
    flat = routes.reshape(picks)
    order = jnp.arange(picks, dtype=jnp.int32)
    earlier = jnp.sum(
        ((flat[None, :] == flat[:, None]) & (order[None, :] < order[:, None])).astype(jnp.int32),
        axis=1,
    )
    owner = flat // (per_dev * shards)
    target = flat // per_dev % shards
    local = flat % per_dev
    slot_id = jnp.where(
        owner == lax.axis_index("role"), (target * per_dev + local) * capacity + earlier, -1
    )
    table = (slot_id[None, :] == jnp.arange(slots, dtype=jnp.int32)[:, None]).reshape(
        slots, rows_here, top_k
    )
    pick_rows = jnp.any(table, axis=2).astype(jnp.bfloat16)
    shares = route_scores / jnp.sum(route_scores, axis=1, keepdims=True)
    mixing = jnp.sum(jnp.where(table, shares[None, :, :], jnp.float32(0.0)), axis=2).T
    outgoing = jnp.dot(pick_rows, normed, preferred_element_type=jnp.float32).astype(jnp.bfloat16)
    outgoing = outgoing.reshape(shards, per_dev, capacity, width)
    incoming = lax.all_to_all(outgoing, "rows", split_axis=0, concat_axis=0, tiled=True)
    gate = jnp.einsum("secd,edf->secf", incoming, w_gate, preferred_element_type=jnp.float32)
    upper = jnp.einsum("secd,edf->secf", incoming, w_up, preferred_element_type=jnp.float32)
    act = (jax.nn.silu(gate) * upper).astype(jnp.bfloat16)
    result = jnp.einsum("secf,efd->secd", act, w_down, preferred_element_type=jnp.float32).astype(
        jnp.bfloat16
    )
    returned = lax.all_to_all(result, "rows", split_axis=0, concat_axis=0, tiled=True)
    flat_back = returned.reshape(slots, width)
    mix_high = mixing.astype(jnp.bfloat16)
    mix_low = (mixing - mix_high.astype(jnp.float32)).astype(jnp.bfloat16)
    mixed = jnp.dot(mix_high, flat_back, preferred_element_type=jnp.float32) + jnp.dot(
        mix_low, flat_back, preferred_element_type=jnp.float32
    )
    moe = lax.psum_scatter(
        mixed.astype(jnp.bfloat16), ("role", "heads"), scatter_dimension=1, tiled=True
    ).astype(jnp.float32)
    return (hidden_part + moe).astype(jnp.bfloat16)


def solution(mesh):
    in_specs = (
        P("rows", "role", "heads", None),
        P("rows", "heads", None, None),
        P("rows", "heads", None, None),
        P("rows", "heads", None),
        P("rows", "heads", None),
        P("rows"),
        P("role", "heads", None, None),
        P("rows", None),
        P(),
        P("rows", None),
        P("rows", None),
        P(("role", "rows"), None, "heads"),
        P(("role", "rows"), None, "heads"),
        P(("role", "rows"), "heads", None),
    )
    out_specs = P("rows", ("role", "heads"))
    return jax.shard_map(
        per_device, mesh=mesh, in_specs=in_specs, out_specs=out_specs, check_vma=False
    )
```

profile of v0, /device:TPU:1, one launch (start us, length us, event | category | flops | bytes accessed | tf_op | source)
XLA Modules:
  0.0 201.6 jit_solution(10474719294296749391)
XLA Ops:
  6.5 0.9 copy.49
  7.4 0.7 iota_compare_fusion.2
  8.2 0.1 fusion.79
  8.3 3.6 %fusion.88 = (f32[32,8]{1,0:T(8,128)S(1)}, f32[32,8,512]{2,1,0:T(8,128)S(1)}) fusion(bf16[32,8,128]{2,1,0:T(8,128)(2,1)S(1)} %bitcast.106, bf16[32,1,512,128]{3,2,1,0:T(8,128)(2,1)} %param.15, pred[32,512]{1,0:T(8,128)(4,1)S(1)} %iota_compare_fusion.2), kind=kOutput, calls=%fused_computation.90 | convolution fusion | flops 33947392 | bytes 4801536 | tf_op jit(solution)/shard_map/rqd,rld->rql/dot_general | solution.py:34
  11.9 0.2 fusion.50
  12.2 2.9 %fusion.47 = bf16[32,8,128]{2,1,0:T(8,128)(2,1)S(1)} fusion(bf16[32,1,512,128]{3,2,1,0:T(8,128)(2,1)} %param.16, f32[32,8,512]{2,1,0:T(8,128)S(1)} %get-tuple-element.10, f32[32,8]{1,0:T(8,128)S(1)} %get-tuple-element.8, f32[32,8]{1,0:T(8,128)S(1)} %multiply_maximum_fusion, f32[32,128]{1,0:T(8,128)S(1)} %bitcast_convert_fusion.3, ...), kind=kOutput, calls=%fused_computation.26 | convolution fusion | flops 34045952 | bytes 4803584 | tf_op jit(solution)/shard_map/rql,rld->rqd/dot_general | solution.py:51
  15.2 2.2 %fusion.4 = bf16[32,4096]{1,0:T(8,128)(2,1)} fusion(bf16[1,1,1024,4096]{3,2,1,0:T(8,128)(2,1)S(1)} %copy-done.1, bf16[4,8,8,128]{3,2,1,0:T(8,128)(2,1)S(1)} %bitcast.104), kind=kOutput, calls=%fused_computation.7 | convolution fusion | flops 268566528 | bytes 8716288 | tf_op jit(solution)/shard_map/dot_general | solution.py:62
  17.6 0.1 eq.42
  17.6 0.2 convert_reduce_fusion
  18.0 0.2 fusion.62
  18.1 60.4 %all-reduce.2.cloned.1.call-done = bf16[32,4096]{1,0:T(8,128)(2,1)} async-done(((bf16[32,4096]{1,0:T(8,128)(2,1)}), bf16[32,4096]{1,0:T(8,128)(2,1)}) %all-reduce.2.cloned.1.call-update) | async-done | bytes 262160 | tf_op jit(solution)/shard_map/psum | solution.py:69
  78.5 1.3 convert_add_fusion
  79.8 1.7 convolution_convert_fusion.1
  81.6 31.8 %all_to_all.10 = bf16[16,2,8,4096]{3,2,1,0:T(8,128)(2,1)S(1)} all-to-all(bf16[16,2,8,4096]{3,2,1,0:T(8,128)(2,1)S(1)} %bitcast.103), channel_id=1, replica_groups=mesh['role'=2,'rows'=16,'heads'=4] {'rows'}, dimensions={0} | all-to-all | bytes 4194304 | tf_op jit(solution)/shard_map/all_to_all | solution.py:101
  113.4 0.8 fusion.24
  114.1 6.3 %fusion.2 = bf16[16,2,8,4096]{3,2,0,1:T(8,128)(2,1)} fusion(bf16[2,256,4096]{2,1,0:T(8,128)(2,1)} %param.27, bf16[2,4096,256]{2,1,0:T(8,128)(2,1)} %param.26, bf16[16,2,8,4096]{3,2,1,0:T(8,128)(2,1)S(1)} %all_to_all.10, f32[16,2,8,256]{3,2,0,1:T(8,128)S(1)} %fusion.24), kind=kOutput, calls=%fused_computation.4 | convolution fusion | flops 1075183616 | bytes 12845056 | tf_op jit(solution)/shard_map/secf,efd->secd/dot_general | solution.py:105
  120.4 3.1 %copy.43 = bf16[16,2,8,4096]{3,2,1,0:T(8,128)(2,1)} copy(bf16[16,2,8,4096]{3,2,0,1:T(8,128)(2,1)} %fusion.2) | data formatting | bytes 4194304 | tf_op jit(solution)/shard_map/convert_element_type | solution.py:105
  123.5 3.7 %all-to-all-start.1 = ((bf16[16,2,8,4096]{3,2,1,0:T(8,128)(2,1)}), bf16[16,2,8,4096]{3,2,1,0:T(8,128)(2,1)S(1)}, u32[]{:S(2)}, u32[]{:S(2)}) async-start(bf16[16,2,8,4096]{3,2,1,0:T(8,128)(2,1)} %copy.43), calls=%async_computation.1 | async-start | bytes 4194304 | tf_op jit(solution)/shard_map/all_to_all | solution.py:108
  127.4 0.2 select_reduce_fusion
  127.6 24.4 %all-to-all-done.1 = bf16[16,2,8,4096]{3,2,1,0:T(8,128)(2,1)S(1)} async-done(((bf16[16,2,8,4096]{3,2,1,0:T(8,128)(2,1)}), bf16[16,2,8,4096]{3,2,1,0:T(8,128)(2,1)S(1)}, u32[]{:S(2)}, u32[]{:S(2)}) %all-to-all-start.1) | async-done | bytes 2097184 | tf_op jit(solution)/shard_map/all_to_all | solution.py:108
  152.0 0.5 fusion.89
  152.5 1.2 fusion.3
  153.7 39.7 %reduce-scatter.2.cloned.1.call-done = bf16[32,512]{1,0:T(8,128)(2,1)} async-done(((bf16[32,4096]{1,0:T(8,128)(2,1)}), bf16[32,512]{1,0:T(8,128)(2,1)}) %reduce-scatter.2.cloned.1.call-update) | async-done | bytes 32784 | tf_op jit(solution)/shard_map/reduce_scatter | solution.py:115
  193.4 1.4 add_convert_fusion
  (30 shorter events, 0.5 us)
Async XLA Ops:
  6.5 1.6 copy-start
  6.5 5.7 %copy-start.6 = (bf16[32,1,128]{2,0,1:T(8,128)(2,1)S(1)}, bf16[32,1,128]{2,0,1:T(8,128)(2,1)}, u32[]{:S(2)}) copy-start(bf16[32,1,128]{2,0,1:T(8,128)(2,1)} %param.18) | copy-start | bytes 24580
  6.5 71.9 %all-reduce.2.cloned.1.call-start = ((), (), s32[]{:S(2)}) async-start(), calls=%async_computation.3 | async-start | bytes 524288 | tf_op jit(solution)/shard_map/psum | solution.py:69
  8.3 6.8 %copy-start.1 = (bf16[1,1,1024,4096]{3,2,1,0:T(8,128)(2,1)S(1)}, bf16[1,1,1024,4096]{3,2,1,0:T(8,128)(2,1)}, u32[]{:S(2)}) copy-start(bf16[1,1,1024,4096]{3,2,1,0:T(8,128)(2,1)} %param.20) | copy-start | bytes 25165828
  15.1 2.3 %copy-start.7 = (s32[32,8]{0,1:T(8,128)S(1)}, s32[32,8]{0,1:T(8,128)}, u32[]{:S(2)}) copy-start(s32[32,8]{0,1:T(8,128)} %param.23) | copy-start | bytes 3076
  15.2 63.3 %copy-start.3 = (bf16[32,4096]{1,0:T(8,128)(2,1)S(1)}, bf16[32,4096]{1,0:T(8,128)(2,1)}, u32[]{:S(2)}) copy-start(bf16[32,4096]{1,0:T(8,128)(2,1)} %param.21) | copy-start | bytes 786436
  15.2 64.6 %copy-start.4 = (f32[4096]{0:T(1024)S(1)}, f32[4096]{0:T(1024)}, u32[]{:S(2)}) copy-start(f32[4096]{0:T(1024)} %param.22) | copy-start | bytes 49156
  78.5 34.9 %copy-start.2 = (bf16[2,4096,256]{2,1,0:T(8,128)(2,1)S(1)}, bf16[2,4096,256]{2,1,0:T(8,128)(2,1)}, u32[]{:S(2)}) copy-start(bf16[2,4096,256]{2,1,0:T(8,128)(2,1)} %param.25) | copy-start | bytes 12582916
  120.4 6.9 %copy-start.5 = (f32[32,8]{0,1:T(8,128)S(1)}, f32[32,8]{0,1:T(8,128)}, u32[]{:S(2)}) copy-start(f32[32,8]{0,1:T(8,128)} %param.24) | copy-start | bytes 3076
  123.5 28.5 %all-to-all-start.1 = ((bf16[16,2,8,4096]{3,2,1,0:T(8,128)(2,1)}), bf16[16,2,8,4096]{3,2,1,0:T(8,128)(2,1)S(1)}, u32[]{:S(2)}, u32[]{:S(2)}) async-start(bf16[16,2,8,4096]{3,2,1,0:T(8,128)(2,1)} %copy.43), calls=%async_computation.1 | async-start | bytes 4194304 | tf_op jit(solution)/shard_map/all_to_all | solution.py:108
  127.3 66.1 %reduce-scatter.2.cloned.1.call-start = ((), (), s32[]{:S(2)}) async-start(), calls=%async_computation.4 | async-start | bytes 294912 | tf_op jit(solution)/shard_map/reduce_scatter | solution.py:115
Sparse Core Ops, SparseCore 0:
  17.6 60.8 all-reduce.1
  153.8 39.5 reduce-scatter.1
where the time goes:
time: 202 us
  waiting for transfers between devices  124 us (61%)
  blocking collectives  31.8 us (16%)
  matrix products  19.3 us (10%)
  between operations  13.6 us (7%)
  local copies, waits for them, and re-layouts  4.36 us (2%)
  other arithmetic  4.28 us (2%)
  starting transfers between devices  3.76 us (2%)
    psum x1, waiting for transfers between devices, per_device(): lax.psum(partial_out.astype(jnp.bfloat16), ('role', 'heads'))  60.4 us
    reduce_scatter x1, waiting for transfers between devices, per_device(): lax.psum_scatter(mixed.astype(jnp.bfloat16), ('role', 'heads'), scatter_d...  39.7 us
    all_to_all x1, blocking collectives, per_device(): lax.all_to_all(outgoing, 'rows', split_axis=0, concat_axis=0, tiled=True)  31.8 us
    all_to_all x1, waiting for transfers between devices, per_device(): lax.all_to_all(result, 'rows', split_axis=0, concat_axis=0, tiled=True)  24.4 us
    dot_general x1, matrix products, per_device(): jnp.einsum('secf,efd->secd', act, w_down, preferred_element_type=jnp.floa...  6.3 us
  transfers between devices with their start and end apart: 3, of which 3 were waited for; matrix products, arithmetic and copies ran while one was open for 0% of the time, Pallas kernels for 0%

commit v1 on v0

v1 whole, which is shorter than its diff:
```python
import math

import jax
import jax.numpy as jnp
from jax import lax
from jax.sharding import PartitionSpec as P

BF = jnp.bfloat16
F32 = jnp.float32
EPS = 1e-06


def attention(queries, k_cache, value_cache, new_token_key, new_token_value, lengths):
    rows_here = queries.shape[0]
    head_size = k_cache.shape[3]
    cache_len = k_cache.shape[2]
    per_group = queries.shape[3] // head_size
    root = math.sqrt(head_size)
    query_vectors = queries[:, 0, 0].reshape(rows_here, per_group, head_size)
    scores = jnp.einsum("rqd,rld->rql", query_vectors, k_cache[:, 0], preferred_element_type=F32)
    scores = scores / root
    fresh = jnp.einsum("rqd,rd->rq", query_vectors, new_token_key[:, 0], preferred_element_type=F32)
    fresh = fresh / root
    valid = lax.broadcasted_iota(jnp.int32, (rows_here, cache_len), 1) < lengths[:, None]
    scores = jnp.where(valid[:, None, :], scores, -jnp.inf)
    top = jnp.maximum(jnp.max(scores, axis=-1), fresh)
    expo = jnp.exp(scores - top[..., None])
    expo_new = jnp.exp(fresh - top)
    denom = jnp.sum(expo, axis=-1) + expo_new
    probs = (expo / denom[..., None]).astype(BF)
    probs_new = (expo_new / denom).astype(BF)
    result = jnp.einsum("rql,rld->rqd", probs, value_cache[:, 0], preferred_element_type=F32)
    result = result + probs_new.astype(F32)[..., None] * new_token_value[:, 0].astype(F32)[:, None]
    return result.astype(BF).reshape(rows_here, per_group * head_size)


def per_device(
    queries,
    k_cache,
    value_cache,
    new_token_key,
    new_token_value,
    lengths,
    output_weight,
    residual,
    norm_gain,
    routes,
    route_scores,
    w_gate,
    w_up,
    w_down,
):
    rows_here = queries.shape[0]
    width = residual.shape[1]
    roles = lax.axis_size("role")
    heads_count = lax.axis_size("heads")
    shards = lax.axis_size("rows")
    half = width // roles
    piece = half // heads_count
    per_dev, _, quarter = w_gate.shape
    experts = per_dev * shards * roles
    capacity = 8
    role = lax.axis_index("role")
    head = lax.axis_index("heads")
    swap = [(i, roles - 1 - i) for i in range(roles)]

    def shift(x, step):
        return lax.ppermute(
            x, "heads", [(i, (i + step) % heads_count) for i in range(heads_count)]
        )

    down = w_down.reshape(per_dev, quarter, roles, heads_count, piece)
    downs = []
    for step in range(heads_count):
        part = lax.dynamic_slice_in_dim(down, (head + step) % heads_count, 1, 3)
        part = part.reshape(per_dev, quarter, roles * piece)
        downs.append(part if step == 0 else shift(part, step))

    attended = attention(
        queries, k_cache, value_cache, new_token_key, new_token_value, lengths
    )
    partial = jnp.dot(attended, output_weight[0, 0], preferred_element_type=F32)
    low, high = partial[:, :half], partial[:, half:]
    first = role == 0
    theirs = jnp.where(first, high, low).astype(BF)
    mine = jnp.where(first, low, high)
    chip = (mine + lax.ppermute(theirs, "role", swap).astype(F32)).astype(BF)
    total = chip.astype(F32)
    for step in range(1, heads_count):
        total = total + shift(chip, step).astype(F32)
    resid = jnp.where(first, residual[:, :half], residual[:, half:]).astype(F32)
    gain = jnp.where(first, norm_gain[:half], norm_gain[half:])
    hidden = resid + total
    scaled = (hidden * gain).astype(BF)

    named = routes[:, :, None] == jnp.arange(experts, dtype=jnp.int32)
    chosen = jnp.any(named, axis=1)
    shares = route_scores / jnp.sum(route_scores, axis=1, keepdims=True)
    coef = jnp.sum(jnp.where(named, shares[:, :, None], F32(0.0)), axis=1)
    order = jnp.arange(rows_here, dtype=jnp.int32)
    before = (order[None, :] < order[:, None]).astype(BF)
    rank = jnp.dot(before, chosen.astype(BF), preferred_element_type=F32).astype(jnp.int32)
    taken = chosen[:, :, None] & (rank[:, :, None] == jnp.arange(capacity, dtype=jnp.int32))
    slots = experts * capacity
    pick = taken.reshape(rows_here, slots).astype(BF)
    mixing = jnp.where(taken, coef[:, :, None], F32(0.0)).reshape(rows_here, slots)

    outgoing = lax.dot_general(
        pick, scaled, (((0,), (0,)), ((), ())), preferred_element_type=F32
    ).astype(BF)
    outgoing = outgoing.reshape(roles * shards, per_dev * capacity, half)
    incoming = lax.all_to_all(outgoing, ("role", "rows"), 0, 0, tiled=True)
    incoming = incoming.reshape(roles, shards, per_dev, capacity, half)

    plain = incoming.astype(F32) / norm_gain.reshape(roles, 1, 1, 1, half)
    meansq = jnp.sum(plain * plain, axis=(0, 4)) / width
    inverse = lax.rsqrt(meansq + EPS)
    inverse = inverse.transpose(1, 0, 2).reshape(per_dev, shards * capacity, 1)
    tokens = incoming.transpose(2, 0, 1, 3, 4).reshape(per_dev, roles, shards * capacity, half)

    def project(weight):
        weight = weight.reshape(per_dev, roles, half, quarter)
        value = jnp.einsum("esd,edf->esf", tokens[:, 0], weight[:, 0], preferred_element_type=F32)
        for s in range(1, roles):
            value = value + jnp.einsum(
                "esd,edf->esf", tokens[:, s], weight[:, s], preferred_element_type=F32
            )
        return value * inverse

    act = (jax.nn.silu(project(w_gate)) * project(w_up)).astype(BF)
    result = jnp.einsum("esf,efd->esd", act, downs[0], preferred_element_type=F32)
    for step in range(1, heads_count):
        result = result + jnp.einsum(
            "esf,efd->esd", shift(act, step), downs[step], preferred_element_type=F32
        )
    result = result.astype(BF).reshape(per_dev, shards, capacity, roles, piece)
    result = result.transpose(3, 1, 0, 2, 4).reshape(roles * shards, per_dev * capacity, piece)
    returned = lax.all_to_all(result, ("role", "rows"), 0, 0, tiled=True)
    returned = returned.reshape(slots, piece)
    mix_high = mixing.astype(BF)
    mix_low = (mixing - mix_high.astype(F32)).astype(BF)
    moe = jnp.dot(mix_high, returned, preferred_element_type=F32) + jnp.dot(
        mix_low, returned, preferred_element_type=F32
    )
    own = lax.dynamic_slice_in_dim(hidden, head * piece, piece, 1)
    return (own + moe).astype(BF)


def solution(mesh):
    in_specs = (
        P("rows", "role", "heads", None),
        P("rows", "heads", None, None),
        P("rows", "heads", None, None),
        P("rows", "heads", None),
        P("rows", "heads", None),
        P("rows"),
        P("role", "heads", None, None),
        P("rows", None),
        P(),
        P("rows", None),
        P("rows", None),
        P(("role", "rows"), None, "heads"),
        P(("role", "rows"), None, "heads"),
        P(("role", "rows"), "heads", None),
    )
    out_specs = P("rows", ("role", "heads"))
    return jax.shard_map(
        per_device, mesh=mesh, in_specs=in_specs, out_specs=out_specs, check_vma=False
    )
```

time: 202 us -> 167 us (0.83)
  waiting for transfers between devices: 124 us -> 55.9 us
  local copies, waits for them, and re-layouts: 4.36 us -> 55.3 us
  blocking collectives: 31.8 us -> 0 us
  starting transfers between devices: 3.76 us -> 27.4 us
  between operations: 13.6 us -> 0.35 us
  matrix products: 19.3 us -> 25.3 us
  other arithmetic: 4.28 us -> 2.21 us
    psum x1 -> x0, waiting for transfers between devices: 60.4 us -> none  [per_device(): lax.psum(partial_out.astype(jnp.bfloat16), ('role', 'heads'))]
    ppermute x0 -> x10, waiting for transfers between devices: none -> 45.2 us  [the longest x9 44.8 us: shift(): lax.ppermute(x, 'heads', [(i, (i + step) % heads_count) for i in range(he...]
    reduce_scatter x1 -> x0, waiting for transfers between devices: 39.7 us -> none  [per_device(): lax.psum_scatter(mixed.astype(jnp.bfloat16), ('role', 'heads'), scatter_d...]
    dynamic_slice x0 -> x1, local copies, waits for them, and re-layouts: none -> 34.9 us  [per_device(): part = lax.dynamic_slice_in_dim(down, (head + step) % heads_count, 1, 3)]
    all_to_all x1 -> x0, blocking collectives: 31.8 us -> none  [per_device(): lax.all_to_all(outgoing, 'rows', split_axis=0, concat_axis=0, tiled=True)]
    reshape x0 -> x7, local copies, waits for them, and re-layouts: none -> 18.7 us  [the longest x4 8.51 us: per_device(): part = part.reshape(per_dev, quarter, roles * piece)]
    all_to_all x1 -> x2, starting transfers between devices: 3.72 us -> 18.2 us  [the longest x1 9.64 us: per_device(): returned = lax.all_to_all(result, ('role', 'rows'), 0, 0, tiled=True)]
    all_to_all x1 -> x2, waiting for transfers between devices: 24.4 us -> 10.8 us  [the longest x1 10.7 us: per_device(): returned = lax.all_to_all(result, ('role', 'rows'), 0, 0, tiled=True)]
  transfers between devices with their start and end apart: 3 -> 12, of which waited for: 3 -> 7; matrix products, arithmetic and copies ran while one was open for 0% -> 38% of each run, Pallas kernels for 0% -> 0%
where the time goes in v1:
time: 167 us
  waiting for transfers between devices  55.9 us (33%)
  local copies, waits for them, and re-layouts  55.3 us (33%)
  starting transfers between devices  27.4 us (16%)
  matrix products  25.3 us (15%)
  other arithmetic  2.21 us (1%)
    ppermute x9, waiting for transfers between devices, shift(): lax.ppermute(x, 'heads', [(i, (i + step) % heads_count) for i in range(he...  44.8 us
    dynamic_slice x1, local copies, waits for them, and re-layouts, per_device(): part = lax.dynamic_slice_in_dim(down, (head + step) % heads_count, 1, 3)  34.9 us
    all_to_all x1, waiting for transfers between devices, per_device(): returned = lax.all_to_all(result, ('role', 'rows'), 0, 0, tiled=True)  10.7 us
    all_to_all x1, starting transfers between devices, per_device(): returned = lax.all_to_all(result, ('role', 'rows'), 0, 0, tiled=True)  9.64 us
    all_to_all x1, starting transfers between devices, per_device(): incoming = lax.all_to_all(outgoing, ('role', 'rows'), 0, 0, tiled=True)  8.6 us
    reshape x4, local copies, waits for them, and re-layouts, per_device(): part = part.reshape(per_dev, quarter, roles * piece)  8.51 us
    reshape x1, local copies, waits for them, and re-layouts, per_device(): down = w_down.reshape(per_dev, quarter, roles, heads_count, piece)  7.83 us
    ppermute x9, starting transfers between devices, shift(): lax.ppermute(x, 'heads', [(i, (i + step) % heads_count) for i in range(he...  7.69 us
  transfers between devices with their start and end apart: 12, of which 7 were waited for; matrix products, arithmetic and copies ran while one was open for 38% of the time, Pallas kernels for 0%

profile of v1, /device:TPU:1, one launch (start us, length us, event | category | flops | bytes accessed | tf_op | source)
XLA Modules:
  0.0 166.5 jit_solution(3235748828169451770)
XLA Ops:
  1.8 3.5 %fusion.69 = (f32[32,8]{1,0:T(8,128)S(1)}, f32[32,8,512]{2,1,0:T(8,128)S(1)}) fusion(bf16[32,8,128]{2,1,0:T(8,128)(2,1)S(1)} %bitcast.145, bf16[32,1,512,128]{3,2,1,0:T(8,128)(2,1)} %param.15, pred[32,512]{1,0:T(8,128)(4,1)S(1)} %iota_compare_fusion.2), kind=kOutput, calls=%fused_computation.95 | convolution fusion | flops 33947392 | bytes 4801536 | tf_op jit(solution)/shard_map/rqd,rld->rql/dot_general | solution.py:20
  5.5 2.9 %fusion.27 = bf16[32,8,128]{2,1,0:T(8,128)(2,1)S(1)} fusion(bf16[32,1,512,128]{3,2,1,0:T(8,128)(2,1)} %param.16, f32[32,8,512]{2,1,0:T(8,128)S(1)} %get-tuple-element.12, f32[32,8]{1,0:T(8,128)S(1)} %get-tuple-element.10, f32[32,8]{1,0:T(8,128)S(1)} %multiply_maximum_fusion, f32[32,128]{1,0:T(8,128)S(1)} %bitcast_convert_fusion, ...), kind=kOutput, calls=%fused_computation.34 | convolution fusion | flops 34045952 | bytes 4803584 | tf_op jit(solution)/shard_map/rql,rld->rqd/dot_general | solution.py:32
  8.5 5.0 %fusion = f32[32,4096]{1,0:T(8,128)S(1)} fusion(bf16[1,1,1024,4096]{3,2,1,0:T(8,128)(2,1)} %param.20, bf16[4,8,8,128]{3,2,1,0:T(8,128)(2,1)S(1)} %bitcast.143), kind=kOutput, calls=%fused_computation | convolution fusion | flops 268435456 | bytes 8978432 | tf_op jit(solution)/shard_map/dot_general | solution.py:82
  16.0 2.6 %collective-permute-start.3 = (bf16[32,2048]{1,0:T(8,128)(2,1)S(1)}, bf16[32,2048]{1,0:T(8,128)(2,1)S(1)}, u32[]{:S(2)}, u32[]{:S(2)}) collective-permute-start(bf16[32,2048]{1,0:T(8,128)(2,1)S(1)} %add_convert_fusion), channel_id=1, source_target_pairs={{0,3},{1,0},{2,1},{3,2},{4,7},{5,4},{6,5},{7,6},{8,11},{9,8},{10,9... | collective-permute-start | bytes 393224 | tf_op jit(solution)/shard_map/ppermute | solution.py:68
  19.8 4.1 %collective-permute-done.3 = bf16[32,2048]{1,0:T(8,128)(2,1)S(1)} collective-permute-done((bf16[32,2048]{1,0:T(8,128)(2,1)S(1)}, bf16[32,2048]{1,0:T(8,128)(2,1)S(1)}, u32[]{:S(2)}, u32[]{:S(2)}) %collective-permute-start.3) | collective-permute-done | bytes 131104 | tf_op jit(solution)/shard_map/ppermute | solution.py:68
  24.6 3.8 %collective-permute-done.1 = bf16[32,2048]{1,0:T(8,128)(2,1)S(1)} collective-permute-done((bf16[32,2048]{1,0:T(8,128)(2,1)S(1)}, bf16[32,2048]{1,0:T(8,128)(2,1)S(1)}, u32[]{:S(2)}, u32[]{:S(2)}) %collective-permute-start.1) | collective-permute-done | bytes 131104 | tf_op jit(solution)/shard_map/ppermute | solution.py:68
  28.5 2.1 %convolution_convert_fusion = bf16[512,2048]{1,0:T(8,128)(2,1)} fusion(f32[32,2048]{1,0:T(8,128)S(1)} %add_add_fusion, f32[2048]{0:T(1024)S(1)} %slice_select_fusion, s32[512]{0:T(512)S(1)} %eq.69, s32[32,64]{0,1:T(8,128)S(1)} %copy.52, pred[32,64]{0,1:T(8,128)(4,1)S(1)} %copy.51), kind=kOutput, calls=%fused_computation.7 | convolution fusion | flops 68321280 | bytes 2379776 | tf_op jit(solution)/shard_map/dot_general | solution.py:108
  30.6 8.6 %all-to-all-start = ((bf16[32,16,2048]{2,1,0:T(8,128)(2,1)}), bf16[32,16,2048]{2,1,0:T(8,128)(2,1)S(1)}, u32[]{:S(2)}, u32[]{:S(2)}) async-start(bf16[32,16,2048]{2,1,0:T(8,128)(2,1)} %bitcast.134), calls=%async_computation | async-start | bytes 4194304 | tf_op jit(solution)/shard_map/all_to_all | solution.py:112
  39.3 7.8 %reshape.160 = bf16[2,256,2,4,512]{4,3,2,1,0:T(4,128)(2,1)} reshape(bf16[2,256,4096]{2,1,0:T(8,128)(2,1)} %param.27) | data formatting | bytes 8388608 | tf_op jit(solution)/shard_map/reshape | solution.py:72
  47.1 34.9 %dynamic-slice_reduce_fusion.1 = (bf16[2,256,2,512]{3,2,1,0:T(2,128)(2,1)S(1)}, bf16[2,256,2,512]{3,2,1,0:T(2,128)(2,1)}, bf16[2,256,2,512]{3,2,1,0:T(2,128)(2,1)}, bf16[2,256,2,512]{3,2,1,0:T(2,128)(2,1)}) fusion(bf16[2,256,2,4,512]{4,3,2,1,0:T(4,128)(2,1)} %reshape.160, s32[]{:T(128)S(6)} %select_n.102, s32[]{:T(128)S(6)} %select_n.100, s32[]{:T(128)S(6)} %select_n.98, ...), kind=kLoop, calls=%fused_computation.18 | loop fusion | bytes 8388624 | tf_op jit(solution)/shard_map/dynamic_slice | solution.py:75
  82.0 2.6 %reshape.164 = bf16[2,256,1024]{2,1,0:T(8,128)(2,1)} reshape(bf16[2,256,2,512]{3,2,1,0:T(2,128)(2,1)} %get-tuple-element.8) | data formatting | bytes 2097152 | tf_op jit(solution)/shard_map/reshape | solution.py:76
  84.9 2.6 %reshape.162 = bf16[2,256,1024]{2,1,0:T(8,128)(2,1)} reshape(bf16[2,256,2,512]{3,2,1,0:T(2,128)(2,1)} %get-tuple-element.6) | data formatting | bytes 2097152 | tf_op jit(solution)/shard_map/reshape | solution.py:76
  88.6 1.5 reshape.163
  90.7 1.8 %reshape.161 = bf16[2,256,1024]{2,1,0:T(8,128)(2,1)S(1)} reshape(bf16[2,256,2,512]{3,2,1,0:T(2,128)(2,1)} %get-tuple-element.7) | data formatting | bytes 2097152 | tf_op jit(solution)/shard_map/reshape | solution.py:76
  95.1 2.5 %fusion.8 = f32[2,128,256]{2,1,0:T(8,128)S(1)} fusion(bf16[2,2,2048,256]{3,2,1,0:T(8,128)(2,1)} %bitcast.150, bf16[2,2,128,2048]{3,2,0,1:T(8,128)(2,1)} %bitcast.137), kind=kOutput, calls=%fused_computation.13 | convolution fusion | flops 268435456 | bytes 3407872 | tf_op jit(solution)/shard_map/esd,edf->esf/dot_general | solution.py:125
  97.6 2.1 %fusion.19 = f32[2,128,256]{2,1,0:T(8,128)S(1)} fusion(f32[2,128,256]{2,1,0:T(8,128)S(1)} %fusion.8, bf16[2,2,2048,256]{3,2,1,0:T(8,128)(2,1)} %bitcast.151, bf16[2,2,128,2048]{3,2,0,1:T(8,128)(2,1)S(1)} %bitcast.138, f32[2,128]{1,0:T(2,128)S(1)} %mul.65), kind=kOutput, calls=%fused_computation.28 | convolution fusion | flops 268566528 | bytes 3671040 | tf_op jit(solution)/shard_map/esd,edf->esf/dot_general | solution.py:123
  100.6 1.9 %collective-permute-start.8 = (bf16[2,128,256]{2,1,0:T(8,128)(2,1)S(1)}, bf16[2,128,256]{2,1,0:T(8,128)(2,1)S(1)}, u32[]{:S(2)}, u32[]{:S(2)}) collective-permute-start(bf16[2,128,256]{2,1,0:T(8,128)(2,1)S(1)} %fusion.23), channel_id=1, source_target_pairs={{0,3},{1,0},{2,1},{3,2},{4,7},{5,4},{6,5},{7,6},{8,11},{9,8},{10,9... | collective-permute-start | bytes 393224 | tf_op jit(solution)/shard_map/ppermute | solution.py:68
  102.9 11.1 %collective-permute-done.5 = bf16[2,256,1024]{2,1,0:T(8,128)(2,1)} collective-permute-done((bf16[2,256,1024]{2,1,0:T(8,128)(2,1)}, bf16[2,256,1024]{2,1,0:T(8,128)(2,1)}, u32[]{:S(2)}, u32[]{:S(2)}) %collective-permute-start.5) | collective-permute-done | bytes 1048608 | tf_op jit(solution)/shard_map/ppermute | solution.py:68
  114.0 25.1 %collective-permute-done.4 = bf16[2,128,256]{2,1,0:T(8,128)(2,1)S(1)} collective-permute-done((bf16[2,128,256]{2,1,0:T(8,128)(2,1)S(1)}, bf16[2,128,256]{2,1,0:T(8,128)(2,1)S(1)}, u32[]{:S(2)}, u32[]{:S(2)}) %collective-permute-start.4) | collective-permute-done | bytes 131104 | tf_op jit(solution)/shard_map/ppermute | solution.py:68
  139.1 1.5 convolution_add_fusion.1
  140.7 1.5 fusion.71
  142.3 1.6 fusion.11
  144.7 9.6 %all-to-all-start.1 = ((bf16[32,16,512]{2,1,0:T(8,128)(2,1)}), bf16[32,16,512]{2,1,0:T(8,128)(2,1)S(1)}, u32[]{:S(2)}, u32[]{:S(2)}) async-start(bf16[32,16,512]{2,1,0:T(8,128)(2,1)} %bitcast.30), calls=%async_computation.1 | async-start | bytes 1048576 | tf_op jit(solution)/shard_map/all_to_all | solution.py:138
  154.7 10.7 %all-to-all-done.1 = bf16[32,16,512]{2,1,0:T(8,128)(2,1)S(1)} async-done(((bf16[32,16,512]{2,1,0:T(8,128)(2,1)}), bf16[32,16,512]{2,1,0:T(8,128)(2,1)S(1)}, u32[]{:S(2)}, u32[]{:S(2)}) %all-to-all-start.1) | async-done | bytes 524320 | tf_op jit(solution)/shard_map/all_to_all | solution.py:138
  (69 shorter events, 14.6 us)
Async XLA Ops:
  0.0 1.6 copy-start
  0.0 5.5 %copy-start.5 = (bf16[32,1,128]{2,0,1:T(8,128)(2,1)S(1)}, bf16[32,1,128]{2,0,1:T(8,128)(2,1)}, u32[]{:S(2)}) copy-start(bf16[32,1,128]{2,0,1:T(8,128)(2,1)} %param.18) | copy-start | bytes 24580
  8.5 6.6 %copy-start.6 = (s32[32,8]{0,1:T(8,128)S(1)}, s32[32,8]{0,1:T(8,128)}, u32[]{:S(2)}) copy-start(s32[32,8]{0,1:T(8,128)} %param.23) | copy-start | bytes 3076
  8.5 11.3 %copy-start.3 = (f32[4096]{0:T(1024)S(1)}, f32[4096]{0:T(1024)}, u32[]{:S(2)}) copy-start(f32[4096]{0:T(1024)} %param.22) | copy-start | bytes 49156
  8.5 19.9 %copy-start.2 = (bf16[32,4096]{1,0:T(8,128)(2,1)S(1)}, bf16[32,4096]{1,0:T(8,128)(2,1)}, u32[]{:S(2)}) copy-start(bf16[32,4096]{1,0:T(8,128)(2,1)} %param.21) | copy-start | bytes 786436
  13.5 2.5 %collective-permute-start = (bf16[32,2048]{1,0:T(8,128)(2,1)S(1)}, bf16[32,2048]{1,0:T(8,128)(2,1)S(1)}, u32[]{:S(2)}, u32[]{:S(2)}) collective-permute-start(bf16[32,2048]{1,0:T(8,128)(2,1)S(1)} %select_convert_fusion.1), channel_id=1, source_target_pairs={{0,64},{64,0},{1,65},{65,1},{2,66},{66,2},{3,67},{67,3},{4,68},{68... | collective-permute-start | bytes 393224 | tf_op jit(solution)/shard_map/ppermute | solution.py:87
  16.0 7.8 %collective-permute-start.3 = (bf16[32,2048]{1,0:T(8,128)(2,1)S(1)}, bf16[32,2048]{1,0:T(8,128)(2,1)S(1)}, u32[]{:S(2)}, u32[]{:S(2)}) collective-permute-start(bf16[32,2048]{1,0:T(8,128)(2,1)S(1)} %add_convert_fusion), channel_id=1, source_target_pairs={{0,3},{1,0},{2,1},{3,2},{4,7},{5,4},{6,5},{7,6},{8,11},{9,8},{10,9... | collective-permute-start | bytes 393224 | tf_op jit(solution)/shard_map/ppermute | solution.py:68
  18.7 5.9 %collective-permute-start.2 = (bf16[32,2048]{1,0:T(8,128)(2,1)S(1)}, bf16[32,2048]{1,0:T(8,128)(2,1)S(1)}, u32[]{:S(2)}, u32[]{:S(2)}) collective-permute-start(bf16[32,2048]{1,0:T(8,128)(2,1)S(1)} %add_convert_fusion), channel_id=1, source_target_pairs={{0,2},{1,3},{2,0},{3,1},{4,6},{5,7},{6,4},{7,5},{8,10},{9,11},{10,... | collective-permute-start | bytes 393224 | tf_op jit(solution)/shard_map/ppermute | solution.py:68
  19.2 9.2 %collective-permute-start.1 = (bf16[32,2048]{1,0:T(8,128)(2,1)S(1)}, bf16[32,2048]{1,0:T(8,128)(2,1)S(1)}, u32[]{:S(2)}, u32[]{:S(2)}) collective-permute-start(bf16[32,2048]{1,0:T(8,128)(2,1)S(1)} %add_convert_fusion), channel_id=1, source_target_pairs={{0,1},{1,2},{2,3},{3,0},{4,5},{5,6},{6,7},{7,4},{8,9},{9,10},{10,1... | collective-permute-start | bytes 393224 | tf_op jit(solution)/shard_map/ppermute | solution.py:68
  30.6 61.9 %all-to-all-start = ((bf16[32,16,2048]{2,1,0:T(8,128)(2,1)}), bf16[32,16,2048]{2,1,0:T(8,128)(2,1)S(1)}, u32[]{:S(2)}, u32[]{:S(2)}) async-start(bf16[32,16,2048]{2,1,0:T(8,128)(2,1)} %bitcast.134), calls=%async_computation | async-start | bytes 4194304 | tf_op jit(solution)/shard_map/all_to_all | solution.py:112
  84.6 56.1 %collective-permute-start.9 = (bf16[2,256,1024]{2,1,0:T(8,128)(2,1)}, bf16[2,256,1024]{2,1,0:T(8,128)(2,1)}, u32[]{:S(2)}, u32[]{:S(2)}) collective-permute-start(bf16[2,256,1024]{2,1,0:T(8,128)(2,1)} %reshape.164), channel_id=1, source_target_pairs={{0,3},{1,0},{2,1},{3,2},{4,7},{5,4},{6,5},{7,6},{8,11},{9,8},{10,9... | collective-permute-start | bytes 3145736 | tf_op jit(solution)/shard_map/ppermute | solution.py:68
  87.5 26.5 %collective-permute-start.5 = (bf16[2,256,1024]{2,1,0:T(8,128)(2,1)}, bf16[2,256,1024]{2,1,0:T(8,128)(2,1)}, u32[]{:S(2)}, u32[]{:S(2)}) collective-permute-start(bf16[2,256,1024]{2,1,0:T(8,128)(2,1)} %reshape.162), channel_id=1, source_target_pairs={{0,1},{1,2},{2,3},{3,0},{4,5},{5,6},{6,7},{7,4},{8,9},{9,10},{10,1... | collective-permute-start | bytes 3145736 | tf_op jit(solution)/shard_map/ppermute | solution.py:68
  90.2 52.1 %collective-permute-start.7 = (bf16[2,256,1024]{2,1,0:T(8,128)(2,1)}, bf16[2,256,1024]{2,1,0:T(8,128)(2,1)}, u32[]{:S(2)}, u32[]{:S(2)}) collective-permute-start(bf16[2,256,1024]{2,1,0:T(8,128)(2,1)} %reshape.163), channel_id=1, source_target_pairs={{0,2},{1,3},{2,0},{3,1},{4,6},{5,7},{6,4},{7,5},{8,10},{9,11},{10,... | collective-permute-start | bytes 3145736 | tf_op jit(solution)/shard_map/ppermute | solution.py:68
  94.8 2.8 %copy-start.1 = (bf16[2,16,2,8,2048]{4,3,1,2,0:T(8,128)(2,1)S(1)}, bf16[2,16,2,8,2048]{4,3,1,2,0:T(8,128)(2,1)}, u32[]{:S(2)}) copy-start(bf16[2,16,2,8,2048]{4,3,1,2,0:T(8,128)(2,1)} %copy.87) | copy-start | bytes 6291460
  95.1 4.6 %copy-start.7 = (bf16[2,4096,256]{2,1,0:T(8,128)(2,1)S(1)}, bf16[2,4096,256]{2,1,0:T(8,128)(2,1)}, u32[]{:S(2)}) copy-start(bf16[2,4096,256]{2,1,0:T(8,128)(2,1)} %param.26) | copy-start | bytes 12582916
  100.6 40.1 %collective-permute-start.8 = (bf16[2,128,256]{2,1,0:T(8,128)(2,1)S(1)}, bf16[2,128,256]{2,1,0:T(8,128)(2,1)S(1)}, u32[]{:S(2)}, u32[]{:S(2)}) collective-permute-start(bf16[2,128,256]{2,1,0:T(8,128)(2,1)S(1)} %fusion.23), channel_id=1, source_target_pairs={{0,3},{1,0},{2,1},{3,2},{4,7},{5,4},{6,5},{7,6},{8,11},{9,8},{10,9... | collective-permute-start | bytes 393224 | tf_op jit(solution)/shard_map/ppermute | solution.py:68
  102.6 36.5 %collective-permute-start.4 = (bf16[2,128,256]{2,1,0:T(8,128)(2,1)S(1)}, bf16[2,128,256]{2,1,0:T(8,128)(2,1)S(1)}, u32[]{:S(2)}, u32[]{:S(2)}) collective-permute-start(bf16[2,128,256]{2,1,0:T(8,128)(2,1)S(1)} %fusion.23), channel_id=1, source_target_pairs={{0,1},{1,2},{2,3},{3,0},{4,5},{5,6},{6,7},{7,4},{8,9},{9,10},{10,1... | collective-permute-start | bytes 393224 | tf_op jit(solution)/shard_map/ppermute | solution.py:68
  114.0 28.3 %collective-permute-start.6 = (bf16[2,128,256]{2,1,0:T(8,128)(2,1)S(1)}, bf16[2,128,256]{2,1,0:T(8,128)(2,1)S(1)}, u32[]{:S(2)}, u32[]{:S(2)}) collective-permute-start(bf16[2,128,256]{2,1,0:T(8,128)(2,1)S(1)} %fusion.23), channel_id=1, source_target_pairs={{0,2},{1,3},{2,0},{3,1},{4,6},{5,7},{6,4},{7,5},{8,10},{9,11},{10,... | collective-permute-start | bytes 393224 | tf_op jit(solution)/shard_map/ppermute | solution.py:68
  140.7 13.7 %copy-start.4 = (f32[32,8]{0,1:T(8,128)S(1)}, f32[32,8]{0,1:T(8,128)}, u32[]{:S(2)}) copy-start(f32[32,8]{0,1:T(8,128)} %param.24) | copy-start | bytes 3076
  144.7 20.7 %all-to-all-start.1 = ((bf16[32,16,512]{2,1,0:T(8,128)(2,1)}), bf16[32,16,512]{2,1,0:T(8,128)(2,1)S(1)}, u32[]{:S(2)}, u32[]{:S(2)}) async-start(bf16[32,16,512]{2,1,0:T(8,128)(2,1)} %bitcast.30), calls=%async_computation.1 | async-start | bytes 1048576 | tf_op jit(solution)/shard_map/all_to_all | solution.py:138

commit v2 on v1

v2 whole, which is shorter than its diff:
```python
import math

import jax
import jax.numpy as jnp
from jax import lax
from jax.experimental import pallas as pl
from jax.experimental.pallas import tpu as pltpu
from jax.sharding import PartitionSpec as P

BF = jnp.bfloat16
F32 = jnp.float32
EPS = 1e-06
VMEM = 60 << 20


def whole(n):
    return [pl.BlockSpec(memory_space=pltpu.VMEM)] * n


def cut_down(w_down, head, heads_count, roles):
    per_dev, quarter, width = w_down.shape
    half = width // roles
    piece = half // heads_count

    def body(head_ref, w_ref, *rest):
        outs, sems = rest[:heads_count], rest[heads_count]
        copies = []
        for step in range(heads_count):
            place = lax.rem(head_ref[0] + step, heads_count)
            for s in range(roles):
                start = pl.multiple_of(s * half + place * piece, piece)
                copies.append(
                    pltpu.make_async_copy(
                        w_ref.at[:, :, pl.ds(start, piece)],
                        outs[step].at[:, :, pl.ds(s * piece, piece)],
                        sems.at[step * roles + s],
                    )
                )
        for copy in copies:
            copy.start()
        for copy in copies:
            copy.wait()

    shape = jax.ShapeDtypeStruct((per_dev, quarter, roles * piece), w_down.dtype)
    return pl.pallas_call(
        body,
        out_shape=[shape] * heads_count,
        in_specs=[pl.BlockSpec(memory_space=pltpu.SMEM), pl.BlockSpec(memory_space=pltpu.HBM)],
        out_specs=[pl.BlockSpec(memory_space=pltpu.HBM)] * heads_count,
        scratch_shapes=[pltpu.SemaphoreType.DMA((heads_count * roles,))],
        compiler_params=pltpu.CompilerParams(vmem_limit_bytes=VMEM),
        cost_estimate=pl.CostEstimate(
            flops=0, bytes_accessed=2 * w_down.size * 2, transcendentals=0
        ),
        name="cut_down",
    )(head.reshape(1), w_down)


def attend(queries, k_cache, value_cache, new_key, new_value, lengths, output_weight, other):
    rows, group, size = queries.shape
    cache = k_cache.shape[1]
    depth, width = output_weight.shape
    half = width // 2
    step = 8
    blocks = rows // step
    scale = 1.0 / math.sqrt(size)

    def body(
        other_ref, q_ref, k_hbm, v_hbm, nk_ref, nv_ref, len_ref, w_hbm,
        attn_ref, out_ref, k_ref, v_ref, w_ref, k_sem, v_sem, w_sem,
    ):
        def copy(hbm, ref, sem, i):
            place = pl.ds(i * step, step)
            return pltpu.make_async_copy(hbm.at[place], ref.at[place], sem.at[i])

        start = pl.multiple_of(other_ref[0] * half, half)
        weight = pltpu.make_async_copy(w_hbm.at[:, pl.ds(start, half)], w_ref, w_sem)
        for i in range(blocks):
            copy(k_hbm, k_ref, k_sem, i).start()
            copy(v_hbm, v_ref, v_sem, i).start()
        weight.start()
        for i in range(blocks):
            place = slice(i * step, (i + 1) * step)
            copy(k_hbm, k_ref, k_sem, i).wait()
            q = q_ref[place]
            scores = lax.dot_general(
                q, k_ref[place], (((2,), (2,)), ((0,), (0,))), preferred_element_type=F32
            )
            scores = scores * scale
            fresh = jnp.sum(
                q.astype(F32) * nk_ref[place].astype(F32)[:, None, :], axis=2, keepdims=True
            )
            fresh = fresh * scale
            position = lax.broadcasted_iota(jnp.int32, (step, group, cache), 2)
            limit = len_ref[place][:, :, None]
            scores = jnp.where(position < limit, scores, -jnp.inf)
            top = jnp.maximum(jnp.max(scores, axis=2, keepdims=True), fresh)
            expo = jnp.exp(scores - top)
            expo_new = jnp.exp(fresh - top)
            denom = jnp.sum(expo, axis=2, keepdims=True) + expo_new
            probs = (expo / denom).astype(BF)
            probs_new = (expo_new / denom).astype(BF).astype(F32)
            copy(v_hbm, v_ref, v_sem, i).wait()
            result = lax.dot_general(
                probs, v_ref[place], (((2,), (1,)), ((0,), (0,))), preferred_element_type=F32
            )
            result = result + probs_new * nv_ref[place].astype(F32)[:, None, :]
            attn_ref[place, :] = result.reshape(step, group * size).astype(BF)
        weight.wait()
        out_ref[...] = jnp.dot(
            attn_ref[...], w_ref[...], preferred_element_type=F32
        ).astype(BF)

    return pl.pallas_call(
        body,
        out_shape=[
            jax.ShapeDtypeStruct((rows, depth), BF),
            jax.ShapeDtypeStruct((rows, half), BF),
        ],
        in_specs=[
            pl.BlockSpec(memory_space=pltpu.SMEM),
            pl.BlockSpec(memory_space=pltpu.VMEM),
            pl.BlockSpec(memory_space=pltpu.HBM),
            pl.BlockSpec(memory_space=pltpu.HBM),
            pl.BlockSpec(memory_space=pltpu.VMEM),
            pl.BlockSpec(memory_space=pltpu.VMEM),
            pl.BlockSpec(memory_space=pltpu.VMEM),
            pl.BlockSpec(memory_space=pltpu.HBM),
        ],
        out_specs=whole(2),
        scratch_shapes=[
            pltpu.VMEM((rows, cache, size), BF),
            pltpu.VMEM((rows, cache, size), BF),
            pltpu.VMEM((depth, half), BF),
            pltpu.SemaphoreType.DMA((blocks,)),
            pltpu.SemaphoreType.DMA((blocks,)),
            pltpu.SemaphoreType.DMA,
        ],
        compiler_params=pltpu.CompilerParams(vmem_limit_bytes=57 << 20),
        cost_estimate=pl.CostEstimate(
            flops=2 * rows * depth * half, bytes_accessed=12 << 20, transcendentals=0
        ),
        name="attend",
    )(other.reshape(1), queries, k_cache, value_cache, new_key, new_value, lengths, output_weight)


def own_half(attended, output_weight, role):
    rows = attended.shape[0]
    depth, width = output_weight.shape
    half = width // 2

    def body(role_ref, a_ref, w_hbm, out_ref, w_ref, sem):
        start = pl.multiple_of(role_ref[0] * half, half)
        copy = pltpu.make_async_copy(w_hbm.at[:, pl.ds(start, half)], w_ref, sem)
        copy.start()
        copy.wait()
        out_ref[...] = jnp.dot(a_ref[...], w_ref[...], preferred_element_type=F32)

    return pl.pallas_call(
        body,
        out_shape=jax.ShapeDtypeStruct((rows, half), F32),
        in_specs=[
            pl.BlockSpec(memory_space=pltpu.SMEM),
            pl.BlockSpec(memory_space=pltpu.VMEM),
            pl.BlockSpec(memory_space=pltpu.HBM),
        ],
        out_specs=pl.BlockSpec(memory_space=pltpu.VMEM),
        scratch_shapes=[pltpu.VMEM((depth, half), BF), pltpu.SemaphoreType.DMA],
        compiler_params=pltpu.CompilerParams(vmem_limit_bytes=57 << 20),
        cost_estimate=pl.CostEstimate(
            flops=2 * rows * depth * half, bytes_accessed=4 << 20, transcendentals=0
        ),
        name="own_half",
    )(role.reshape(1), attended, output_weight)


def experts_act(tokens, gain, w_gate, w_up, capacity):
    roles, slots, half = tokens.shape
    per_dev, width, quarter = w_gate.shape

    def body(x_ref, gain_ref, g_hbm, u_hbm, act_ref, g_ref, u_ref, sems):
        copies = []
        for e in range(per_dev):
            for i, (hbm, ref) in enumerate(((g_hbm, g_ref), (u_hbm, u_ref))):
                copies.append(pltpu.make_async_copy(hbm.at[e], ref.at[e], sems.at[2 * e + i]))
        for copy in copies:
            copy.start()
        square = jnp.zeros((slots, 1), F32)
        for s in range(roles):
            plain = x_ref[s].astype(F32) / gain_ref[s]
            square = square + jnp.sum(plain * plain, axis=1, keepdims=True)
        inverse = lax.rsqrt(square / width + EPS)

        def product(w_ref, e):
            value = jnp.dot(x_ref[0], w_ref[e, :half], preferred_element_type=F32)
            for s in range(1, roles):
                value = value + jnp.dot(
                    x_ref[s], w_ref[e, s * half : (s + 1) * half], preferred_element_type=F32
                )
            return value

        expert = lax.broadcasted_iota(jnp.int32, (slots, 1), 0) // capacity % per_dev
        gate = upper = jnp.zeros((slots, quarter), F32)
        for e in range(per_dev):
            copies[2 * e].wait()
            gate = jnp.where(expert == e, product(g_ref, e), gate)
            copies[2 * e + 1].wait()
            upper = jnp.where(expert == e, product(u_ref, e), upper)
        gate, upper = gate * inverse, upper * inverse
        act_ref[...] = (gate / (1.0 + jnp.exp(-gate)) * upper).astype(BF)

    return pl.pallas_call(
        body,
        out_shape=jax.ShapeDtypeStruct((slots, quarter), BF),
        in_specs=whole(2) + [pl.BlockSpec(memory_space=pltpu.HBM)] * 2,
        out_specs=pl.BlockSpec(memory_space=pltpu.VMEM),
        scratch_shapes=[
            pltpu.VMEM(w_gate.shape, BF),
            pltpu.VMEM(w_up.shape, BF),
            pltpu.SemaphoreType.DMA((2 * per_dev,)),
        ],
        compiler_params=pltpu.CompilerParams(vmem_limit_bytes=57 << 20),
        cost_estimate=pl.CostEstimate(
            flops=4 * per_dev * slots * width * quarter,
            bytes_accessed=10 << 20,
            transcendentals=0,
        ),
        name="experts_act",
    )(tokens, gain, w_gate, w_up)


def experts_down(acts, downs, capacity, roles):
    count = len(acts)
    slots, quarter = acts[0].shape
    per_dev, _, columns = downs[0].shape
    piece = columns // roles

    def body(*refs):
        a_refs, w_refs, out_ref = refs[:count], refs[count : 2 * count], refs[2 * count]
        expert = lax.broadcasted_iota(jnp.int32, (slots, 1), 0) // capacity % per_dev
        zero = jnp.zeros((slots, quarter), BF)
        for s in range(roles):
            total = jnp.zeros((slots, piece), F32)
            for a_ref, w_ref in zip(a_refs, w_refs):
                for e in range(per_dev):
                    total = total + jnp.dot(
                        jnp.where(expert == e, a_ref[...], zero),
                        w_ref[e, :, s * piece : (s + 1) * piece],
                        preferred_element_type=F32,
                    )
            out_ref[s * slots : (s + 1) * slots] = total.astype(BF)

    return pl.pallas_call(
        body,
        out_shape=jax.ShapeDtypeStruct((roles * slots, piece), BF),
        in_specs=whole(2 * count),
        out_specs=pl.BlockSpec(memory_space=pltpu.VMEM),
        compiler_params=pltpu.CompilerParams(vmem_limit_bytes=24 << 20),
        cost_estimate=pl.CostEstimate(
            flops=2 * slots * count * per_dev * quarter * columns,
            bytes_accessed=5 << 20,
            transcendentals=0,
        ),
        name="experts_down",
    )(*acts, *downs)


def per_device(
    queries,
    k_cache,
    value_cache,
    new_token_key,
    new_token_value,
    lengths,
    output_weight,
    residual,
    norm_gain,
    routes,
    route_scores,
    w_gate,
    w_up,
    w_down,
):
    rows_here = queries.shape[0]
    width = residual.shape[1]
    roles = lax.axis_size("role")
    heads_count = lax.axis_size("heads")
    shards = lax.axis_size("rows")
    half = width // roles
    piece = half // heads_count
    per_dev, _, quarter = w_gate.shape
    experts = per_dev * shards * roles
    capacity = 8
    role = lax.axis_index("role")
    head = lax.axis_index("heads")
    swap = [(i, roles - 1 - i) for i in range(roles)]

    def shift(x, step):
        return lax.ppermute(
            x, "heads", [(i, (i + step) % heads_count) for i in range(heads_count)]
        )

    downs = cut_down(w_down, head, heads_count, roles)

    head_size = k_cache.shape[3]
    query_vectors = queries.reshape(rows_here, -1, head_size)
    attended, theirs = attend(
        query_vectors,
        k_cache[:, 0],
        value_cache[:, 0],
        new_token_key[:, 0],
        new_token_value[:, 0],
        lengths.reshape(rows_here, 1),
        output_weight[0, 0],
        1 - role,
    )
    received = lax.ppermute(theirs, "role", swap)
    mine = own_half(attended, output_weight[0, 0], role)
    chip = (mine + received.astype(F32)).astype(BF)
    total = chip.astype(F32)
    for step in range(1, heads_count):
        total = total + shift(chip, step).astype(F32)
    first = role == 0
    resid = jnp.where(first, residual[:, :half], residual[:, half:]).astype(F32)
    gain = jnp.where(first, norm_gain[:half], norm_gain[half:])
    hidden = resid + total
    hidden, *downs = lax.optimization_barrier((hidden, *downs))
    downs = [w if step == 0 else shift(w, step) for step, w in enumerate(downs)]
    scaled = (hidden * gain).astype(BF)

    named = routes[:, :, None] == jnp.arange(experts, dtype=jnp.int32)
    chosen = jnp.any(named, axis=1)
    shares = route_scores / jnp.sum(route_scores, axis=1, keepdims=True)
    coef = jnp.sum(jnp.where(named, shares[:, :, None], F32(0.0)), axis=1)
    order = jnp.arange(rows_here, dtype=jnp.int32)
    before = (order[None, :] < order[:, None]).astype(BF)
    rank = jnp.dot(before, chosen.astype(BF), preferred_element_type=F32).astype(jnp.int32)
    taken = chosen[:, :, None] & (rank[:, :, None] == jnp.arange(capacity, dtype=jnp.int32))
    slots = experts * capacity
    pick = taken.reshape(rows_here, slots).astype(BF)
    mixing = jnp.where(taken, coef[:, :, None], F32(0.0)).reshape(rows_here, slots)

    outgoing = lax.dot_general(
        pick, scaled, (((0,), (0,)), ((), ())), preferred_element_type=F32
    ).astype(BF)
    outgoing = outgoing.reshape(roles * shards, per_dev * capacity, half)
    incoming = lax.all_to_all(outgoing, ("role", "rows"), 0, 0, tiled=True)
    tokens = incoming.reshape(roles, shards * per_dev * capacity, half)
    act = experts_act(tokens, norm_gain.reshape(roles, 1, half), w_gate, w_up, capacity)
    acts = [act if step == 0 else shift(act, step) for step in range(heads_count)]
    result = experts_down(acts, downs, capacity, roles)
    result = result.reshape(roles * shards, per_dev * capacity, piece)
    returned = lax.all_to_all(result, ("role", "rows"), 0, 0, tiled=True)
    returned = returned.reshape(slots, piece)
    mix_high = mixing.astype(BF)
    mix_low = (mixing - mix_high.astype(F32)).astype(BF)
    moe = jnp.dot(mix_high, returned, preferred_element_type=F32) + jnp.dot(
        mix_low, returned, preferred_element_type=F32
    )
    own = lax.dynamic_slice_in_dim(hidden, head * piece, piece, 1)
    return (own + moe).astype(BF)


def solution(mesh):
    in_specs = (
        P("rows", "role", "heads", None),
        P("rows", "heads", None, None),
        P("rows", "heads", None, None),
        P("rows", "heads", None),
        P("rows", "heads", None),
        P("rows"),
        P("role", "heads", None, None),
        P("rows", None),
        P(),
        P("rows", None),
        P("rows", None),
        P(("role", "rows"), None, "heads"),
        P(("role", "rows"), None, "heads"),
        P(("role", "rows"), "heads", None),
    )
    out_specs = P("rows", ("role", "heads"))
    return jax.shard_map(
        per_device, mesh=mesh, in_specs=in_specs, out_specs=out_specs, check_vma=False
    )
```

time: 167 us -> 246 us (1.47)
  Pallas kernels: 0 us -> 151 us
  local copies, waits for them, and re-layouts: 55.3 us -> 4.25 us
  matrix products: 25.3 us -> 3.3 us
  starting transfers between devices: 27.4 us -> 32.7 us
  waiting for transfers between devices: 55.9 us -> 52.7 us
    pallas_call x0 -> x5, Pallas kernels: none -> 151 us  [the longest x1 128 us: cut_down(): pl.pallas_call(body, out_shape=[shape] * heads_count, in_specs=[pl.BlockS...]
    dynamic_slice x1 -> x0, local copies, waits for them, and re-layouts: 34.9 us -> none  [per_device(): part = lax.dynamic_slice_in_dim(down, (head + step) % heads_count, 1, 3)]
    ppermute x9, waiting for transfers between devices: 44.8 us -> 18 us  [shift(): lax.ppermute(x, 'heads', [(i, (i + step) % heads_count) for i in range(he...]
    all_to_all x1, waiting for transfers between devices: 0.01 us -> 23.9 us  [per_device(): incoming = lax.all_to_all(outgoing, ('role', 'rows'), 0, 0, tiled=True)]
    dot_general x12 -> x0, matrix products: 22 us -> none  [the longest x1 4.97 us: per_device(): partial = jnp.dot(attended, output_weight[0, 0], preferred_element_type=F32)]
    reshape x7 -> x1, local copies, waits for them, and re-layouts: 18.7 us -> 1.34 us  [per_device(): lengths.reshape(rows_here, 1)]
    ppermute x9, starting transfers between devices: 7.69 us -> 14 us  [shift(): lax.ppermute(x, 'heads', [(i, (i + step) % heads_count) for i in range(he...]
  transfers between devices with their start and end apart: 12 -> 12, of which waited for: 7 -> 8; matrix products, arithmetic and copies ran while one was open for 38% -> 0% of each run, Pallas kernels for 0% -> 58%
where the time goes in v2:
time: 246 us; the launch traced here: 245 us
  Pallas kernels  151 us (61%)
  waiting for transfers between devices  52.7 us (21%)
  starting transfers between devices  32.7 us (13%)
  local copies, waits for them, and re-layouts  4.25 us (2%)
  matrix products  3.3 us (1%)
    pallas_call x1, Pallas kernels, cut_down(): pl.pallas_call(body, out_shape=[shape] * heads_count, in_specs=[pl.BlockS...  128 us
    all_to_all x1, waiting for transfers between devices, per_device(): incoming = lax.all_to_all(outgoing, ('role', 'rows'), 0, 0, tiled=True)  23.9 us
    ppermute x9, waiting for transfers between devices, shift(): lax.ppermute(x, 'heads', [(i, (i + step) % heads_count) for i in range(he...  18 us
    ppermute x9, starting transfers between devices, shift(): lax.ppermute(x, 'heads', [(i, (i + step) % heads_count) for i in range(he...  14 us
    all_to_all x1, waiting for transfers between devices, per_device(): returned = lax.all_to_all(result, ('role', 'rows'), 0, 0, tiled=True)  10.7 us
    all_to_all x1, starting transfers between devices, per_device(): incoming = lax.all_to_all(outgoing, ('role', 'rows'), 0, 0, tiled=True)  8.97 us
    pallas_call x1, Pallas kernels, experts_act(): pl.pallas_call(body, out_shape=jax.ShapeDtypeStruct((slots, quarter), BF)...  8.86 us
    all_to_all x1, starting transfers between devices, per_device(): returned = lax.all_to_all(result, ('role', 'rows'), 0, 0, tiled=True)  8.24 us
  transfers between devices with their start and end apart: 12, of which 8 were waited for; matrix products, arithmetic and copies ran while one was open for 0% of the time, Pallas kernels for 58%

profile of v2, /device:TPU:1, one launch (start us, length us, event | category | flops | bytes accessed | tf_op | source)
XLA Modules:
  0.0 245.3 jit_solution(8567678384262385933)
XLA Ops:
  0.0 1.5 copy.28
  1.5 1.3 copy.22.len_ref
  2.8 7.1 %attend.1 = (bf16[32,1024]{1,0:T(8,128)(2,1)}, bf16[32,2048]{1,0:T(8,128)(2,1)}) custom-call(s32[1]{0:T(128)} %bitcast.1.other_ref, bf16[32,8,128]{2,1,0:T(8,128)(2,1)} %bitcast.44, bf16[32,512,128]{2,1,0:T(8,128)(2,1)} %bitcast.42, bf16[32,512,128]{2,1,0:T(8,128)(2,1)} %bitcast.43, bf16[32,128]{1,0:T(8,128)(2,1)} %bitcast.47, bf16[32,128]{1,0:T(8,128)(2,1)} %bitcast.48, ...), custom_call_target="tpu_custom_call" | custom-call | flops 134217728 | bytes 12582912 | tf_op jit(solution)/shard_map/attend/pallas_call | solution.py:114
  9.9 1.5 collective-permute-start
  12.1 128.2 %cut_down.1 = (bf16[2,256,1024]{2,1,0:T(8,128)(2,1)}, bf16[2,256,1024]{2,1,0:T(8,128)(2,1)}, bf16[2,256,1024]{2,1,0:T(8,128)(2,1)}, bf16[2,256,1024]{2,1,0:T(8,128)(2,1)}) custom-call(s32[1]{0:T(128)} %bitcast.8.head_ref, bf16[2,256,4096]{2,1,0:T(8,128)(2,1)} %w_ref.1), custom_call_target="tpu_custom_call" | custom-call | bytes 8388608 | tf_op jit(solution)/shard_map/cut_down/pallas_call | solution.py:45
  140.3 4.6 %own_half.1 = f32[32,2048]{1,0:T(8,128)} custom-call(s32[1]{0:T(128)} %bitcast.role_ref, bf16[32,1024]{1,0:T(8,128)(2,1)} %get-tuple-element.16.a_ref, bf16[1024,4096]{1,0:T(8,128)(2,1)} %bitcast.39), custom_call_target="tpu_custom_call" | custom-call | flops 134217728 | bytes 4194304 | tf_op jit(solution)/shard_map/own_half/pallas_call | solution.py:159
  145.9 1.4 collective-permute-start.1
  147.3 2.4 collective-permute-start.2
  150.9 1.4 collective-permute-done.1
  152.3 3.9 %collective-permute-done.2 = bf16[32,2048]{1,0:T(8,128)(2,1)S(1)} collective-permute-done((bf16[32,2048]{1,0:T(8,128)(2,1)S(1)}, bf16[32,2048]{1,0:T(8,128)(2,1)S(1)}, u32[]{:S(2)}, u32[]{:S(2)}) %collective-permute-start.2) | collective-permute-done | bytes 131104 | tf_op jit(solution)/shard_map/ppermute | solution.py:299
  156.3 2.1 convolution_convert_fusion
  158.4 9.0 %all-to-all-start = ((bf16[32,16,2048]{2,1,0:T(8,128)(2,1)}), bf16[32,16,2048]{2,1,0:T(8,128)(2,1)}, u32[]{:S(2)}, u32[]{:S(2)}) async-start(bf16[32,16,2048]{2,1,0:T(8,128)(2,1)} %bitcast.12), calls=%async_computation | async-start | bytes 4194304 | tf_op jit(solution)/shard_map/all_to_all | solution.py:347
  168.5 2.1 collective-permute-start.8
  170.6 1.3 collective-permute-start.9
  171.9 23.9 %all-to-all-done = bf16[32,16,2048]{2,1,0:T(8,128)(2,1)} async-done(((bf16[32,16,2048]{2,1,0:T(8,128)(2,1)}), bf16[32,16,2048]{2,1,0:T(8,128)(2,1)}, u32[]{:S(2)}, u32[]{:S(2)}) %all-to-all-start) | async-done | bytes 2097184 | tf_op jit(solution)/shard_map/all_to_all | solution.py:347
  195.8 8.9 %experts_act.1.refs_0_ = bf16[256,256]{1,0:T(8,128)(2,1)} custom-call(bf16[2,256,2048]{2,1,0:T(8,128)(2,1)} %bitcast.13.x_ref, f32[2,1,2048]{2,1,0:T(1,128)} %bitcast.45, bf16[2,4096,256]{2,1,0:T(8,128)(2,1)} %g_hbm.1, bf16[2,4096,256]{2,1,0:T(8,128)(2,1)} %u_hbm.1), custom_call_target="tpu_custom_call" | custom-call | flops 2147483648 | bytes 10485760 | tf_op jit(solution)/shard_map/experts_act/pallas_call | solution.py:212
  205.8 2.1 collective-permute-start.5
  207.9 1.3 collective-permute-start.6
  209.2 7.1 %collective-permute-done.8.refs_6_ = bf16[2,256,1024]{2,1,0:T(8,128)(2,1)S(1)} collective-permute-done((bf16[2,256,1024]{2,1,0:T(8,128)(2,1)}, bf16[2,256,1024]{2,1,0:T(8,128)(2,1)S(1)}, u32[]{:S(2)}, u32[]{:S(2)}) %collective-permute-start.8) | collective-permute-done | bytes 1048608 | tf_op jit(solution)/shard_map/ppermute | solution.py:299
  216.5 3.8 %collective-permute-done.4.refs_1_ = bf16[256,256]{1,0:T(8,128)(2,1)S(1)} collective-permute-done((bf16[256,256]{1,0:T(8,128)(2,1)}, bf16[256,256]{1,0:T(8,128)(2,1)S(1)}, u32[]{:S(2)}, u32[]{:S(2)}) %collective-permute-start.4) | collective-permute-done | bytes 131104 | tf_op jit(solution)/shard_map/ppermute | solution.py:299
  220.3 1.6 collective-permute-done.5.refs_2_
  222.8 2.1 experts_down.1
  224.9 8.2 %all-to-all-start.1 = ((bf16[32,16,512]{2,1,0:T(8,128)(2,1)}), bf16[32,16,512]{2,1,0:T(8,128)(2,1)S(1)}, u32[]{:S(2)}, u32[]{:S(2)}) async-start(bf16[32,16,512]{2,1,0:T(8,128)(2,1)} %bitcast.15), calls=%async_computation.1 | async-start | bytes 1048576 | tf_op jit(solution)/shard_map/all_to_all | solution.py:353
  233.5 10.7 %all-to-all-done.1 = bf16[32,16,512]{2,1,0:T(8,128)(2,1)S(1)} async-done(((bf16[32,16,512]{2,1,0:T(8,128)(2,1)}), bf16[32,16,512]{2,1,0:T(8,128)(2,1)S(1)}, u32[]{:S(2)}, u32[]{:S(2)}) %all-to-all-start.1) | async-done | bytes 524320 | tf_op jit(solution)/shard_map/all_to_all | solution.py:353
  (37 shorter events, 7.6 us)
Async XLA Ops:
  2.8 8.6 %copy-start.5 = (s32[32,8]{0,1:T(8,128)S(1)}, s32[32,8]{0,1:T(8,128)}, u32[]{:S(2)}) copy-start(s32[32,8]{0,1:T(8,128)} %param.23) | copy-start | bytes 3076
  9.9 135.0 %collective-permute-start = (bf16[32,2048]{1,0:T(8,128)(2,1)}, bf16[32,2048]{1,0:T(8,128)(2,1)S(1)}, u32[]{:S(2)}, u32[]{:S(2)}) collective-permute-start(bf16[32,2048]{1,0:T(8,128)(2,1)} %get-tuple-element.17), channel_id=1, source_target_pairs={{0,64},{64,0},{1,65},{65,1},{2,66},{66,2},{3,67},{67,3},{4,68},{68... | collective-permute-start | bytes 393224 | tf_op jit(solution)/shard_map/ppermute | solution.py:317
  140.3 10.6 %copy-start.3 = (f32[4096]{0:T(1024)S(1)}, f32[4096]{0:T(1024)}, u32[]{:S(2)}) copy-start(f32[4096]{0:T(1024)} %param.22) | copy-start | bytes 49156
  140.3 15.9 %copy-start.2 = (bf16[32,4096]{1,0:T(8,128)(2,1)S(1)}, bf16[32,4096]{1,0:T(8,128)(2,1)}, u32[]{:S(2)}) copy-start(bf16[32,4096]{1,0:T(8,128)(2,1)} %param.21) | copy-start | bytes 786436
  145.9 6.4 %collective-permute-start.1 = (bf16[32,2048]{1,0:T(8,128)(2,1)S(1)}, bf16[32,2048]{1,0:T(8,128)(2,1)S(1)}, u32[]{:S(2)}, u32[]{:S(2)}) collective-permute-start(bf16[32,2048]{1,0:T(8,128)(2,1)S(1)} %add_convert_fusion), channel_id=1, source_target_pairs={{0,1},{1,2},{2,3},{3,0},{4,5},{5,6},{6,7},{7,4},{8,9},{9,10},{10,1... | collective-permute-start | bytes 393224 | tf_op jit(solution)/shard_map/ppermute | solution.py:299
  147.3 8.9 %collective-permute-start.2 = (bf16[32,2048]{1,0:T(8,128)(2,1)S(1)}, bf16[32,2048]{1,0:T(8,128)(2,1)S(1)}, u32[]{:S(2)}, u32[]{:S(2)}) collective-permute-start(bf16[32,2048]{1,0:T(8,128)(2,1)S(1)} %add_convert_fusion), channel_id=1, source_target_pairs={{0,2},{1,3},{2,0},{3,1},{4,6},{5,7},{6,4},{7,5},{8,10},{9,11},{10,... | collective-permute-start | bytes 393224 | tf_op jit(solution)/shard_map/ppermute | solution.py:299
  149.8 6.5 %collective-permute-start.3 = (bf16[32,2048]{1,0:T(8,128)(2,1)S(1)}, bf16[32,2048]{1,0:T(8,128)(2,1)S(1)}, u32[]{:S(2)}, u32[]{:S(2)}) collective-permute-start(bf16[32,2048]{1,0:T(8,128)(2,1)S(1)} %add_convert_fusion), channel_id=1, source_target_pairs={{0,3},{1,0},{2,1},{3,2},{4,7},{5,4},{6,5},{7,6},{8,11},{9,8},{10,9... | collective-permute-start | bytes 393224 | tf_op jit(solution)/shard_map/ppermute | solution.py:299
  158.4 37.4 %all-to-all-start = ((bf16[32,16,2048]{2,1,0:T(8,128)(2,1)}), bf16[32,16,2048]{2,1,0:T(8,128)(2,1)}, u32[]{:S(2)}, u32[]{:S(2)}) async-start(bf16[32,16,2048]{2,1,0:T(8,128)(2,1)} %bitcast.12), calls=%async_computation | async-start | bytes 4194304 | tf_op jit(solution)/shard_map/all_to_all | solution.py:347
  167.4 40.6 %collective-permute-start.7 = (bf16[2,256,1024]{2,1,0:T(8,128)(2,1)}, bf16[2,256,1024]{2,1,0:T(8,128)(2,1)S(1)}, u32[]{:S(2)}, u32[]{:S(2)}) collective-permute-start(bf16[2,256,1024]{2,1,0:T(8,128)(2,1)} %get-tuple-element.24), channel_id=1, source_target_pairs={{0,1},{1,2},{2,3},{3,0},{4,5},{5,6},{6,7},{7,4},{8,9},{9,10},{10,1... | collective-permute-start | bytes 3145736 | tf_op jit(solution)/shard_map/ppermute | solution.py:299
  168.5 47.8 %collective-permute-start.8 = (bf16[2,256,1024]{2,1,0:T(8,128)(2,1)}, bf16[2,256,1024]{2,1,0:T(8,128)(2,1)S(1)}, u32[]{:S(2)}, u32[]{:S(2)}) collective-permute-start(bf16[2,256,1024]{2,1,0:T(8,128)(2,1)} %get-tuple-element.25), channel_id=1, source_target_pairs={{0,2},{1,3},{2,0},{3,1},{4,6},{5,7},{6,4},{7,5},{8,10},{9,11},{10,... | collective-permute-start | bytes 3145736 | tf_op jit(solution)/shard_map/ppermute | solution.py:299
  170.6 45.9 %collective-permute-start.9 = (bf16[2,256,1024]{2,1,0:T(8,128)(2,1)}, bf16[2,256,1024]{2,1,0:T(8,128)(2,1)S(1)}, u32[]{:S(2)}, u32[]{:S(2)}) collective-permute-start(bf16[2,256,1024]{2,1,0:T(8,128)(2,1)} %get-tuple-element.26), channel_id=1, source_target_pairs={{0,3},{1,0},{2,1},{3,2},{4,7},{5,4},{6,5},{7,6},{8,11},{9,8},{10,9... | collective-permute-start | bytes 3145736 | tf_op jit(solution)/shard_map/ppermute | solution.py:299
  195.8 26.1 %copy-start = (bf16[2,256,1024]{2,1,0:T(8,128)(2,1)S(1)}, bf16[2,256,1024]{2,1,0:T(8,128)(2,1)}, u32[]{:S(2)}) copy-start(bf16[2,256,1024]{2,1,0:T(8,128)(2,1)} %get-tuple-element.23.refs_4_) | copy-start | bytes 3145732
  195.8 37.3 %copy-start.4 = (f32[32,8]{0,1:T(8,128)S(1)}, f32[32,8]{0,1:T(8,128)}, u32[]{:S(2)}) copy-start(f32[32,8]{0,1:T(8,128)} %param.24) | copy-start | bytes 3076
  204.7 15.6 %collective-permute-start.4 = (bf16[256,256]{1,0:T(8,128)(2,1)}, bf16[256,256]{1,0:T(8,128)(2,1)S(1)}, u32[]{:S(2)}, u32[]{:S(2)}) collective-permute-start(bf16[256,256]{1,0:T(8,128)(2,1)} %experts_act.1.refs_0_), channel_id=1, source_target_pairs={{0,1},{1,2},{2,3},{3,0},{4,5},{5,6},{6,7},{7,4},{8,9},{9,10},{10,1... | collective-permute-start | bytes 393224 | tf_op jit(solution)/shard_map/ppermute | solution.py:299
  205.8 16.1 %collective-permute-start.5 = (bf16[256,256]{1,0:T(8,128)(2,1)}, bf16[256,256]{1,0:T(8,128)(2,1)S(1)}, u32[]{:S(2)}, u32[]{:S(2)}) collective-permute-start(bf16[256,256]{1,0:T(8,128)(2,1)} %experts_act.1.refs_0_), channel_id=1, source_target_pairs={{0,2},{1,3},{2,0},{3,1},{4,6},{5,7},{6,4},{7,5},{8,10},{9,11},{10,... | collective-permute-start | bytes 393224 | tf_op jit(solution)/shard_map/ppermute | solution.py:299
  207.9 14.0 %collective-permute-start.6 = (bf16[256,256]{1,0:T(8,128)(2,1)}, bf16[256,256]{1,0:T(8,128)(2,1)S(1)}, u32[]{:S(2)}, u32[]{:S(2)}) collective-permute-start(bf16[256,256]{1,0:T(8,128)(2,1)} %experts_act.1.refs_0_), channel_id=1, source_target_pairs={{0,3},{1,0},{2,1},{3,2},{4,7},{5,4},{6,5},{7,6},{8,11},{9,8},{10,9... | collective-permute-start | bytes 393224 | tf_op jit(solution)/shard_map/ppermute | solution.py:299
  221.9 0.9 copy-start.1
  224.9 19.3 %all-to-all-start.1 = ((bf16[32,16,512]{2,1,0:T(8,128)(2,1)}), bf16[32,16,512]{2,1,0:T(8,128)(2,1)S(1)}, u32[]{:S(2)}, u32[]{:S(2)}) async-start(bf16[32,16,512]{2,1,0:T(8,128)(2,1)} %bitcast.15), calls=%async_computation.1 | async-start | bytes 1048576 | tf_op jit(solution)/shard_map/all_to_all | solution.py:353

commit v3 on v2

--- a/solution.py
+++ b/solution.py
@@ -21,25 +21,40 @@
     per_dev, quarter, width = w_down.shape
     half = width // roles
     piece = half // heads_count
-
-    def body(head_ref, w_ref, *rest):
-        outs, sems = rest[:heads_count], rest[heads_count]
-        copies = []
-        for step in range(heads_count):
-            place = lax.rem(head_ref[0] + step, heads_count)
-            for s in range(roles):
-                start = pl.multiple_of(s * half + place * piece, piece)
-                copies.append(
+    parts = 4
+
+    def body(head_ref, w_hbm, *rest):
+        outs, w_ref, in_sems, out_sems = rest[:heads_count], *rest[heads_count:]
+        loads, stores = [], []
+        for e in range(per_dev):
+            for i in range(parts):
+                rows = pl.ds(i * (quarter // parts), quarter // parts)
+                loads.append(
                     pltpu.make_async_copy(
-                        w_ref.at[:, :, pl.ds(start, piece)],
-                        outs[step].at[:, :, pl.ds(s * piece, piece)],
-                        sems.at[step * roles + s],
+                        w_hbm.at[e, rows], w_ref.at[e, rows], in_sems.at[e * parts + i]
                     )
                 )
-        for copy in copies:
-            copy.start()
-        for copy in copies:
-            copy.wait()
+            for step in range(heads_count):
+                place = lax.rem(head_ref[0] + step, heads_count)
+                for s in range(roles):
+                    start = pl.multiple_of(s * half + place * piece, piece)
+                    stores.append(
+                        pltpu.make_async_copy(
+                            w_ref.at[e, :, pl.ds(start, piece)],
+                            outs[step].at[e, :, pl.ds(s * piece, piece)],
+                            out_sems.at[(e * heads_count + step) * roles + s],
+                        )
+                    )
+        for load in loads:
+            load.start()
+        for e in range(per_dev):
+            for load in loads[e * parts : (e + 1) * parts]:
+                load.wait()
+            each = heads_count * roles
+            for store in stores[e * each : (e + 1) * each]:
+                store.start()
+        for store in stores:
+            store.wait()
 
     shape = jax.ShapeDtypeStruct((per_dev, quarter, roles * piece), w_down.dtype)
     return pl.pallas_call(
@@ -47,7 +62,11 @@
         out_shape=[shape] * heads_count,
         in_specs=[pl.BlockSpec(memory_space=pltpu.SMEM), pl.BlockSpec(memory_space=pltpu.HBM)],
         out_specs=[pl.BlockSpec(memory_space=pltpu.HBM)] * heads_count,
-        scratch_shapes=[pltpu.SemaphoreType.DMA((heads_count * roles,))],
+        scratch_shapes=[
+            pltpu.VMEM(w_down.shape, BF),
+            pltpu.SemaphoreType.DMA((per_dev * parts,)),
+            pltpu.SemaphoreType.DMA((per_dev * heads_count * roles,)),
+        ],
         compiler_params=pltpu.CompilerParams(vmem_limit_bytes=VMEM),
         cost_estimate=pl.CostEstimate(
             flops=0, bytes_accessed=2 * w_down.size * 2, transcendentals=0
@@ -56,33 +75,46 @@
     )(head.reshape(1), w_down)
 
 
-def attend(queries, k_cache, value_cache, new_key, new_value, lengths, output_weight, other):
-    rows, group, size = queries.shape
-    cache = k_cache.shape[1]
-    depth, width = output_weight.shape
+def attend(queries, k_cache, value_cache, new_key, new_value, lengths, output_weight, role):
+    rows, depth = queries.shape
+    cache, size = k_cache.shape[1:]
+    group = depth // size
+    width = output_weight.shape[1]
     half = width // 2
     step = 8
     blocks = rows // step
     scale = 1.0 / math.sqrt(size)
 
     def body(
-        other_ref, q_ref, k_hbm, v_hbm, nk_ref, nv_ref, len_ref, w_hbm,
-        attn_ref, out_ref, k_ref, v_ref, w_ref, k_sem, v_sem, w_sem,
+        role_ref, len_ref, q_ref, k_hbm, v_hbm, nk_ref, nv_ref, w_hbm,
+        theirs_ref, mine_ref, k_ref, v_ref, w_ref, attn_ref, k_sem, v_sem, w_sem,
     ):
         def copy(hbm, ref, sem, i):
             place = pl.ds(i * step, step)
             return pltpu.make_async_copy(hbm.at[place], ref.at[place], sem.at[i])
 
-        start = pl.multiple_of(other_ref[0] * half, half)
-        weight = pltpu.make_async_copy(w_hbm.at[:, pl.ds(start, half)], w_ref, w_sem)
+        weights = []
+        for s in range(2):
+            side = role_ref[0] if s else 1 - role_ref[0]
+            start = pl.multiple_of(side * half, half)
+            for i in range(4):
+                place = pl.ds(i * (depth // 4), depth // 4)
+                weights.append(
+                    pltpu.make_async_copy(
+                        w_hbm.at[place, pl.ds(start, half)],
+                        w_ref.at[s, place],
+                        w_sem.at[4 * s + i],
+                    )
+                )
         for i in range(blocks):
             copy(k_hbm, k_ref, k_sem, i).start()
             copy(v_hbm, v_ref, v_sem, i).start()
-        weight.start()
+        for weight in weights:
+            weight.start()
         for i in range(blocks):
             place = slice(i * step, (i + 1) * step)
+            q = q_ref[place].reshape(step, group, size)
             copy(k_hbm, k_ref, k_sem, i).wait()
-            q = q_ref[place]
             scores = lax.dot_general(
                 q, k_ref[place], (((2,), (2,)), ((0,), (0,))), preferred_element_type=F32
             )
@@ -92,86 +124,63 @@
             )
             fresh = fresh * scale
             position = lax.broadcasted_iota(jnp.int32, (step, group, cache), 2)
-            limit = len_ref[place][:, :, None]
+            row = lax.broadcasted_iota(jnp.int32, (step, group, cache), 0)
+            limit = jnp.full((step, group, cache), len_ref[i * step])
+            for j in range(1, step):
+                limit = jnp.where(row == j, len_ref[i * step + j], limit)
             scores = jnp.where(position < limit, scores, -jnp.inf)
             top = jnp.maximum(jnp.max(scores, axis=2, keepdims=True), fresh)
             expo = jnp.exp(scores - top)
             expo_new = jnp.exp(fresh - top)
-            denom = jnp.sum(expo, axis=2, keepdims=True) + expo_new
-            probs = (expo / denom).astype(BF)
-            probs_new = (expo_new / denom).astype(BF).astype(F32)
+            inverse = 1.0 / (jnp.sum(expo, axis=2, keepdims=True) + expo_new)
+            probs = (expo * inverse).astype(BF)
+            probs_new = (expo_new * inverse).astype(BF).astype(F32)
             copy(v_hbm, v_ref, v_sem, i).wait()
             result = lax.dot_general(
                 probs, v_ref[place], (((2,), (1,)), ((0,), (0,))), preferred_element_type=F32
             )
             result = result + probs_new * nv_ref[place].astype(F32)[:, None, :]
-            attn_ref[place, :] = result.reshape(step, group * size).astype(BF)
-        weight.wait()
-        out_ref[...] = jnp.dot(
-            attn_ref[...], w_ref[...], preferred_element_type=F32
-        ).astype(BF)
+            attn_ref[place, :] = result.reshape(step, depth).astype(BF)
+        for weight in weights[:4]:
+            weight.wait()
+        product = jnp.dot(attn_ref[...], w_ref[0], preferred_element_type=F32)
+        theirs_ref[...] = product.astype(BF)
+        for weight in weights[4:]:
+            weight.wait()
+        mine_ref[...] = jnp.dot(attn_ref[...], w_ref[1], preferred_element_type=F32)
 
     return pl.pallas_call(
         body,
         out_shape=[
-            jax.ShapeDtypeStruct((rows, depth), BF),
             jax.ShapeDtypeStruct((rows, half), BF),
+            jax.ShapeDtypeStruct((rows, half), F32),
         ],
         in_specs=[
+            pl.BlockSpec(memory_space=pltpu.SMEM),
             pl.BlockSpec(memory_space=pltpu.SMEM),
             pl.BlockSpec(memory_space=pltpu.VMEM),
             pl.BlockSpec(memory_space=pltpu.HBM),
             pl.BlockSpec(memory_space=pltpu.HBM),
             pl.BlockSpec(memory_space=pltpu.VMEM),
             pl.BlockSpec(memory_space=pltpu.VMEM),
-            pl.BlockSpec(memory_space=pltpu.VMEM),
             pl.BlockSpec(memory_space=pltpu.HBM),
         ],
         out_specs=whole(2),
         scratch_shapes=[
             pltpu.VMEM((rows, cache, size), BF),
             pltpu.VMEM((rows, cache, size), BF),
-            pltpu.VMEM((depth, half), BF),
+            pltpu.VMEM((2, depth, half), BF),
+            pltpu.VMEM((rows, depth), BF),
             pltpu.SemaphoreType.DMA((blocks,)),
             pltpu.SemaphoreType.DMA((blocks,)),
-            pltpu.SemaphoreType.DMA,
+            pltpu.SemaphoreType.DMA((8,)),
         ],
         compiler_params=pltpu.CompilerParams(vmem_limit_bytes=57 << 20),
         cost_estimate=pl.CostEstimate(
-            flops=2 * rows * depth * half, bytes_accessed=12 << 20, transcendentals=0
+            flops=2 * rows * depth * width, bytes_accessed=16 << 20, transcendentals=0
         ),
         name="attend",
-    )(other.reshape(1), queries, k_cache, value_cache, new_key, new_value, lengths, output_weight)
-
-
-def own_half(attended, output_weight, role):
-    rows = attended.shape[0]
-    depth, width = output_weight.shape
-    half = width // 2
-
-    def body(role_ref, a_ref, w_hbm, out_ref, w_ref, sem):
-        start = pl.multiple_of(role_ref[0] * half, half)
-        copy = pltpu.make_async_copy(w_hbm.at[:, pl.ds(start, half)], w_ref, sem)
-        copy.start()
-        copy.wait()
-        out_ref[...] = jnp.dot(a_ref[...], w_ref[...], preferred_element_type=F32)
-
-    return pl.pallas_call(
-        body,
-        out_shape=jax.ShapeDtypeStruct((rows, half), F32),
-        in_specs=[
-            pl.BlockSpec(memory_space=pltpu.SMEM),
-            pl.BlockSpec(memory_space=pltpu.VMEM),
-            pl.BlockSpec(memory_space=pltpu.HBM),
-        ],
-        out_specs=pl.BlockSpec(memory_space=pltpu.VMEM),
-        scratch_shapes=[pltpu.VMEM((depth, half), BF), pltpu.SemaphoreType.DMA],
-        compiler_params=pltpu.CompilerParams(vmem_limit_bytes=57 << 20),
-        cost_estimate=pl.CostEstimate(
-            flops=2 * rows * depth * half, bytes_accessed=4 << 20, transcendentals=0
-        ),
-        name="own_half",
-    )(role.reshape(1), attended, output_weight)
+    )(role.reshape(1), lengths, queries, k_cache, value_cache, new_key, new_value, output_weight)
 
 
 def experts_act(tokens, gain, w_gate, w_up, capacity):
@@ -187,7 +196,7 @@
             copy.start()
         square = jnp.zeros((slots, 1), F32)
         for s in range(roles):
-            plain = x_ref[s].astype(F32) / gain_ref[s]
+            plain = x_ref[s].astype(F32) * (1.0 / gain_ref[s])
             square = square + jnp.sum(plain * plain, axis=1, keepdims=True)
         inverse = lax.rsqrt(square / width + EPS)
 
@@ -300,23 +309,19 @@
             x, "heads", [(i, (i + step) % heads_count) for i in range(heads_count)]
         )
 
-    downs = cut_down(w_down, head, heads_count, roles)
-
-    head_size = k_cache.shape[3]
-    query_vectors = queries.reshape(rows_here, -1, head_size)
-    attended, theirs = attend(
-        query_vectors,
+    theirs, mine = attend(
+        queries[:, 0, 0],
         k_cache[:, 0],
         value_cache[:, 0],
         new_token_key[:, 0],
         new_token_value[:, 0],
-        lengths.reshape(rows_here, 1),
+        lengths,
         output_weight[0, 0],
-        1 - role,
+        role,
     )
     received = lax.ppermute(theirs, "role", swap)
-    mine = own_half(attended, output_weight[0, 0], role)
-    chip = (mine + received.astype(F32)).astype(BF)
+    chip, w_down = lax.optimization_barrier(((mine + received.astype(F32)).astype(BF), w_down))
+    downs = cut_down(w_down, head, heads_count, roles)
     total = chip.astype(F32)
     for step in range(1, heads_count):
         total = total + shift(chip, step).astype(F32)

time: 246 us -> 113 us (0.46)
  Pallas kernels: 151 us -> 24 us
  waiting for transfers between devices: 52.7 us -> 49.1 us
  local copies, waits for them, and re-layouts: 4.25 us -> 1.44 us
    pallas_call x1, Pallas kernels: 128 us -> 3.71 us  [cut_down(): pl.pallas_call(body, out_shape=[shape] * heads_count, in_specs=[pl.BlockS...]
    ppermute x9, waiting for transfers between devices: 18 us -> 13.9 us  [shift(): lax.ppermute(x, 'heads', [(i, (i + step) % heads_count) for i in range(he...]
    pallas_call x2 -> x1, Pallas kernels: 11.7 us -> 9.41 us  [attend(): pl.pallas_call(body, out_shape=[jax.ShapeDtypeStruct((rows, half), BF), j...]
  transfers between devices with their start and end apart: 12 -> 12, of which waited for: 8 -> 8; matrix products, arithmetic and copies ran while one was open for 0% -> 1% of each run, Pallas kernels for 58% -> 11%
where the time goes in v3:
time: 113 us
  waiting for transfers between devices  49.1 us (43%)
  starting transfers between devices  33.1 us (29%)
  Pallas kernels  24 us (21%)
  matrix products  3.29 us (3%)
  local copies, waits for them, and re-layouts  1.44 us (1%)
  other arithmetic  1.39 us (1%)
    all_to_all x1, waiting for transfers between devices, per_device(): incoming = lax.all_to_all(outgoing, ('role', 'rows'), 0, 0, tiled=True)  23.9 us
    ppermute x9, starting transfers between devices, shift(): lax.ppermute(x, 'heads', [(i, (i + step) % heads_count) for i in range(he...  14 us
    ppermute x9, waiting for transfers between devices, shift(): lax.ppermute(x, 'heads', [(i, (i + step) % heads_count) for i in range(he...  13.9 us
    all_to_all x1, waiting for transfers between devices, per_device(): returned = lax.all_to_all(result, ('role', 'rows'), 0, 0, tiled=True)  10.7 us
    pallas_call x1, Pallas kernels, attend(): pl.pallas_call(body, out_shape=[jax.ShapeDtypeStruct((rows, half), BF), j...  9.41 us
    all_to_all x1, starting transfers between devices, per_device(): incoming = lax.all_to_all(outgoing, ('role', 'rows'), 0, 0, tiled=True)  9.35 us
    pallas_call x1, Pallas kernels, experts_act(): pl.pallas_call(body, out_shape=jax.ShapeDtypeStruct((slots, quarter), BF)...  8.86 us
    all_to_all x1, starting transfers between devices, per_device(): returned = lax.all_to_all(result, ('role', 'rows'), 0, 0, tiled=True)  8.24 us
  transfers between devices with their start and end apart: 12, of which 8 were waited for; matrix products, arithmetic and copies ran while one was open for 1% of the time, Pallas kernels for 11%

profile of v3, /device:TPU:1, one launch (start us, length us, event | category | flops | bytes accessed | tf_op | source)
XLA Modules:
  0.0 112.5 jit_solution(6780014417676973496)
XLA Ops:
  0.0 9.4 %attend.1 = (bf16[32,2048]{1,0:T(8,128)(2,1)}, f32[32,2048]{1,0:T(8,128)}) custom-call(s32[1]{0:T(128)} %bitcast.role_ref, s32[32]{0:T(128)} %len_ref.1, bf16[32,1024]{1,0:T(8,128)(2,1)} %bitcast.37, bf16[32,512,128]{2,1,0:T(8,128)(2,1)} %bitcast.35, bf16[32,512,128]{2,1,0:T(8,128)(2,1)} %bitcast.36, bf16[32,128]{1,0:T(8,128)(2,1)} %bitcast.39, ...), custom_call_target="tpu_custom_call" | custom-call | flops 268435456 | bytes 16777216 | tf_op jit(solution)/shard_map/attend/pallas_call | solution.py:152
  9.4 1.5 %collective-permute-start = (bf16[32,2048]{1,0:T(8,128)(2,1)}, bf16[32,2048]{1,0:T(8,128)(2,1)S(1)}, u32[]{:S(2)}, u32[]{:S(2)}) collective-permute-start(bf16[32,2048]{1,0:T(8,128)(2,1)} %get-tuple-element.19), channel_id=1, source_target_pairs={{0,64},{64,0},{1,65},{65,1},{2,66},{66,2},{3,67},{67,3},{4,68},{68... | collective-permute-start | bytes 393224 | tf_op jit(solution)/shard_map/ppermute | solution.py:322
  12.1 1.0 add_convert_fusion
  13.1 1.4 %collective-permute-start.1 = (bf16[32,2048]{1,0:T(8,128)(2,1)S(1)}, bf16[32,2048]{1,0:T(8,128)(2,1)S(1)}, u32[]{:S(2)}, u32[]{:S(2)}) collective-permute-start(bf16[32,2048]{1,0:T(8,128)(2,1)S(1)} %add_convert_fusion), channel_id=1, source_target_pairs={{0,1},{1,2},{2,3},{3,0},{4,5},{5,6},{6,7},{7,4},{8,9},{9,10},{10,1... | collective-permute-start | bytes 393224 | tf_op jit(solution)/shard_map/ppermute | solution.py:308
  14.5 2.5 %collective-permute-start.2 = (bf16[32,2048]{1,0:T(8,128)(2,1)S(1)}, bf16[32,2048]{1,0:T(8,128)(2,1)S(1)}, u32[]{:S(2)}, u32[]{:S(2)}) collective-permute-start(bf16[32,2048]{1,0:T(8,128)(2,1)S(1)} %add_convert_fusion), channel_id=1, source_target_pairs={{0,2},{1,3},{2,0},{3,1},{4,6},{5,7},{6,4},{7,5},{8,10},{9,11},{10,... | collective-permute-start | bytes 393224 | tf_op jit(solution)/shard_map/ppermute | solution.py:308
  16.9 1.2 %collective-permute-start.3 = (bf16[32,2048]{1,0:T(8,128)(2,1)S(1)}, bf16[32,2048]{1,0:T(8,128)(2,1)S(1)}, u32[]{:S(2)}, u32[]{:S(2)}) collective-permute-start(bf16[32,2048]{1,0:T(8,128)(2,1)S(1)} %add_convert_fusion), channel_id=1, source_target_pairs={{0,3},{1,0},{2,1},{3,2},{4,7},{5,4},{6,5},{7,6},{8,11},{9,8},{10,9... | collective-permute-start | bytes 393224 | tf_op jit(solution)/shard_map/ppermute | solution.py:308
  18.1 3.7 %cut_down.1 = (bf16[2,256,1024]{2,1,0:T(8,128)(2,1)}, bf16[2,256,1024]{2,1,0:T(8,128)(2,1)}, bf16[2,256,1024]{2,1,0:T(8,128)(2,1)}, bf16[2,256,1024]{2,1,0:T(8,128)(2,1)}) custom-call(s32[1]{0:T(128)} %bitcast.7.head_ref, bf16[2,256,4096]{2,1,0:T(8,128)(2,1)} %w_hbm), custom_call_target="tpu_custom_call" | custom-call | bytes 8388608 | tf_op jit(solution)/shard_map/cut_down/pallas_call | solution.py:60
  21.8 1.2 %collective-permute-done.2 = bf16[32,2048]{1,0:T(8,128)(2,1)S(1)} collective-permute-done((bf16[32,2048]{1,0:T(8,128)(2,1)S(1)}, bf16[32,2048]{1,0:T(8,128)(2,1)S(1)}, u32[]{:S(2)}, u32[]{:S(2)}) %collective-permute-start.2) | collective-permute-done | bytes 131104 | tf_op jit(solution)/shard_map/ppermute | solution.py:308
  23.1 2.1 %convolution_convert_fusion = bf16[512,2048]{1,0:T(8,128)(2,1)} fusion(f32[32,2048]{1,0:T(8,128)S(1)} %add_add_fusion, f32[2048]{0:T(1024)S(1)} %slice_select_fusion, s32[512]{0:T(512)S(1)} %eq.64, s32[32,64]{0,1:T(8,128)S(1)} %copy.22, pred[32,64]{0,1:T(8,128)(4,1)S(1)} %copy.21), kind=kOutput, calls=%fused_computation | convolution fusion | flops 68321280 | bytes 2379776 | tf_op jit(solution)/shard_map/dot_general | solution.py:348
  25.2 9.4 %all-to-all-start = ((bf16[32,16,2048]{2,1,0:T(8,128)(2,1)}), bf16[32,16,2048]{2,1,0:T(8,128)(2,1)}, u32[]{:S(2)}, u32[]{:S(2)}) async-start(bf16[32,16,2048]{2,1,0:T(8,128)(2,1)} %bitcast.11), calls=%async_computation | async-start | bytes 4194304 | tf_op jit(solution)/shard_map/all_to_all | solution.py:352
  34.5 1.1 collective-permute-start.7
  35.7 2.1 %collective-permute-start.8 = (bf16[2,256,1024]{2,1,0:T(8,128)(2,1)}, bf16[2,256,1024]{2,1,0:T(8,128)(2,1)S(1)}, u32[]{:S(2)}, u32[]{:S(2)}) collective-permute-start(bf16[2,256,1024]{2,1,0:T(8,128)(2,1)} %get-tuple-element.29), channel_id=1, source_target_pairs={{0,2},{1,3},{2,0},{3,1},{4,6},{5,7},{6,4},{7,5},{8,10},{9,11},{10,... | collective-permute-start | bytes 3145736 | tf_op jit(solution)/shard_map/ppermute | solution.py:308
  37.8 1.3 %collective-permute-start.9 = (bf16[2,256,1024]{2,1,0:T(8,128)(2,1)}, bf16[2,256,1024]{2,1,0:T(8,128)(2,1)S(1)}, u32[]{:S(2)}, u32[]{:S(2)}) collective-permute-start(bf16[2,256,1024]{2,1,0:T(8,128)(2,1)} %get-tuple-element.30), channel_id=1, source_target_pairs={{0,3},{1,0},{2,1},{3,2},{4,7},{5,4},{6,5},{7,6},{8,11},{9,8},{10,9... | collective-permute-start | bytes 3145736 | tf_op jit(solution)/shard_map/ppermute | solution.py:308
  39.1 23.9 %all-to-all-done = bf16[32,16,2048]{2,1,0:T(8,128)(2,1)} async-done(((bf16[32,16,2048]{2,1,0:T(8,128)(2,1)}), bf16[32,16,2048]{2,1,0:T(8,128)(2,1)}, u32[]{:S(2)}, u32[]{:S(2)}) %all-to-all-start) | async-done | bytes 2097184 | tf_op jit(solution)/shard_map/all_to_all | solution.py:352
  63.0 8.9 %experts_act.1.refs_0_ = bf16[256,256]{1,0:T(8,128)(2,1)} custom-call(bf16[2,256,2048]{2,1,0:T(8,128)(2,1)} %bitcast.12.x_ref, f32[2,1,2048]{2,1,0:T(1,128)} %bitcast.38, bf16[2,4096,256]{2,1,0:T(8,128)(2,1)} %g_hbm.1, bf16[2,4096,256]{2,1,0:T(8,128)(2,1)} %u_hbm.1), custom_call_target="tpu_custom_call" | custom-call | flops 2147483648 | bytes 10485760 | tf_op jit(solution)/shard_map/experts_act/pallas_call | solution.py:221
  71.9 1.1 collective-permute-start.4
  73.0 2.1 %collective-permute-start.5 = (bf16[256,256]{1,0:T(8,128)(2,1)}, bf16[256,256]{1,0:T(8,128)(2,1)S(1)}, u32[]{:S(2)}, u32[]{:S(2)}) collective-permute-start(bf16[256,256]{1,0:T(8,128)(2,1)} %experts_act.1.refs_0_), channel_id=1, source_target_pairs={{0,2},{1,3},{2,0},{3,1},{4,6},{5,7},{6,4},{7,5},{8,10},{9,11},{10,... | collective-permute-start | bytes 393224 | tf_op jit(solution)/shard_map/ppermute | solution.py:308
  75.1 1.3 %collective-permute-start.6 = (bf16[256,256]{1,0:T(8,128)(2,1)}, bf16[256,256]{1,0:T(8,128)(2,1)S(1)}, u32[]{:S(2)}, u32[]{:S(2)}) collective-permute-start(bf16[256,256]{1,0:T(8,128)(2,1)} %experts_act.1.refs_0_), channel_id=1, source_target_pairs={{0,3},{1,0},{2,1},{3,2},{4,7},{5,4},{6,5},{7,6},{8,11},{9,8},{10,9... | collective-permute-start | bytes 393224 | tf_op jit(solution)/shard_map/ppermute | solution.py:308
  76.4 7.1 %collective-permute-done.8.refs_6_ = bf16[2,256,1024]{2,1,0:T(8,128)(2,1)S(1)} collective-permute-done((bf16[2,256,1024]{2,1,0:T(8,128)(2,1)}, bf16[2,256,1024]{2,1,0:T(8,128)(2,1)S(1)}, u32[]{:S(2)}, u32[]{:S(2)}) %collective-permute-start.8) | collective-permute-done | bytes 1048608 | tf_op jit(solution)/shard_map/ppermute | solution.py:308
  83.7 3.8 %collective-permute-done.4.refs_1_ = bf16[256,256]{1,0:T(8,128)(2,1)S(1)} collective-permute-done((bf16[256,256]{1,0:T(8,128)(2,1)}, bf16[256,256]{1,0:T(8,128)(2,1)S(1)}, u32[]{:S(2)}, u32[]{:S(2)}) %collective-permute-start.4) | collective-permute-done | bytes 131104 | tf_op jit(solution)/shard_map/ppermute | solution.py:308
  87.5 1.6 %collective-permute-done.5.refs_2_ = bf16[256,256]{1,0:T(8,128)(2,1)S(1)} collective-permute-done((bf16[256,256]{1,0:T(8,128)(2,1)}, bf16[256,256]{1,0:T(8,128)(2,1)S(1)}, u32[]{:S(2)}, u32[]{:S(2)}) %collective-permute-start.5) | collective-permute-done | bytes 131104 | tf_op jit(solution)/shard_map/ppermute | solution.py:308
  90.0 2.1 %experts_down.1 = bf16[512,512]{1,0:T(8,128)(2,1)} custom-call(bf16[256,256]{1,0:T(8,128)(2,1)S(1)} %copy-done.1, bf16[256,256]{1,0:T(8,128)(2,1)S(1)} %collective-permute-done.4.refs_1_, bf16[256,256]{1,0:T(8,128)(2,1)S(1)} %collective-permute-done.5.refs_2_, bf16[256,256]{1,0:T(8,128)(2,1)S(1)} %collective-permute-done.6.refs_3_, ...), custom_call_target="tpu_custom_call" | custom-call | flops 1073741824 | bytes 5242880 | tf_op jit(solution)/shard_map/experts_down/pallas_call | solution.py:262
  92.1 8.2 %all-to-all-start.1 = ((bf16[32,16,512]{2,1,0:T(8,128)(2,1)}), bf16[32,16,512]{2,1,0:T(8,128)(2,1)S(1)}, u32[]{:S(2)}, u32[]{:S(2)}) async-start(bf16[32,16,512]{2,1,0:T(8,128)(2,1)} %bitcast.14), calls=%async_computation.1 | async-start | bytes 1048576 | tf_op jit(solution)/shard_map/all_to_all | solution.py:358
  100.7 10.7 %all-to-all-done.1 = bf16[32,16,512]{2,1,0:T(8,128)(2,1)S(1)} async-done(((bf16[32,16,512]{2,1,0:T(8,128)(2,1)}), bf16[32,16,512]{2,1,0:T(8,128)(2,1)S(1)}, u32[]{:S(2)}, u32[]{:S(2)}) %all-to-all-start.1) | async-done | bytes 524320 | tf_op jit(solution)/shard_map/all_to_all | solution.py:358
  (34 shorter events, 3.8 us)
Async XLA Ops:
  0.0 10.9 %copy-start.5 = (s32[32,8]{0,1:T(8,128)S(1)}, s32[32,8]{0,1:T(8,128)}, u32[]{:S(2)}) copy-start(s32[32,8]{0,1:T(8,128)} %param.23) | copy-start | bytes 3076
  0.0 18.1 %copy-start.3 = (f32[4096]{0:T(1024)S(1)}, f32[4096]{0:T(1024)}, u32[]{:S(2)}) copy-start(f32[4096]{0:T(1024)} %param.22) | copy-start | bytes 49156
  9.4 13.6 %copy-start.2 = (bf16[32,4096]{1,0:T(8,128)(2,1)S(1)}, bf16[32,4096]{1,0:T(8,128)(2,1)}, u32[]{:S(2)}) copy-start(bf16[32,4096]{1,0:T(8,128)(2,1)} %param.21) | copy-start | bytes 786436
  9.4 2.7 %collective-permute-start = (bf16[32,2048]{1,0:T(8,128)(2,1)}, bf16[32,2048]{1,0:T(8,128)(2,1)S(1)}, u32[]{:S(2)}, u32[]{:S(2)}) collective-permute-start(bf16[32,2048]{1,0:T(8,128)(2,1)} %get-tuple-element.19), channel_id=1, source_target_pairs={{0,64},{64,0},{1,65},{65,1},{2,66},{66,2},{3,67},{67,3},{4,68},{68... | collective-permute-start | bytes 393224 | tf_op jit(solution)/shard_map/ppermute | solution.py:322
  13.1 8.7 %collective-permute-start.1 = (bf16[32,2048]{1,0:T(8,128)(2,1)S(1)}, bf16[32,2048]{1,0:T(8,128)(2,1)S(1)}, u32[]{:S(2)}, u32[]{:S(2)}) collective-permute-start(bf16[32,2048]{1,0:T(8,128)(2,1)S(1)} %add_convert_fusion), channel_id=1, source_target_pairs={{0,1},{1,2},{2,3},{3,0},{4,5},{5,6},{6,7},{7,4},{8,9},{9,10},{10,1... | collective-permute-start | bytes 393224 | tf_op jit(solution)/shard_map/ppermute | solution.py:308
  14.5 8.5 %collective-permute-start.2 = (bf16[32,2048]{1,0:T(8,128)(2,1)S(1)}, bf16[32,2048]{1,0:T(8,128)(2,1)S(1)}, u32[]{:S(2)}, u32[]{:S(2)}) collective-permute-start(bf16[32,2048]{1,0:T(8,128)(2,1)S(1)} %add_convert_fusion), channel_id=1, source_target_pairs={{0,2},{1,3},{2,0},{3,1},{4,6},{5,7},{6,4},{7,5},{8,10},{9,11},{10,... | collective-permute-start | bytes 393224 | tf_op jit(solution)/shard_map/ppermute | solution.py:308
  16.9 6.1 %collective-permute-start.3 = (bf16[32,2048]{1,0:T(8,128)(2,1)S(1)}, bf16[32,2048]{1,0:T(8,128)(2,1)S(1)}, u32[]{:S(2)}, u32[]{:S(2)}) collective-permute-start(bf16[32,2048]{1,0:T(8,128)(2,1)S(1)} %add_convert_fusion), channel_id=1, source_target_pairs={{0,3},{1,0},{2,1},{3,2},{4,7},{5,4},{6,5},{7,6},{8,11},{9,8},{10,9... | collective-permute-start | bytes 393224 | tf_op jit(solution)/shard_map/ppermute | solution.py:308
  25.2 37.8 %all-to-all-start = ((bf16[32,16,2048]{2,1,0:T(8,128)(2,1)}), bf16[32,16,2048]{2,1,0:T(8,128)(2,1)}, u32[]{:S(2)}, u32[]{:S(2)}) async-start(bf16[32,16,2048]{2,1,0:T(8,128)(2,1)} %bitcast.11), calls=%async_computation | async-start | bytes 4194304 | tf_op jit(solution)/shard_map/all_to_all | solution.py:352
  34.5 40.6 %collective-permute-start.7 = (bf16[2,256,1024]{2,1,0:T(8,128)(2,1)}, bf16[2,256,1024]{2,1,0:T(8,128)(2,1)S(1)}, u32[]{:S(2)}, u32[]{:S(2)}) collective-permute-start(bf16[2,256,1024]{2,1,0:T(8,128)(2,1)} %get-tuple-element.28), channel_id=1, source_target_pairs={{0,1},{1,2},{2,3},{3,0},{4,5},{5,6},{6,7},{7,4},{8,9},{9,10},{10,1... | collective-permute-start | bytes 3145736 | tf_op jit(solution)/shard_map/ppermute | solution.py:308
  35.7 47.8 %collective-permute-start.8 = (bf16[2,256,1024]{2,1,0:T(8,128)(2,1)}, bf16[2,256,1024]{2,1,0:T(8,128)(2,1)S(1)}, u32[]{:S(2)}, u32[]{:S(2)}) collective-permute-start(bf16[2,256,1024]{2,1,0:T(8,128)(2,1)} %get-tuple-element.29), channel_id=1, source_target_pairs={{0,2},{1,3},{2,0},{3,1},{4,6},{5,7},{6,4},{7,5},{8,10},{9,11},{10,... | collective-permute-start | bytes 3145736 | tf_op jit(solution)/shard_map/ppermute | solution.py:308
  37.8 45.9 %collective-permute-start.9 = (bf16[2,256,1024]{2,1,0:T(8,128)(2,1)}, bf16[2,256,1024]{2,1,0:T(8,128)(2,1)S(1)}, u32[]{:S(2)}, u32[]{:S(2)}) collective-permute-start(bf16[2,256,1024]{2,1,0:T(8,128)(2,1)} %get-tuple-element.30), channel_id=1, source_target_pairs={{0,3},{1,0},{2,1},{3,2},{4,7},{5,4},{6,5},{7,6},{8,11},{9,8},{10,9... | collective-permute-start | bytes 3145736 | tf_op jit(solution)/shard_map/ppermute | solution.py:308
  63.0 26.1 %copy-start = (bf16[2,256,1024]{2,1,0:T(8,128)(2,1)S(1)}, bf16[2,256,1024]{2,1,0:T(8,128)(2,1)}, u32[]{:S(2)}) copy-start(bf16[2,256,1024]{2,1,0:T(8,128)(2,1)} %get-tuple-element.27.refs_4_) | copy-start | bytes 3145732
  63.0 37.3 %copy-start.4 = (f32[32,8]{0,1:T(8,128)S(1)}, f32[32,8]{0,1:T(8,128)}, u32[]{:S(2)}) copy-start(f32[32,8]{0,1:T(8,128)} %param.24) | copy-start | bytes 3076
  71.9 15.6 %collective-permute-start.4 = (bf16[256,256]{1,0:T(8,128)(2,1)}, bf16[256,256]{1,0:T(8,128)(2,1)S(1)}, u32[]{:S(2)}, u32[]{:S(2)}) collective-permute-start(bf16[256,256]{1,0:T(8,128)(2,1)} %experts_act.1.refs_0_), channel_id=1, source_target_pairs={{0,1},{1,2},{2,3},{3,0},{4,5},{5,6},{6,7},{7,4},{8,9},{9,10},{10,1... | collective-permute-start | bytes 393224 | tf_op jit(solution)/shard_map/ppermute | solution.py:308
  73.0 16.1 %collective-permute-start.5 = (bf16[256,256]{1,0:T(8,128)(2,1)}, bf16[256,256]{1,0:T(8,128)(2,1)S(1)}, u32[]{:S(2)}, u32[]{:S(2)}) collective-permute-start(bf16[256,256]{1,0:T(8,128)(2,1)} %experts_act.1.refs_0_), channel_id=1, source_target_pairs={{0,2},{1,3},{2,0},{3,1},{4,6},{5,7},{6,4},{7,5},{8,10},{9,11},{10,... | collective-permute-start | bytes 393224 | tf_op jit(solution)/shard_map/ppermute | solution.py:308
  75.1 14.0 %collective-permute-start.6 = (bf16[256,256]{1,0:T(8,128)(2,1)}, bf16[256,256]{1,0:T(8,128)(2,1)S(1)}, u32[]{:S(2)}, u32[]{:S(2)}) collective-permute-start(bf16[256,256]{1,0:T(8,128)(2,1)} %experts_act.1.refs_0_), channel_id=1, source_target_pairs={{0,3},{1,0},{2,1},{3,2},{4,7},{5,4},{6,5},{7,6},{8,11},{9,8},{10,9... | collective-permute-start | bytes 393224 | tf_op jit(solution)/shard_map/ppermute | solution.py:308
  89.1 0.9 copy-start.1
  92.1 19.3 %all-to-all-start.1 = ((bf16[32,16,512]{2,1,0:T(8,128)(2,1)}), bf16[32,16,512]{2,1,0:T(8,128)(2,1)S(1)}, u32[]{:S(2)}, u32[]{:S(2)}) async-start(bf16[32,16,512]{2,1,0:T(8,128)(2,1)} %bitcast.14), calls=%async_computation.1 | async-start | bytes 1048576 | tf_op jit(solution)/shard_map/all_to_all | solution.py:358

commit v4 on v3

--- a/solution.py
+++ b/solution.py
@@ -17,14 +17,15 @@
     return [pl.BlockSpec(memory_space=pltpu.VMEM)] * n
 
 
-def cut_down(w_down, head, heads_count, roles):
+def cut_down(w_down, head, heads_count, roles, pieces):
     per_dev, quarter, width = w_down.shape
     half = width // roles
     piece = half // heads_count
     parts = 4
+    count = len(pieces)
 
     def body(head_ref, w_hbm, *rest):
-        outs, w_ref, in_sems, out_sems = rest[:heads_count], *rest[heads_count:]
+        outs, w_ref, in_sems, out_sems = rest[:count], *rest[count:]
         loads, stores = [], []
         for e in range(per_dev):
             for i in range(parts):
@@ -34,38 +35,38 @@
                         w_hbm.at[e, rows], w_ref.at[e, rows], in_sems.at[e * parts + i]
                     )
                 )
-            for step in range(heads_count):
-                place = lax.rem(head_ref[0] + step, heads_count)
-                for s in range(roles):
-                    start = pl.multiple_of(s * half + place * piece, piece)
-                    stores.append(
-                        pltpu.make_async_copy(
-                            w_ref.at[e, :, pl.ds(start, piece)],
-                            outs[step].at[e, :, pl.ds(s * piece, piece)],
-                            out_sems.at[(e * heads_count + step) * roles + s],
-                        )
-                    )
+        for i, (step, e) in enumerate(pieces):
+            place = lax.rem(head_ref[0] + step, heads_count)
+            for s in range(roles):
+                start = pl.multiple_of(s * half + place * piece, piece)
+                stores.append(
+                    pltpu.make_async_copy(
+                        w_ref.at[e, :, pl.ds(start, piece)],
+                        outs[i].at[:, pl.ds(s * piece, piece)],
+                        out_sems.at[i * roles + s],
+                    )
+                )
         for load in loads:
             load.start()
         for e in range(per_dev):
             for load in loads[e * parts : (e + 1) * parts]:
                 load.wait()
-            each = heads_count * roles
-            for store in stores[e * each : (e + 1) * each]:
-                store.start()
+            for i, (_, mine) in enumerate(pieces):
+                if mine == e:
+                    for store in stores[i * roles : (i + 1) * roles]:
+                        store.start()
         for store in stores:
             store.wait()
 
-    shape = jax.ShapeDtypeStruct((per_dev, quarter, roles * piece), w_down.dtype)
     return pl.pallas_call(
         body,
-        out_shape=[shape] * heads_count,
+        out_shape=[jax.ShapeDtypeStruct((quarter, roles * piece), BF)] * count,
         in_specs=[pl.BlockSpec(memory_space=pltpu.SMEM), pl.BlockSpec(memory_space=pltpu.HBM)],
-        out_specs=[pl.BlockSpec(memory_space=pltpu.HBM)] * heads_count,
+        out_specs=[pl.BlockSpec(memory_space=pltpu.HBM)] * count,
         scratch_shapes=[
             pltpu.VMEM(w_down.shape, BF),
             pltpu.SemaphoreType.DMA((per_dev * parts,)),
-            pltpu.SemaphoreType.DMA((per_dev * heads_count * roles,)),
+            pltpu.SemaphoreType.DMA((count * roles,)),
         ],
         compiler_params=pltpu.CompilerParams(vmem_limit_bytes=VMEM),
         cost_estimate=pl.CostEstimate(
@@ -177,101 +178,156 @@
         ],
         compiler_params=pltpu.CompilerParams(vmem_limit_bytes=57 << 20),
         cost_estimate=pl.CostEstimate(
-            flops=2 * rows * depth * width, bytes_accessed=16 << 20, transcendentals=0
+            flops=0, bytes_accessed=1 << 20, transcendentals=0
         ),
         name="attend",
     )(role.reshape(1), lengths, queries, k_cache, value_cache, new_key, new_value, output_weight)
 
 
+def of_expert(value, e, per_dev, capacity):
+    rows, columns = value.shape
+    blocks = rows // (per_dev * capacity)
+    return value.reshape(blocks, per_dev, capacity, columns)[:, e].reshape(
+        blocks * capacity, columns
+    )
+
+
+def of_all(values, capacity):
+    rows, columns = values[0].shape
+    blocks = rows // capacity
+    parts = [v.reshape(blocks, 1, capacity, columns) for v in values]
+    return jnp.concatenate(parts, axis=1).reshape(len(values) * rows, columns)
+
+
 def experts_act(tokens, gain, w_gate, w_up, capacity):
     roles, slots, half = tokens.shape
     per_dev, width, quarter = w_gate.shape
-
-    def body(x_ref, gain_ref, g_hbm, u_hbm, act_ref, g_ref, u_ref, sems):
+    chunk = 512
+
+    def body(x_ref, gain_ref, g_any, u_any, act_ref, g_ref, u_ref, sums, sems):
         copies = []
-        for e in range(per_dev):
-            for i, (hbm, ref) in enumerate(((g_hbm, g_ref), (u_hbm, u_ref))):
-                copies.append(pltpu.make_async_copy(hbm.at[e], ref.at[e], sems.at[2 * e + i]))
-        for copy in copies:
-            copy.start()
+        for k in range(width // chunk):
+            rows = pl.ds(k * chunk, chunk)
+            copies.append(
+                [
+                    pltpu.make_async_copy(
+                        source.at[:, rows], target.at[:, rows], sems.at[2 * k + i]
+                    )
+                    for i, (source, target) in enumerate(((g_any, g_ref), (u_any, u_ref)))
+                ]
+            )
+        for pair in copies:
+            for copy in pair:
+                copy.start()
         square = jnp.zeros((slots, 1), F32)
-        for s in range(roles):
-            plain = x_ref[s].astype(F32) * (1.0 / gain_ref[s])
+        for k in range(width // chunk):
+            s, place = divmod(k * chunk, half)
+            x = x_ref[s, :, place : place + chunk].astype(F32)
+            plain = x * (1.0 / gain_ref[s, :, place : place + chunk])
             square = square + jnp.sum(plain * plain, axis=1, keepdims=True)
+            for copy in copies[k]:
+                copy.wait()
+            for e in range(per_dev):
+                one = of_expert(x, e, per_dev, capacity).astype(BF)
+                for i, w_ref in enumerate((g_ref, u_ref)):
+                    product = jnp.dot(
+                        one, w_ref[e, k * chunk : (k + 1) * chunk], preferred_element_type=F32
+                    )
+                    if k:
+                        product = product + sums[2 * e + i]
+                    sums[2 * e + i] = product
         inverse = lax.rsqrt(square / width + EPS)
-
-        def product(w_ref, e):
-            value = jnp.dot(x_ref[0], w_ref[e, :half], preferred_element_type=F32)
-            for s in range(1, roles):
-                value = value + jnp.dot(
-                    x_ref[s], w_ref[e, s * half : (s + 1) * half], preferred_element_type=F32
-                )
-            return value
-
-        expert = lax.broadcasted_iota(jnp.int32, (slots, 1), 0) // capacity % per_dev
-        gate = upper = jnp.zeros((slots, quarter), F32)
-        for e in range(per_dev):
-            copies[2 * e].wait()
-            gate = jnp.where(expert == e, product(g_ref, e), gate)
-            copies[2 * e + 1].wait()
-            upper = jnp.where(expert == e, product(u_ref, e), upper)
-        gate, upper = gate * inverse, upper * inverse
+        gate = of_all([sums[2 * e] for e in range(per_dev)], capacity) * inverse
+        upper = of_all([sums[2 * e + 1] for e in range(per_dev)], capacity) * inverse
         act_ref[...] = (gate / (1.0 + jnp.exp(-gate)) * upper).astype(BF)
 
     return pl.pallas_call(
         body,
         out_shape=jax.ShapeDtypeStruct((slots, quarter), BF),
-        in_specs=whole(2) + [pl.BlockSpec(memory_space=pltpu.HBM)] * 2,
+        in_specs=whole(2) + [pl.BlockSpec(memory_space=pl.ANY)] * 2,
         out_specs=pl.BlockSpec(memory_space=pltpu.VMEM),
         scratch_shapes=[
             pltpu.VMEM(w_gate.shape, BF),
             pltpu.VMEM(w_up.shape, BF),
-            pltpu.SemaphoreType.DMA((2 * per_dev,)),
+            pltpu.VMEM((2 * per_dev, slots // per_dev, quarter), F32),
+            pltpu.SemaphoreType.DMA((2 * (width // chunk),)),
         ],
         compiler_params=pltpu.CompilerParams(vmem_limit_bytes=57 << 20),
         cost_estimate=pl.CostEstimate(
-            flops=4 * per_dev * slots * width * quarter,
-            bytes_accessed=10 << 20,
-            transcendentals=0,
+            flops=4 * slots * width * quarter, bytes_accessed=10 << 20, transcendentals=0
         ),
         name="experts_act",
     )(tokens, gain, w_gate, w_up)
 
 
-def experts_down(acts, downs, capacity, roles):
+def far_down(act, downs, capacity):
+    slots, _ = act.shape
+    per_dev = len(downs)
+    columns = downs[0].shape[1]
+
+    def body(a_ref, *refs):
+        w_refs, out_ref = refs[:-1], refs[-1]
+        value = a_ref[...].astype(F32)
+        products = [
+            jnp.dot(
+                of_expert(value, e, per_dev, capacity).astype(BF),
+                w_ref[...],
+                preferred_element_type=F32,
+            )
+            for e, w_ref in enumerate(w_refs)
+        ]
+        out_ref[...] = of_all(products, capacity).astype(BF)
+
+    return pl.pallas_call(
+        body,
+        out_shape=jax.ShapeDtypeStruct((slots, columns), BF),
+        in_specs=whole(1 + per_dev),
+        out_specs=pl.BlockSpec(memory_space=pltpu.VMEM),
+        compiler_params=pltpu.CompilerParams(vmem_limit_bytes=24 << 20),
+        name="far_down",
+    )(act, *downs)
+
+
+def experts_down(acts, downs, far, capacity, roles):
     count = len(acts)
     slots, quarter = acts[0].shape
-    per_dev, _, columns = downs[0].shape
+    per_dev = len(downs[0])
+    columns = downs[0][0].shape[1]
     piece = columns // roles
 
     def body(*refs):
-        a_refs, w_refs, out_ref = refs[:count], refs[count : 2 * count], refs[2 * count]
-        expert = lax.broadcasted_iota(jnp.int32, (slots, 1), 0) // capacity % per_dev
-        zero = jnp.zeros((slots, quarter), BF)
+        a_refs, w_refs, (far_ref, out_ref) = refs[:count], refs[count:-2], refs[-2:]
+        ones = [
+            [of_expert(a[...].astype(F32), e, per_dev, capacity).astype(BF) for e in range(per_dev)]
+            for a in a_refs
+        ]
         for s in range(roles):
-            total = jnp.zeros((slots, piece), F32)
-            for a_ref, w_ref in zip(a_refs, w_refs):
-                for e in range(per_dev):
-                    total = total + jnp.dot(
-                        jnp.where(expert == e, a_ref[...], zero),
-                        w_ref[e, :, s * piece : (s + 1) * piece],
+            totals = []
+            for e in range(per_dev):
+                total = None
+                for i in range(count):
+                    product = jnp.dot(
+                        ones[i][e],
+                        w_refs[i * per_dev + e][:, s * piece : (s + 1) * piece],
                         preferred_element_type=F32,
                     )
+                    total = product if total is None else total + product
+                totals.append(total)
+            total = of_all(totals, capacity) + far_ref[:, s * piece : (s + 1) * piece].astype(F32)
             out_ref[s * slots : (s + 1) * slots] = total.astype(BF)
 
+    flat = [w for each in downs for w in each]
     return pl.pallas_call(
         body,
         out_shape=jax.ShapeDtypeStruct((roles * slots, piece), BF),
-        in_specs=whole(2 * count),
+        in_specs=whole(count + len(flat) + 1),
         out_specs=pl.BlockSpec(memory_space=pltpu.VMEM),
         compiler_params=pltpu.CompilerParams(vmem_limit_bytes=24 << 20),
         cost_estimate=pl.CostEstimate(
-            flops=2 * slots * count * per_dev * quarter * columns,
-            bytes_accessed=5 << 20,
-            transcendentals=0,
+            flops=2 * slots * count * quarter * columns, bytes_accessed=5 << 20, transcendentals=0
         ),
         name="experts_down",
-    )(*acts, *downs)
+    )(*acts, *flat, far)
 
 
 def per_device(
@@ -320,8 +376,11 @@
         role,
     )
     received = lax.ppermute(theirs, "role", swap)
-    chip, w_down = lax.optimization_barrier(((mine + received.astype(F32)).astype(BF), w_down))
-    downs = cut_down(w_down, head, heads_count, roles)
+    chip = (mine + received.astype(F32)).astype(BF)
+    chip, w_down = lax.optimization_barrier((chip, w_down))
+    across, near = heads_count // 2, (0, 1, heads_count - 1)
+    pieces = [(step, e) for step in (*near, across) for e in range(per_dev)]
+    rest = cut_down(w_down, head, heads_count, roles, pieces)
     total = chip.astype(F32)
     for step in range(1, heads_count):
         total = total + shift(chip, step).astype(F32)
@@ -329,8 +388,11 @@
     resid = jnp.where(first, residual[:, :half], residual[:, half:]).astype(F32)
     gain = jnp.where(first, norm_gain[:half], norm_gain[half:])
     hidden = resid + total
-    hidden, *downs = lax.optimization_barrier((hidden, *downs))
-    downs = [w if step == 0 else shift(w, step) for step, w in enumerate(downs)]
+    hidden, *rest = lax.optimization_barrier((hidden, *rest))
+    downs = [
+        [shift(part, step) if step else part for part in rest[i * per_dev : (i + 1) * per_dev]]
+        for i, step in enumerate(near)
+    ]
     scaled = (hidden * gain).astype(BF)
 
     named = routes[:, :, None] == jnp.arange(experts, dtype=jnp.int32)
@@ -352,8 +414,9 @@
     incoming = lax.all_to_all(outgoing, ("role", "rows"), 0, 0, tiled=True)
     tokens = incoming.reshape(roles, shards * per_dev * capacity, half)
     act = experts_act(tokens, norm_gain.reshape(roles, 1, half), w_gate, w_up, capacity)
-    acts = [act if step == 0 else shift(act, step) for step in range(heads_count)]
-    result = experts_down(acts, downs, capacity, roles)
+    far = shift(far_down(act, rest[len(near) * per_dev :], capacity), across)
+    acts = [shift(act, step) if step else act for step in near]
+    result = experts_down(acts, downs, far, capacity, roles)
     result = result.reshape(roles * shards, per_dev * capacity, piece)
     returned = lax.all_to_all(result, ("role", "rows"), 0, 0, tiled=True)
     returned = returned.reshape(slots, piece)

time: 113 us -> 107 us (0.947)
  starting transfers between devices: 33.1 us -> 29.4 us
  Pallas kernels: 24 us -> 21.1 us
    all_to_all x1, starting transfers between devices: 8.24 us -> 4.2 us  [per_device(): returned = lax.all_to_all(result, ('role', 'rows'), 0, 0, tiled=True)]
    pallas_call x1, Pallas kernels: 8.86 us -> 6.23 us  [experts_act(): pl.pallas_call(body, out_shape=jax.ShapeDtypeStruct((slots, quarter), BF)...]
    ppermute x9 -> x10, waiting for transfers between devices: 13.9 us -> 14.2 us  [shift(): lax.ppermute(x, 'heads', [(i, (i + step) % heads_count) for i in range(he...]
    pallas_call x1 -> x2, Pallas kernels: 3.71 us -> 4.03 us  [the longest x1 3.73 us: cut_down(): pl.pallas_call(body, out_shape=[jax.ShapeDtypeStruct((quarter, roles * pi...]
    ppermute x9 -> x10, starting transfers between devices: 14 us -> 14.3 us  [shift(): lax.ppermute(x, 'heads', [(i, (i + step) % heads_count) for i in range(he...]
  transfers between devices with their start and end apart: 12 -> 13, of which waited for: 8 -> 5; matrix products, arithmetic and copies ran while one was open for 1% -> 1% of each run, Pallas kernels for 11% -> 10%
where the time goes in v4:
time: 107 us
  waiting for transfers between devices  49.8 us (47%)
  starting transfers between devices  29.4 us (27%)
  Pallas kernels  21.1 us (20%)
  matrix products  3.3 us (3%)
  local copies, waits for them, and re-layouts  1.45 us (1%)
  other arithmetic  1.38 us (1%)
    all_to_all x1, waiting for transfers between devices, per_device(): incoming = lax.all_to_all(outgoing, ('role', 'rows'), 0, 0, tiled=True)  24.2 us
    ppermute x10, starting transfers between devices, shift(): lax.ppermute(x, 'heads', [(i, (i + step) % heads_count) for i in range(he...  14.3 us
    ppermute x10, waiting for transfers between devices, shift(): lax.ppermute(x, 'heads', [(i, (i + step) % heads_count) for i in range(he...  14.2 us
    all_to_all x1, waiting for transfers between devices, per_device(): returned = lax.all_to_all(result, ('role', 'rows'), 0, 0, tiled=True)  10.7 us
    pallas_call x1, Pallas kernels, attend(): pl.pallas_call(body, out_shape=[jax.ShapeDtypeStruct((rows, half), BF), j...  9.41 us
    all_to_all x1, starting transfers between devices, per_device(): incoming = lax.all_to_all(outgoing, ('role', 'rows'), 0, 0, tiled=True)  9.35 us
    pallas_call x1, Pallas kernels, experts_act(): pl.pallas_call(body, out_shape=jax.ShapeDtypeStruct((slots, quarter), BF)...  6.23 us
    all_to_all x1, starting transfers between devices, per_device(): returned = lax.all_to_all(result, ('role', 'rows'), 0, 0, tiled=True)  4.2 us
  transfers between devices with their start and end apart: 13, of which 5 were waited for; matrix products, arithmetic and copies ran while one was open for 1% of the time, Pallas kernels for 10%

profile of v4, /device:TPU:1, one launch (start us, length us, event | category | flops | bytes accessed | tf_op | source)
XLA Modules:
  0.0 106.5 jit_solution(2434261729845675519)
XLA Ops:
  0.0 9.4 %attend.1 = (bf16[32,2048]{1,0:T(8,128)(2,1)}, f32[32,2048]{1,0:T(8,128)}) custom-call(s32[1]{0:T(128)} %bitcast.role_ref, s32[32]{0:T(128)} %len_ref.1, bf16[32,1024]{1,0:T(8,128)(2,1)} %bitcast.37, bf16[32,512,128]{2,1,0:T(8,128)(2,1)} %bitcast.35, bf16[32,512,128]{2,1,0:T(8,128)(2,1)} %bitcast.36, bf16[32,128]{1,0:T(8,128)(2,1)} %bitcast.39, ...), custom_call_target="tpu_custom_call" | custom-call | bytes 1048576 | tf_op jit(solution)/shard_map/attend/pallas_call | solution.py:153
  9.4 1.5 %collective-permute-start = (bf16[32,2048]{1,0:T(8,128)(2,1)}, bf16[32,2048]{1,0:T(8,128)(2,1)S(1)}, u32[]{:S(2)}, u32[]{:S(2)}) collective-permute-start(bf16[32,2048]{1,0:T(8,128)(2,1)} %get-tuple-element.27), channel_id=1, source_target_pairs={{0,64},{64,0},{1,65},{65,1},{2,66},{66,2},{3,67},{67,3},{4,68},{68... | collective-permute-start | bytes 393224 | tf_op jit(solution)/shard_map/ppermute | solution.py:378
  11.6 0.6 collective-permute-done
  12.1 1.0 add_convert_fusion
  13.1 1.4 %collective-permute-start.1 = (bf16[32,2048]{1,0:T(8,128)(2,1)S(1)}, bf16[32,2048]{1,0:T(8,128)(2,1)S(1)}, u32[]{:S(2)}, u32[]{:S(2)}) collective-permute-start(bf16[32,2048]{1,0:T(8,128)(2,1)S(1)} %add_convert_fusion), channel_id=1, source_target_pairs={{0,1},{1,2},{2,3},{3,0},{4,5},{5,6},{6,7},{7,4},{8,9},{9,10},{10,1... | collective-permute-start | bytes 393224 | tf_op jit(solution)/shard_map/ppermute | solution.py:364
  14.5 2.5 %collective-permute-start.2 = (bf16[32,2048]{1,0:T(8,128)(2,1)S(1)}, bf16[32,2048]{1,0:T(8,128)(2,1)S(1)}, u32[]{:S(2)}, u32[]{:S(2)}) collective-permute-start(bf16[32,2048]{1,0:T(8,128)(2,1)S(1)} %add_convert_fusion), channel_id=1, source_target_pairs={{0,2},{1,3},{2,0},{3,1},{4,6},{5,7},{6,4},{7,5},{8,10},{9,11},{10,... | collective-permute-start | bytes 393224 | tf_op jit(solution)/shard_map/ppermute | solution.py:364
  16.9 1.2 %collective-permute-start.3 = (bf16[32,2048]{1,0:T(8,128)(2,1)S(1)}, bf16[32,2048]{1,0:T(8,128)(2,1)S(1)}, u32[]{:S(2)}, u32[]{:S(2)}) collective-permute-start(bf16[32,2048]{1,0:T(8,128)(2,1)S(1)} %add_convert_fusion), channel_id=1, source_target_pairs={{0,3},{1,0},{2,1},{3,2},{4,7},{5,4},{6,5},{7,6},{8,11},{9,8},{10,9... | collective-permute-start | bytes 393224 | tf_op jit(solution)/shard_map/ppermute | solution.py:364
  18.1 3.7 %cut_down.1 = (bf16[256,1024]{1,0:T(8,128)(2,1)}, bf16[256,1024]{1,0:T(8,128)(2,1)}, bf16[256,1024]{1,0:T(8,128)(2,1)}, bf16[256,1024]{1,0:T(8,128)(2,1)}, bf16[...) custom-call(s32[1]{0:T(128)} %bitcast.7.head_ref, ...), custom_call_target="tpu_custom_call" | custom-call | bytes 8388608 | tf_op jit(solution)/shard_map/cut_down/pallas_call | solution.py:61
  21.9 1.1 %collective-permute-done.2 = bf16[32,2048]{1,0:T(8,128)(2,1)S(1)} collective-permute-done((bf16[32,2048]{1,0:T(8,128)(2,1)S(1)}, bf16[32,2048]{1,0:T(8,128)(2,1)S(1)}, u32[]{:S(2)}, u32[]{:S(2)}) %collective-permute-start.2) | collective-permute-done | bytes 131104 | tf_op jit(solution)/shard_map/ppermute | solution.py:364
  23.1 2.1 %convolution_convert_fusion = bf16[512,2048]{1,0:T(8,128)(2,1)} fusion(f32[32,2048]{1,0:T(8,128)S(1)} %add_add_fusion, f32[2048]{0:T(1024)S(1)} %slice_select_fusion, s32[512]{0:T(512)S(1)} %eq.64, s32[32,64]{0,1:T(8,128)S(1)} %copy.22, pred[32,64]{0,1:T(8,128)(4,1)S(1)} %copy.21), kind=kOutput, calls=%fused_computation | convolution fusion | flops 68321280 | bytes 2379776 | tf_op jit(solution)/shard_map/dot_general | solution.py:410
  25.2 9.4 %all-to-all-start = ((bf16[32,16,2048]{2,1,0:T(8,128)(2,1)}), bf16[32,16,2048]{2,1,0:T(8,128)(2,1)}, u32[]{:S(2)}, u32[]{:S(2)}) async-start(bf16[32,16,2048]{2,1,0:T(8,128)(2,1)} %bitcast.11), calls=%async_computation | async-start | bytes 4194304 | tf_op jit(solution)/shard_map/all_to_all | solution.py:414
  34.5 1.1 %collective-permute-start.6 = (bf16[256,1024]{1,0:T(8,128)(2,1)}, bf16[256,1024]{1,0:T(8,128)(2,1)S(1)}, u32[]{:S(2)}, u32[]{:S(2)}) collective-permute-start(bf16[256,1024]{1,0:T(8,128)(2,1)} %get-tuple-element.41), channel_id=1, source_target_pairs={{0,1},{1,2},{2,3},{3,0},{4,5},{5,6},{6,7},{7,4},{8,9},{9,10},{10,1... | collective-permute-start | bytes 1572872 | tf_op jit(solution)/shard_map/ppermute | solution.py:364
  35.7 1.0 collective-permute-start.7
  36.7 1.7 %collective-permute-start.8 = (bf16[256,1024]{1,0:T(8,128)(2,1)S(1)}, bf16[256,1024]{1,0:T(8,128)(2,1)S(1)}, u32[]{:S(2)}, u32[]{:S(2)}) collective-permute-start(bf16[256,1024]{1,0:T(8,128)(2,1)S(1)} %copy-done.10), channel_id=1, source_target_pairs={{0,3},{1,0},{2,1},{3,2},{4,7},{5,4},{6,5},{7,6},{8,11},{9,8},{10,9... | collective-permute-start | bytes 1572872 | tf_op jit(solution)/shard_map/ppermute | solution.py:364
  38.7 24.2 %all-to-all-done = bf16[32,16,2048]{2,1,0:T(8,128)(2,1)} async-done(((bf16[32,16,2048]{2,1,0:T(8,128)(2,1)}), bf16[32,16,2048]{2,1,0:T(8,128)(2,1)}, u32[]{:S(2)}, u32[]{:S(2)}) %all-to-all-start) | async-done | bytes 2097184 | tf_op jit(solution)/shard_map/all_to_all | solution.py:414
  63.0 6.2 %experts_act.1.a_ref.refs_0_ = bf16[256,256]{1,0:T(8,128)(2,1)} custom-call(bf16[2,256,2048]{2,1,0:T(8,128)(2,1)} %bitcast.12.x_ref, f32[2,1,2048]{2,1,0:T(1,128)} %bitcast.38, bf16[2,4096,256]{2,1,0:T(8,128)(2,1)} %g_any.1, bf16[2,4096,256]{2,1,0:T(8,128)(2,1)} %u_any.1), custom_call_target="tpu_custom_call" | custom-call | flops 1073741824 | bytes 10485760 | tf_op jit(solution)/shard_map/experts_act/pallas_call | solution.py:244
  69.2 0.9 copy-done
  70.5 2.5 %collective-permute-start.10 = (bf16[256,1024]{1,0:T(8,128)(2,1)S(1)}, bf16[256,1024]{1,0:T(8,128)(2,1)S(1)}, u32[]{:S(2)}, u32[]{:S(2)}) collective-permute-start(bf16[256,1024]{1,0:T(8,128)(2,1)S(1)} %far_down.1), channel_id=1, source_target_pairs={{0,2},{1,3},{2,0},{3,1},{4,6},{5,7},{6,4},{7,5},{8,10},{9,11},{10,... | collective-permute-start | bytes 1572872 | tf_op jit(solution)/shard_map/ppermute | solution.py:364
  73.1 2.5 %collective-permute-start.5 = (bf16[256,256]{1,0:T(8,128)(2,1)S(1)}, bf16[256,256]{1,0:T(8,128)(2,1)S(1)}, u32[]{:S(2)}, u32[]{:S(2)}) collective-permute-start(bf16[256,256]{1,0:T(8,128)(2,1)S(1)} %copy-done), channel_id=1, source_target_pairs={{0,3},{1,0},{2,1},{3,2},{4,7},{5,4},{6,5},{7,6},{8,11},{9,8},{10,9... | collective-permute-start | bytes 393224 | tf_op jit(solution)/shard_map/ppermute | solution.py:364
  75.6 13.1 %collective-permute-done.4.refs_1_ = bf16[256,256]{1,0:T(8,128)(2,1)S(1)} collective-permute-done((bf16[256,256]{1,0:T(8,128)(2,1)S(1)}, bf16[256,256]{1,0:T(8,128)(2,1)S(1)}, u32[]{:S(2)}, u32[]{:S(2)}) %collective-permute-start.4) | collective-permute-done | bytes 131104 | tf_op jit(solution)/shard_map/ppermute | solution.py:364
  88.7 1.4 %experts_down.1 = bf16[512,512]{1,0:T(8,128)(2,1)} custom-call(bf16[256,256]{1,0:T(8,128)(2,1)S(1)} %copy-done, bf16[256,256]{1,0:T(8,128)(2,1)S(1)} %collective-permute-done.4.refs_1_, bf16[256,256]{1,0:T(8,128)(2,1)S(1)} %collective-permute-done.5.refs_2_, bf16[256,1024]{1,0:T(8,128)(2,1)S(1)} %copy-done.1, bf16[256,1024]{1,0:T(8,128)(2,1)S(1)} %copy-done.2, ...), custom_call_target="tpu_custom_call" | custom-call | flops 402653184 | bytes 5242880 | tf_op jit(solution)/shard_map/experts_down/pallas_call | solution.py:320
  90.1 4.2 %all-to-all-start.1 = ((bf16[32,16,512]{2,1,0:T(8,128)(2,1)}), bf16[32,16,512]{2,1,0:T(8,128)(2,1)S(1)}, u32[]{:S(2)}, u32[]{:S(2)}) async-start(bf16[32,16,512]{2,1,0:T(8,128)(2,1)} %bitcast.14), calls=%async_computation.1 | async-start | bytes 1048576 | tf_op jit(solution)/shard_map/all_to_all | solution.py:421
  94.7 10.7 %all-to-all-done.1 = bf16[32,16,512]{2,1,0:T(8,128)(2,1)S(1)} async-done(((bf16[32,16,512]{2,1,0:T(8,128)(2,1)}), bf16[32,16,512]{2,1,0:T(8,128)(2,1)S(1)}, u32[]{:S(2)}, u32[]{:S(2)}) %all-to-all-start.1) | async-done | bytes 524320 | tf_op jit(solution)/shard_map/all_to_all | solution.py:421
  105.7 0.9 fusion.1
  (47 shorter events, 2.2 us)
Async XLA Ops:
  0.0 10.9 %copy-start.8 = (s32[32,8]{0,1:T(8,128)S(1)}, s32[32,8]{0,1:T(8,128)}, u32[]{:S(2)}) copy-start(s32[32,8]{0,1:T(8,128)} %param.23) | copy-start | bytes 3076
  0.0 18.1 %copy-start.6 = (f32[4096]{0:T(1024)S(1)}, f32[4096]{0:T(1024)}, u32[]{:S(2)}) copy-start(f32[4096]{0:T(1024)} %param.22) | copy-start | bytes 49156
  9.4 13.6 %copy-start.5 = (bf16[32,4096]{1,0:T(8,128)(2,1)S(1)}, bf16[32,4096]{1,0:T(8,128)(2,1)}, u32[]{:S(2)}) copy-start(bf16[32,4096]{1,0:T(8,128)(2,1)} %param.21) | copy-start | bytes 786436
  9.4 2.7 %collective-permute-start = (bf16[32,2048]{1,0:T(8,128)(2,1)}, bf16[32,2048]{1,0:T(8,128)(2,1)S(1)}, u32[]{:S(2)}, u32[]{:S(2)}) collective-permute-start(bf16[32,2048]{1,0:T(8,128)(2,1)} %get-tuple-element.27), channel_id=1, source_target_pairs={{0,64},{64,0},{1,65},{65,1},{2,66},{66,2},{3,67},{67,3},{4,68},{68... | collective-permute-start | bytes 393224 | tf_op jit(solution)/shard_map/ppermute | solution.py:378
  13.1 8.7 %collective-permute-start.1 = (bf16[32,2048]{1,0:T(8,128)(2,1)S(1)}, bf16[32,2048]{1,0:T(8,128)(2,1)S(1)}, u32[]{:S(2)}, u32[]{:S(2)}) collective-permute-start(bf16[32,2048]{1,0:T(8,128)(2,1)S(1)} %add_convert_fusion), channel_id=1, source_target_pairs={{0,1},{1,2},{2,3},{3,0},{4,5},{5,6},{6,7},{7,4},{8,9},{9,10},{10,1... | collective-permute-start | bytes 393224 | tf_op jit(solution)/shard_map/ppermute | solution.py:364
  14.5 8.5 %collective-permute-start.2 = (bf16[32,2048]{1,0:T(8,128)(2,1)S(1)}, bf16[32,2048]{1,0:T(8,128)(2,1)S(1)}, u32[]{:S(2)}, u32[]{:S(2)}) collective-permute-start(bf16[32,2048]{1,0:T(8,128)(2,1)S(1)} %add_convert_fusion), channel_id=1, source_target_pairs={{0,2},{1,3},{2,0},{3,1},{4,6},{5,7},{6,4},{7,5},{8,10},{9,11},{10,... | collective-permute-start | bytes 393224 | tf_op jit(solution)/shard_map/ppermute | solution.py:364
  16.9 6.1 %collective-permute-start.3 = (bf16[32,2048]{1,0:T(8,128)(2,1)S(1)}, bf16[32,2048]{1,0:T(8,128)(2,1)S(1)}, u32[]{:S(2)}, u32[]{:S(2)}) collective-permute-start(bf16[32,2048]{1,0:T(8,128)(2,1)S(1)} %add_convert_fusion), channel_id=1, source_target_pairs={{0,3},{1,0},{2,1},{3,2},{4,7},{5,4},{6,5},{7,6},{8,11},{9,8},{10,9... | collective-permute-start | bytes 393224 | tf_op jit(solution)/shard_map/ppermute | solution.py:364
  21.8 14.8 %copy-start.10 = (bf16[256,1024]{1,0:T(8,128)(2,1)S(1)}, bf16[256,1024]{1,0:T(8,128)(2,1)}, u32[]{:S(2)}) copy-start(bf16[256,1024]{1,0:T(8,128)(2,1)} %get-tuple-element.43) | copy-start | bytes 1572868
  21.8 16.5 %copy-start.9 = (bf16[256,1024]{1,0:T(8,128)(2,1)S(1)}, bf16[256,1024]{1,0:T(8,128)(2,1)}, u32[]{:S(2)}) copy-start(bf16[256,1024]{1,0:T(8,128)(2,1)} %get-tuple-element.44) | copy-start | bytes 1572868
  25.2 37.8 %all-to-all-start = ((bf16[32,16,2048]{2,1,0:T(8,128)(2,1)}), bf16[32,16,2048]{2,1,0:T(8,128)(2,1)}, u32[]{:S(2)}, u32[]{:S(2)}) async-start(bf16[32,16,2048]{2,1,0:T(8,128)(2,1)} %bitcast.11), calls=%async_computation | async-start | bytes 4194304 | tf_op jit(solution)/shard_map/all_to_all | solution.py:414
  34.5 38.4 %collective-permute-start.6 = (bf16[256,1024]{1,0:T(8,128)(2,1)}, bf16[256,1024]{1,0:T(8,128)(2,1)S(1)}, u32[]{:S(2)}, u32[]{:S(2)}) collective-permute-start(bf16[256,1024]{1,0:T(8,128)(2,1)} %get-tuple-element.41), channel_id=1, source_target_pairs={{0,1},{1,2},{2,3},{3,0},{4,5},{5,6},{6,7},{7,4},{8,9},{9,10},{10,1... | collective-permute-start | bytes 1572872 | tf_op jit(solution)/shard_map/ppermute | solution.py:364
  35.7 37.5 %collective-permute-start.7 = (bf16[256,1024]{1,0:T(8,128)(2,1)}, bf16[256,1024]{1,0:T(8,128)(2,1)S(1)}, u32[]{:S(2)}, u32[]{:S(2)}) collective-permute-start(bf16[256,1024]{1,0:T(8,128)(2,1)} %get-tuple-element.42), channel_id=1, source_target_pairs={{0,1},{1,2},{2,3},{3,0},{4,5},{5,6},{6,7},{7,4},{8,9},{9,10},{10,1... | collective-permute-start | bytes 1572872 | tf_op jit(solution)/shard_map/ppermute | solution.py:364
  36.7 39.0 %collective-permute-start.8 = (bf16[256,1024]{1,0:T(8,128)(2,1)S(1)}, bf16[256,1024]{1,0:T(8,128)(2,1)S(1)}, u32[]{:S(2)}, u32[]{:S(2)}) collective-permute-start(bf16[256,1024]{1,0:T(8,128)(2,1)S(1)} %copy-done.10), channel_id=1, source_target_pairs={{0,3},{1,0},{2,1},{3,2},{4,7},{5,4},{6,5},{7,6},{8,11},{9,8},{10,9... | collective-permute-start | bytes 1572872 | tf_op jit(solution)/shard_map/ppermute | solution.py:364
  38.3 37.3 %collective-permute-start.9 = (bf16[256,1024]{1,0:T(8,128)(2,1)S(1)}, bf16[256,1024]{1,0:T(8,128)(2,1)S(1)}, u32[]{:S(2)}, u32[]{:S(2)}) collective-permute-start(bf16[256,1024]{1,0:T(8,128)(2,1)S(1)} %copy-done.9), channel_id=1, source_target_pairs={{0,3},{1,0},{2,1},{3,2},{4,7},{5,4},{6,5},{7,6},{8,11},{9,8},{10,9... | collective-permute-start | bytes 1572872 | tf_op jit(solution)/shard_map/ppermute | solution.py:364
  63.0 6.3 %copy-start.3 = (bf16[256,1024]{1,0:T(8,128)(2,1)S(1)}, bf16[256,1024]{1,0:T(8,128)(2,1)}, u32[]{:S(2)}) copy-start(bf16[256,1024]{1,0:T(8,128)(2,1)} %get-tuple-element.45.refs_0_) | copy-start | bytes 1572868
  63.0 6.3 %copy-start.4 = (bf16[256,1024]{1,0:T(8,128)(2,1)S(1)}, bf16[256,1024]{1,0:T(8,128)(2,1)}, u32[]{:S(2)}) copy-start(bf16[256,1024]{1,0:T(8,128)(2,1)} %get-tuple-element.46.refs_1_) | copy-start | bytes 1572868
  63.0 25.7 %copy-start.1 = (bf16[256,1024]{1,0:T(8,128)(2,1)S(1)}, bf16[256,1024]{1,0:T(8,128)(2,1)}, u32[]{:S(2)}) copy-start(bf16[256,1024]{1,0:T(8,128)(2,1)} %get-tuple-element.39.refs_3_) | copy-start | bytes 1572868
  63.0 25.7 %copy-start.2 = (bf16[256,1024]{1,0:T(8,128)(2,1)S(1)}, bf16[256,1024]{1,0:T(8,128)(2,1)}, u32[]{:S(2)}) copy-start(bf16[256,1024]{1,0:T(8,128)(2,1)} %get-tuple-element.40.refs_4_) | copy-start | bytes 1572868
  69.2 0.9 copy-start
  70.1 24.2 %copy-start.7 = (f32[32,8]{0,1:T(8,128)S(1)}, f32[32,8]{0,1:T(8,128)}, u32[]{:S(2)}) copy-start(f32[32,8]{0,1:T(8,128)} %param.24) | copy-start | bytes 3076
  70.5 18.2 %collective-permute-start.10 = (bf16[256,1024]{1,0:T(8,128)(2,1)S(1)}, bf16[256,1024]{1,0:T(8,128)(2,1)S(1)}, u32[]{:S(2)}, u32[]{:S(2)}) collective-permute-start(bf16[256,1024]{1,0:T(8,128)(2,1)S(1)} %far_down.1), channel_id=1, source_target_pairs={{0,2},{1,3},{2,0},{3,1},{4,6},{5,7},{6,4},{7,5},{8,10},{9,11},{10,... | collective-permute-start | bytes 1572872 | tf_op jit(solution)/shard_map/ppermute | solution.py:364
  72.9 15.8 %collective-permute-start.4 = (bf16[256,256]{1,0:T(8,128)(2,1)S(1)}, bf16[256,256]{1,0:T(8,128)(2,1)S(1)}, u32[]{:S(2)}, u32[]{:S(2)}) collective-permute-start(bf16[256,256]{1,0:T(8,128)(2,1)S(1)} %copy-done), channel_id=1, source_target_pairs={{0,1},{1,2},{2,3},{3,0},{4,5},{5,6},{6,7},{7,4},{8,9},{9,10},{10,1... | collective-permute-start | bytes 393224 | tf_op jit(solution)/shard_map/ppermute | solution.py:364
  73.1 15.6 %collective-permute-start.5 = (bf16[256,256]{1,0:T(8,128)(2,1)S(1)}, bf16[256,256]{1,0:T(8,128)(2,1)S(1)}, u32[]{:S(2)}, u32[]{:S(2)}) collective-permute-start(bf16[256,256]{1,0:T(8,128)(2,1)S(1)} %copy-done), channel_id=1, source_target_pairs={{0,3},{1,0},{2,1},{3,2},{4,7},{5,4},{6,5},{7,6},{8,11},{9,8},{10,9... | collective-permute-start | bytes 393224 | tf_op jit(solution)/shard_map/ppermute | solution.py:364
  90.1 15.3 %all-to-all-start.1 = ((bf16[32,16,512]{2,1,0:T(8,128)(2,1)}), bf16[32,16,512]{2,1,0:T(8,128)(2,1)S(1)}, u32[]{:S(2)}, u32[]{:S(2)}) async-start(bf16[32,16,512]{2,1,0:T(8,128)(2,1)} %bitcast.14), calls=%async_computation.1 | async-start | bytes 1048576 | tf_op jit(solution)/shard_map/all_to_all | solution.py:421

commit v5 on v4

--- a/solution.py
+++ b/solution.py
@@ -82,7 +82,7 @@
     group = depth // size
     width = output_weight.shape[1]
     half = width // 2
-    step = 8
+    step = 16
     blocks = rows // step
     scale = 1.0 / math.sqrt(size)
 
@@ -110,12 +110,13 @@
         for i in range(blocks):
             copy(k_hbm, k_ref, k_sem, i).start()
             copy(v_hbm, v_ref, v_sem, i).start()
-        for weight in weights:
-            weight.start()
         for i in range(blocks):
             place = slice(i * step, (i + 1) * step)
             q = q_ref[place].reshape(step, group, size)
             copy(k_hbm, k_ref, k_sem, i).wait()
+            if i == 0:
+                for weight in weights:
+                    weight.start()
             scores = lax.dot_general(
                 q, k_ref[place], (((2,), (2,)), ((0,), (0,))), preferred_element_type=F32
             )
@@ -199,135 +200,154 @@
     return jnp.concatenate(parts, axis=1).reshape(len(values) * rows, columns)
 
 
-def experts_act(tokens, gain, w_gate, w_up, capacity):
+def expert_act(tokens, gain, w_gate, w_up, across, e, before, capacity):
     roles, slots, half = tokens.shape
     per_dev, width, quarter = w_gate.shape
+    columns = across.shape[1]
     chunk = 512
-
-    def body(x_ref, gain_ref, g_any, u_any, act_ref, g_ref, u_ref, sums, sems):
+    rows = slots // per_dev
+    done = e * rows
+
+    def body(x_ref, gain_ref, g_hbm, u_hbm, w_ref, *rest):
+        before_ref = rest[0] if e else None
+        act_ref, far_ref, g_ref, u_ref, sums, sems = rest[1 if e else 0 :]
         copies = []
         for k in range(width // chunk):
-            rows = pl.ds(k * chunk, chunk)
+            place = pl.ds(k * chunk, chunk)
             copies.append(
                 [
-                    pltpu.make_async_copy(
-                        source.at[:, rows], target.at[:, rows], sems.at[2 * k + i]
-                    )
-                    for i, (source, target) in enumerate(((g_any, g_ref), (u_any, u_ref)))
+                    pltpu.make_async_copy(hbm.at[e, place], ref.at[place], sems.at[2 * k + i])
+                    for i, (hbm, ref) in enumerate(((g_hbm, g_ref), (u_hbm, u_ref)))
                 ]
             )
         for pair in copies:
             for copy in pair:
                 copy.start()
-        square = jnp.zeros((slots, 1), F32)
+        square = jnp.zeros((rows, 1), F32)
         for k in range(width // chunk):
             s, place = divmod(k * chunk, half)
             x = x_ref[s, :, place : place + chunk].astype(F32)
+            x = of_expert(x, e, per_dev, capacity)
             plain = x * (1.0 / gain_ref[s, :, place : place + chunk])
             square = square + jnp.sum(plain * plain, axis=1, keepdims=True)
+            x = x.astype(BF)
             for copy in copies[k]:
                 copy.wait()
-            for e in range(per_dev):
-                one = of_expert(x, e, per_dev, capacity).astype(BF)
-                for i, w_ref in enumerate((g_ref, u_ref)):
-                    product = jnp.dot(
-                        one, w_ref[e, k * chunk : (k + 1) * chunk], preferred_element_type=F32
-                    )
-                    if k:
-                        product = product + sums[2 * e + i]
-                    sums[2 * e + i] = product
+            for i, ref in enumerate((g_ref, u_ref)):
+                product = jnp.dot(
+                    x, ref[k * chunk : (k + 1) * chunk], preferred_element_type=F32
+                )
+                sums[i] = product + sums[i] if k else product
         inverse = lax.rsqrt(square / width + EPS)
-        gate = of_all([sums[2 * e] for e in range(per_dev)], capacity) * inverse
-        upper = of_all([sums[2 * e + 1] for e in range(per_dev)], capacity) * inverse
-        act_ref[...] = (gate / (1.0 + jnp.exp(-gate)) * upper).astype(BF)
+        gate, upper = sums[0] * inverse, sums[1] * inverse
+        act = (gate / (1.0 + jnp.exp(-gate)) * upper).astype(BF)
+        if e:
+            act_ref[:done] = before_ref[...]
+        act_ref[done:] = act
+        far_ref[...] = jnp.dot(act, w_ref[...], preferred_element_type=F32).astype(BF)
 
     return pl.pallas_call(
         body,
-        out_shape=jax.ShapeDtypeStruct((slots, quarter), BF),
-        in_specs=whole(2) + [pl.BlockSpec(memory_space=pl.ANY)] * 2,
-        out_specs=pl.BlockSpec(memory_space=pltpu.VMEM),
+        out_shape=[
+            jax.ShapeDtypeStruct((done + rows, quarter), BF),
+            jax.ShapeDtypeStruct((rows, columns), BF),
+        ],
+        in_specs=whole(2)
+        + [pl.BlockSpec(memory_space=pltpu.HBM)] * 2
+        + whole(2 if e else 1),
+        out_specs=whole(2),
         scratch_shapes=[
-            pltpu.VMEM(w_gate.shape, BF),
-            pltpu.VMEM(w_up.shape, BF),
-            pltpu.VMEM((2 * per_dev, slots // per_dev, quarter), F32),
+            pltpu.VMEM((width, quarter), BF),
+            pltpu.VMEM((width, quarter), BF),
+            pltpu.VMEM((2, rows, quarter), F32),
             pltpu.SemaphoreType.DMA((2 * (width // chunk),)),
         ],
         compiler_params=pltpu.CompilerParams(vmem_limit_bytes=57 << 20),
         cost_estimate=pl.CostEstimate(
-            flops=4 * slots * width * quarter, bytes_accessed=10 << 20, transcendentals=0
+            flops=4 * rows * width * quarter, bytes_accessed=6 << 20, transcendentals=0
         ),
-        name="experts_act",
-    )(tokens, gain, w_gate, w_up)
-
-
-def far_down(act, downs, capacity):
-    slots, _ = act.shape
-    per_dev = len(downs)
-    columns = downs[0].shape[1]
-
-    def body(a_ref, *refs):
-        w_refs, out_ref = refs[:-1], refs[-1]
-        value = a_ref[...].astype(F32)
-        products = [
-            jnp.dot(
-                of_expert(value, e, per_dev, capacity).astype(BF),
-                w_ref[...],
-                preferred_element_type=F32,
-            )
-            for e, w_ref in enumerate(w_refs)
-        ]
-        out_ref[...] = of_all(products, capacity).astype(BF)
-
-    return pl.pallas_call(
-        body,
-        out_shape=jax.ShapeDtypeStruct((slots, columns), BF),
-        in_specs=whole(1 + per_dev),
-        out_specs=pl.BlockSpec(memory_space=pltpu.VMEM),
-        compiler_params=pltpu.CompilerParams(vmem_limit_bytes=24 << 20),
-        name="far_down",
-    )(act, *downs)
-
-
-def experts_down(acts, downs, far, capacity, roles):
+        name=f"expert_act_{e}",
+    )(tokens, gain, w_gate, w_up, across, *([before] if e else []))
+
+
+def experts_down(acts, downs, fars, capacity, roles):
     count = len(acts)
     slots, quarter = acts[0].shape
-    per_dev = len(downs[0])
-    columns = downs[0][0].shape[1]
+    per_dev = len(fars)
+    rows, columns = fars[0].shape
     piece = columns // roles
 
     def body(*refs):
-        a_refs, w_refs, (far_ref, out_ref) = refs[:count], refs[count:-2], refs[-2:]
-        ones = [
-            [of_expert(a[...].astype(F32), e, per_dev, capacity).astype(BF) for e in range(per_dev)]
-            for a in a_refs
-        ]
+        a_refs, w_refs = refs[:count], refs[count : count + count * per_dev]
+        far_refs, out_ref = refs[count + count * per_dev : -1], refs[-1]
         for s in range(roles):
             totals = []
             for e in range(per_dev):
-                total = None
+                total = far_refs[e][:, s * piece : (s + 1) * piece].astype(F32)
                 for i in range(count):
-                    product = jnp.dot(
-                        ones[i][e],
+                    total = total + jnp.dot(
+                        a_refs[i][e * rows : (e + 1) * rows],
                         w_refs[i * per_dev + e][:, s * piece : (s + 1) * piece],
                         preferred_element_type=F32,
                     )
-                    total = product if total is None else total + product
                 totals.append(total)
-            total = of_all(totals, capacity) + far_ref[:, s * piece : (s + 1) * piece].astype(F32)
-            out_ref[s * slots : (s + 1) * slots] = total.astype(BF)
+            out_ref[s * slots : (s + 1) * slots] = of_all(totals, capacity).astype(BF)
 
     flat = [w for each in downs for w in each]
     return pl.pallas_call(
         body,
         out_shape=jax.ShapeDtypeStruct((roles * slots, piece), BF),
-        in_specs=whole(count + len(flat) + 1),
+        in_specs=whole(count + len(flat) + per_dev),
         out_specs=pl.BlockSpec(memory_space=pltpu.VMEM),
         compiler_params=pltpu.CompilerParams(vmem_limit_bytes=24 << 20),
         cost_estimate=pl.CostEstimate(
             flops=2 * slots * count * quarter * columns, bytes_accessed=5 << 20, transcendentals=0
         ),
         name="experts_down",
-    )(*acts, *flat, far)
+    )(*acts, *flat, *fars)
+
+
+def choose(parts, residual, gain, pick):
+    rows, half = residual.shape
+    slots = pick.shape[0]
+    count = len(parts)
+    steps = 4
+    block = slots // steps
+
+    def body(*refs):
+        part_refs = refs[:count]
+        resid_ref, gain_ref, pick_ref, hidden_ref, out_ref, scaled_ref = refs[count:]
+
+        @pl.when(pl.program_id(0) == 0)
+        def _():
+            hidden = resid_ref[...].astype(F32)
+            for ref in part_refs:
+                hidden = hidden + ref[...].astype(F32)
+            hidden_ref[...] = hidden
+            scaled_ref[...] = (hidden * gain_ref[...]).astype(BF)
+
+        out_ref[...] = jnp.dot(
+            pick_ref[...], scaled_ref[...], preferred_element_type=F32
+        ).astype(BF)
+
+    fixed = pl.BlockSpec((rows, half), lambda i: (0, 0))
+    return pl.pallas_call(
+        body,
+        grid=(steps,),
+        out_shape=[
+            jax.ShapeDtypeStruct((rows, half), F32),
+            jax.ShapeDtypeStruct((slots, half), BF),
+        ],
+        in_specs=[fixed] * (count + 1)
+        + [
+            pl.BlockSpec((1, half), lambda i: (0, 0)),
+            pl.BlockSpec((block, rows), lambda i: (i, 0)),
+        ],
+        out_specs=[fixed, pl.BlockSpec((block, half), lambda i: (i, 0))],
+        scratch_shapes=[pltpu.VMEM((rows, half), BF)],
+        compiler_params=pltpu.CompilerParams(vmem_limit_bytes=24 << 20),
+        name="choose",
+    )(*parts, residual, gain, pick)
 
 
 def per_device(
@@ -381,19 +401,6 @@
     across, near = heads_count // 2, (0, 1, heads_count - 1)
     pieces = [(step, e) for step in (*near, across) for e in range(per_dev)]
     rest = cut_down(w_down, head, heads_count, roles, pieces)
-    total = chip.astype(F32)
-    for step in range(1, heads_count):
-        total = total + shift(chip, step).astype(F32)
-    first = role == 0
-    resid = jnp.where(first, residual[:, :half], residual[:, half:]).astype(F32)
-    gain = jnp.where(first, norm_gain[:half], norm_gain[half:])
-    hidden = resid + total
-    hidden, *rest = lax.optimization_barrier((hidden, *rest))
-    downs = [
-        [shift(part, step) if step else part for part in rest[i * per_dev : (i + 1) * per_dev]]
-        for i, step in enumerate(near)
-    ]
-    scaled = (hidden * gain).astype(BF)
 
     named = routes[:, :, None] == jnp.arange(experts, dtype=jnp.int32)
     chosen = jnp.any(named, axis=1)
@@ -404,19 +411,31 @@
     rank = jnp.dot(before, chosen.astype(BF), preferred_element_type=F32).astype(jnp.int32)
     taken = chosen[:, :, None] & (rank[:, :, None] == jnp.arange(capacity, dtype=jnp.int32))
     slots = experts * capacity
-    pick = taken.reshape(rows_here, slots).astype(BF)
+    pick = taken.reshape(rows_here, slots).T.astype(BF)
     mixing = jnp.where(taken, coef[:, :, None], F32(0.0)).reshape(rows_here, slots)
 
-    outgoing = lax.dot_general(
-        pick, scaled, (((0,), (0,)), ((), ())), preferred_element_type=F32
-    ).astype(BF)
+    parts = [shift(chip, step) if step else chip for step in range(heads_count)]
+    first = role == 0
+    resid = jnp.where(first, residual[:, :half], residual[:, half:])
+    gain = jnp.where(first, norm_gain[:half], norm_gain[half:]).reshape(1, half)
+    parts[0], *rest = lax.optimization_barrier((parts[0], *rest))
+    hidden, outgoing = choose(parts, resid, gain, pick)
+    hidden, *rest = lax.optimization_barrier((hidden, *rest))
+    downs = [
+        [shift(part, step) if step else part for part in rest[i * per_dev : (i + 1) * per_dev]]
+        for i, step in enumerate(near)
+    ]
     outgoing = outgoing.reshape(roles * shards, per_dev * capacity, half)
     incoming = lax.all_to_all(outgoing, ("role", "rows"), 0, 0, tiled=True)
     tokens = incoming.reshape(roles, shards * per_dev * capacity, half)
-    act = experts_act(tokens, norm_gain.reshape(roles, 1, half), w_gate, w_up, capacity)
-    far = shift(far_down(act, rest[len(near) * per_dev :], capacity), across)
+    flat_gain = norm_gain.reshape(roles, 1, half)
+    act, fars = None, []
+    for e in range(per_dev):
+        opposite = rest[len(near) * per_dev + e]
+        act, far = expert_act(tokens, flat_gain, w_gate, w_up, opposite, e, act, capacity)
+        fars.append(shift(far, across))
     acts = [shift(act, step) if step else act for step in near]
-    result = experts_down(acts, downs, far, capacity, roles)
+    result = experts_down(acts, downs, fars, capacity, roles)
     result = result.reshape(roles * shards, per_dev * capacity, piece)
     returned = lax.all_to_all(result, ("role", "rows"), 0, 0, tiled=True)
     returned = returned.reshape(slots, piece)

time: 107 us -> 110 us (1.028)
  Pallas kernels: 21.1 us -> 26.5 us
  matrix products: 3.3 us -> 1.23 us
    pallas_call x2 -> x3, Pallas kernels: 6.54 us -> 12.8 us  [the longest x2 10.3 us: expert_act(): pl.pallas_call(body, out_shape=[jax.ShapeDtypeStruct((done + rows, quarte...]
    dot_general x1 -> x0, matrix products: 2.07 us -> none  [per_device(): lax.dot_general(pick, scaled, (((0,), (0,)), ((), ())), preferred_element...]
    ppermute x10 -> x11, starting transfers between devices: 14.3 us -> 14.9 us  [shift(): lax.ppermute(x, 'heads', [(i, (i + step) % heads_count) for i in range(he...]
    ppermute x10 -> x11, waiting for transfers between devices: 14.2 us -> 13.8 us  [shift(): lax.ppermute(x, 'heads', [(i, (i + step) % heads_count) for i in range(he...]
  transfers between devices with their start and end apart: 13 -> 14, of which waited for: 5 -> 5; matrix products, arithmetic and copies ran while one was open for 1% -> 1% of each run, Pallas kernels for 10% -> 13%
where the time goes in v5:
time: 110 us
  waiting for transfers between devices  49.2 us (45%)
  starting transfers between devices  30 us (27%)
  Pallas kernels  26.5 us (24%)
  local copies, waits for them, and re-layouts  1.44 us (1%)
  other arithmetic  1.43 us (1%)
  matrix products  1.23 us (1%)
    all_to_all x1, waiting for transfers between devices, per_device(): incoming = lax.all_to_all(outgoing, ('role', 'rows'), 0, 0, tiled=True)  24.2 us
    ppermute x11, starting transfers between devices, shift(): lax.ppermute(x, 'heads', [(i, (i + step) % heads_count) for i in range(he...  14.9 us
    ppermute x11, waiting for transfers between devices, shift(): lax.ppermute(x, 'heads', [(i, (i + step) % heads_count) for i in range(he...  13.8 us
    all_to_all x1, waiting for transfers between devices, per_device(): returned = lax.all_to_all(result, ('role', 'rows'), 0, 0, tiled=True)  10.7 us
    pallas_call x2, Pallas kernels, expert_act(): pl.pallas_call(body, out_shape=[jax.ShapeDtypeStruct((done + rows, quarte...  10.3 us
    all_to_all x1, starting transfers between devices, per_device(): incoming = lax.all_to_all(outgoing, ('role', 'rows'), 0, 0, tiled=True)  9.36 us
    pallas_call x1, Pallas kernels, attend(): pl.pallas_call(body, out_shape=[jax.ShapeDtypeStruct((rows, half), BF), j...  8.54 us
    all_to_all x1, starting transfers between devices, per_device(): returned = lax.all_to_all(result, ('role', 'rows'), 0, 0, tiled=True)  4.19 us
  transfers between devices with their start and end apart: 14, of which 5 were waited for; matrix products, arithmetic and copies ran while one was open for 1% of the time, Pallas kernels for 13%

profile of v5, /device:TPU:1, one launch (start us, length us, event | category | flops | bytes accessed | tf_op | source)
XLA Modules:
  0.0 110.0 jit_solution(8286851068713472566)
XLA Ops:
  0.0 8.5 %attend.1 = (bf16[32,2048]{1,0:T(8,128)(2,1)}, f32[32,2048]{1,0:T(8,128)}) custom-call(s32[1]{0:T(128)} %bitcast.role_ref, s32[32]{0:T(128)} %len_ref.1, bf16[32,1024]{1,0:T(8,128)(2,1)} %bitcast.45, bf16[32,512,128]{2,1,0:T(8,128)(2,1)} %bitcast.41, bf16[32,512,128]{2,1,0:T(8,128)(2,1)} %bitcast.42, bf16[32,128]{1,0:T(8,128)(2,1)} %bitcast.46, ...), custom_call_target="tpu_custom_call" | custom-call | bytes 1048576 | tf_op jit(solution)/shard_map/attend/pallas_call | solution.py:154
  8.6 1.5 %collective-permute-start = (bf16[32,2048]{1,0:T(8,128)(2,1)}, bf16[32,2048]{1,0:T(8,128)(2,1)S(1)}, u32[]{:S(2)}, u32[]{:S(2)}) collective-permute-start(bf16[32,2048]{1,0:T(8,128)(2,1)} %get-tuple-element.42), channel_id=1, source_target_pairs={{0,64},{64,0},{1,65},{65,1},{2,66},{66,2},{3,67},{67,3},{4,68},{68... | collective-permute-start | bytes 393224 | tf_op jit(solution)/shard_map/ppermute | solution.py:398
  11.3 1.0 add_convert_fusion.refs_0_
  12.2 1.4 %collective-permute-start.1 = (bf16[32,2048]{1,0:T(8,128)(2,1)S(1)}, bf16[32,2048]{1,0:T(8,128)(2,1)S(1)}, u32[]{:S(2)}, u32[]{:S(2)}) collective-permute-start(bf16[32,2048]{1,0:T(8,128)(2,1)S(1)} %add_convert_fusion.refs_0_), channel_id=1, source_target_pairs={{0,1},{1,2},{2,3},{3,0},{4,5},{5,6},{6,7},{7,4},{8,9},{9,10},{10,1... | collective-permute-start | bytes 393224 | tf_op jit(solution)/shard_map/ppermute | solution.py:384
  13.6 2.5 %collective-permute-start.2 = (bf16[32,2048]{1,0:T(8,128)(2,1)S(1)}, bf16[32,2048]{1,0:T(8,128)(2,1)S(1)}, u32[]{:S(2)}, u32[]{:S(2)}) collective-permute-start(bf16[32,2048]{1,0:T(8,128)(2,1)S(1)} %add_convert_fusion.refs_0_), channel_id=1, source_target_pairs={{0,2},{1,3},{2,0},{3,1},{4,6},{5,7},{6,4},{7,5},{8,10},{9,11},{10,... | collective-permute-start | bytes 393224 | tf_op jit(solution)/shard_map/ppermute | solution.py:384
  16.1 1.2 %collective-permute-start.3 = (bf16[32,2048]{1,0:T(8,128)(2,1)S(1)}, bf16[32,2048]{1,0:T(8,128)(2,1)S(1)}, u32[]{:S(2)}, u32[]{:S(2)}) collective-permute-start(bf16[32,2048]{1,0:T(8,128)(2,1)S(1)} %add_convert_fusion.refs_0_), channel_id=1, source_target_pairs={{0,3},{1,0},{2,1},{3,2},{4,7},{5,4},{6,5},{7,6},{8,11},{9,8},{10,9... | collective-permute-start | bytes 393224 | tf_op jit(solution)/shard_map/ppermute | solution.py:384
  17.2 3.8 %cut_down.1 = (bf16[256,1024]{1,0:T(8,128)(2,1)}, bf16[256,1024]{1,0:T(8,128)(2,1)}, bf16[256,1024]{1,0:T(8,128)(2,1)}, bf16[256,1024]{1,0:T(8,128)(2,1)}, bf16[...) custom-call(s32[1]{0:T(128)} %bitcast.7.head_ref, ...), custom_call_target="tpu_custom_call" | custom-call | bytes 8388608 | tf_op jit(solution)/shard_map/cut_down/pallas_call | solution.py:61
  21.0 1.1 collective-permute-done.2.refs_2_
  22.1 2.5 %choose.1 = (f32[32,2048]{1,0:T(8,128)S(1)}, bf16[512,2048]{1,0:T(8,128)(2,1)}) custom-call(bf16[32,2048]{1,0:T(8,128)(2,1)S(1)} %add_convert_fusion.refs_0_, bf16[32,2048]{1,0:T(8,128)(2,1)S(1)} %collective-permute-done.1.refs_1_, bf16[32,2048]{1,0:T(8,128)(2,1)S(1)} %collective-permute-done.2.refs_2_, bf16[32,2048]{1,0:T(8,128)(2,1)S(1)} %collective-permute-done.3.refs_3_, ...), custom_call_target="tpu_custom_call" | custom-call | tf_op jit(solution)/shard_map/choose/pallas_call | solution.py:334
  24.6 9.4 %all-to-all-start = ((bf16[32,16,2048]{2,1,0:T(8,128)(2,1)}), bf16[32,16,2048]{2,1,0:T(8,128)(2,1)}, u32[]{:S(2)}, u32[]{:S(2)}) async-start(bf16[32,16,2048]{2,1,0:T(8,128)(2,1)} %bitcast.13), calls=%async_computation | async-start | bytes 4194304 | tf_op jit(solution)/shard_map/all_to_all | solution.py:429
  34.0 1.1 %collective-permute-start.6 = (bf16[256,1024]{1,0:T(8,128)(2,1)}, bf16[256,1024]{1,0:T(8,128)(2,1)S(1)}, u32[]{:S(2)}, u32[]{:S(2)}) collective-permute-start(bf16[256,1024]{1,0:T(8,128)(2,1)} %get-tuple-element.71), channel_id=1, source_target_pairs={{0,1},{1,2},{2,3},{3,0},{4,5},{5,6},{6,7},{7,4},{8,9},{9,10},{10,1... | collective-permute-start | bytes 1572872 | tf_op jit(solution)/shard_map/ppermute | solution.py:384
  35.1 1.0 collective-permute-start.7
  36.1 1.7 %collective-permute-start.8 = (bf16[256,1024]{1,0:T(8,128)(2,1)S(1)}, bf16[256,1024]{1,0:T(8,128)(2,1)S(1)}, u32[]{:S(2)}, u32[]{:S(2)}) collective-permute-start(bf16[256,1024]{1,0:T(8,128)(2,1)S(1)} %copy-done.8), channel_id=1, source_target_pairs={{0,3},{1,0},{2,1},{3,2},{4,7},{5,4},{6,5},{7,6},{8,11},{9,8},{10,9... | collective-permute-start | bytes 1572872 | tf_op jit(solution)/shard_map/ppermute | solution.py:384
  38.2 24.2 %all-to-all-done = bf16[32,16,2048]{2,1,0:T(8,128)(2,1)} async-done(((bf16[32,16,2048]{2,1,0:T(8,128)(2,1)}), bf16[32,16,2048]{2,1,0:T(8,128)(2,1)}, u32[]{:S(2)}, u32[]{:S(2)}) %all-to-all-start) | async-done | bytes 2097184 | tf_op jit(solution)/shard_map/all_to_all | solution.py:429
  62.4 5.1 %expert_act_0.1 = (bf16[128,256]{1,0:T(8,128)(2,1)}, bf16[128,1024]{1,0:T(8,128)(2,1)}) custom-call(bf16[2,256,2048]{2,1,0:T(8,128)(2,1)} %bitcast.14.x_ref, f32[2,1,2048]{2,1,0:T(1,128)} %bitcast.43, bf16[2,4096,256]{2,1,0:T(8,128)(2,1)} %g_hbm.3, bf16[2,4096,256]{2,1,0:T(8,128)(2,1)} %u_hbm.3, bf16[256,1024]{1,0:T(8,128)(2,1)} %get-tuple-element.66.w_ref), custom_call_target="tpu_custom_call" | custom-call | flops 536870912 | bytes 6291456 | tf_op jit(solution)/shard_map/expert_act_0/pallas_call | solution.py:249
  67.6 5.2 %expert_act_1.1 = (bf16[256,256]{1,0:T(8,128)(2,1)}, bf16[128,1024]{1,0:T(8,128)(2,1)}) custom-call(bf16[2,256,2048]{2,1,0:T(8,128)(2,1)} %bitcast.14.x_ref, f32[2,1,2048]{2,1,0:T(1,128)} %bitcast.44, bf16[2,4096,256]{2,1,0:T(8,128)(2,1)} %g_hbm.3, bf16[2,4096,256]{2,1,0:T(8,128)(2,1)} %u_hbm.3, bf16[256,1024]{1,0:T(8,128)(2,1)} %get-tuple-element.65.w_ref, ...), custom_call_target="tpu_custom_call" | custom-call | flops 536870912 | bytes 6291456 | tf_op jit(solution)/shard_map/expert_act_1/pallas_call | solution.py:249
  72.8 2.4 %collective-permute-start.11 = (bf16[128,1024]{1,0:T(8,128)(2,1)}, bf16[128,1024]{1,0:T(8,128)(2,1)S(1)}, u32[]{:S(2)}, u32[]{:S(2)}) collective-permute-start(bf16[128,1024]{1,0:T(8,128)(2,1)} %get-tuple-element.76), channel_id=1, source_target_pairs={{0,2},{1,3},{2,0},{3,1},{4,6},{5,7},{6,4},{7,5},{8,10},{9,11},{10,... | collective-permute-start | bytes 786440 | tf_op jit(solution)/shard_map/ppermute | solution.py:384
  75.8 1.0 collective-permute-start.4
  76.9 1.6 %collective-permute-start.5 = (bf16[256,256]{1,0:T(8,128)(2,1)}, bf16[256,256]{1,0:T(8,128)(2,1)S(1)}, u32[]{:S(2)}, u32[]{:S(2)}) collective-permute-start(bf16[256,256]{1,0:T(8,128)(2,1)} %get-tuple-element.68.refs_0_), channel_id=1, source_target_pairs={{0,3},{1,0},{2,1},{3,2},{4,7},{5,4},{6,5},{7,6},{8,11},{9,8},{10,9... | collective-permute-start | bytes 393224 | tf_op jit(solution)/shard_map/ppermute | solution.py:384
  78.5 12.7 %collective-permute-done.4.refs_1_ = bf16[256,256]{1,0:T(8,128)(2,1)S(1)} collective-permute-done((bf16[256,256]{1,0:T(8,128)(2,1)}, bf16[256,256]{1,0:T(8,128)(2,1)S(1)}, u32[]{:S(2)}, u32[]{:S(2)}) %collective-permute-start.4) | collective-permute-done | bytes 131104 | tf_op jit(solution)/shard_map/ppermute | solution.py:384
  91.3 0.9 copy-done.2
  92.2 1.4 %experts_down.1 = bf16[512,512]{1,0:T(8,128)(2,1)} custom-call(bf16[256,256]{1,0:T(8,128)(2,1)S(1)} %copy-done.2, bf16[256,256]{1,0:T(8,128)(2,1)S(1)} %collective-permute-done.4.refs_1_, bf16[256,256]{1,0:T(8,128)(2,1)S(1)} %collective-permute-done.5.refs_2_, bf16[256,1024]{1,0:T(8,128)(2,1)S(1)} %copy-done, bf16[256,1024]{1,0:T(8,128)(2,1)S(1)} %copy-done.1, ...), custom_call_target="tpu_custom_call" | custom-call | flops 402653184 | bytes 5242880 | tf_op jit(solution)/shard_map/experts_down/pallas_call | solution.py:297
  93.6 4.2 %all-to-all-start.1 = ((bf16[32,16,512]{2,1,0:T(8,128)(2,1)}), bf16[32,16,512]{2,1,0:T(8,128)(2,1)S(1)}, u32[]{:S(2)}, u32[]{:S(2)}) async-start(bf16[32,16,512]{2,1,0:T(8,128)(2,1)} %bitcast.16), calls=%async_computation.1 | async-start | bytes 1048576 | tf_op jit(solution)/shard_map/all_to_all | solution.py:440
  98.1 10.7 %all-to-all-done.1 = bf16[32,16,512]{2,1,0:T(8,128)(2,1)S(1)} async-done(((bf16[32,16,512]{2,1,0:T(8,128)(2,1)}), bf16[32,16,512]{2,1,0:T(8,128)(2,1)S(1)}, u32[]{:S(2)}, u32[]{:S(2)}) %all-to-all-start.1) | async-done | bytes 524320 | tf_op jit(solution)/shard_map/all_to_all | solution.py:440
  (48 shorter events, 3.7 us)
Async XLA Ops:
  0.0 10.1 %copy-start.6 = (s32[32,8]{0,1:T(8,128)S(1)}, s32[32,8]{0,1:T(8,128)}, u32[]{:S(2)}) copy-start(s32[32,8]{0,1:T(8,128)} %param.23) | copy-start | bytes 3076
  0.0 10.7 %copy-start.3 = (bf16[32,4096]{1,0:T(8,128)(2,1)S(1)}, bf16[32,4096]{1,0:T(8,128)(2,1)}, u32[]{:S(2)}) copy-start(bf16[32,4096]{1,0:T(8,128)(2,1)} %param.21) | copy-start | bytes 786436
  0.0 17.2 %copy-start.4 = (f32[4096]{0:T(1024)S(1)}, f32[4096]{0:T(1024)}, u32[]{:S(2)}) copy-start(f32[4096]{0:T(1024)} %param.22) | copy-start | bytes 49156
  8.6 2.7 %collective-permute-start = (bf16[32,2048]{1,0:T(8,128)(2,1)}, bf16[32,2048]{1,0:T(8,128)(2,1)S(1)}, u32[]{:S(2)}, u32[]{:S(2)}) collective-permute-start(bf16[32,2048]{1,0:T(8,128)(2,1)} %get-tuple-element.42), channel_id=1, source_target_pairs={{0,64},{64,0},{1,65},{65,1},{2,66},{66,2},{3,67},{67,3},{4,68},{68... | collective-permute-start | bytes 393224 | tf_op jit(solution)/shard_map/ppermute | solution.py:398
  12.2 8.8 %collective-permute-start.1 = (bf16[32,2048]{1,0:T(8,128)(2,1)S(1)}, bf16[32,2048]{1,0:T(8,128)(2,1)S(1)}, u32[]{:S(2)}, u32[]{:S(2)}) collective-permute-start(bf16[32,2048]{1,0:T(8,128)(2,1)S(1)} %add_convert_fusion.refs_0_), channel_id=1, source_target_pairs={{0,1},{1,2},{2,3},{3,0},{4,5},{5,6},{6,7},{7,4},{8,9},{9,10},{10,1... | collective-permute-start | bytes 393224 | tf_op jit(solution)/shard_map/ppermute | solution.py:384
  13.6 8.5 %collective-permute-start.2 = (bf16[32,2048]{1,0:T(8,128)(2,1)S(1)}, bf16[32,2048]{1,0:T(8,128)(2,1)S(1)}, u32[]{:S(2)}, u32[]{:S(2)}) collective-permute-start(bf16[32,2048]{1,0:T(8,128)(2,1)S(1)} %add_convert_fusion.refs_0_), channel_id=1, source_target_pairs={{0,2},{1,3},{2,0},{3,1},{4,6},{5,7},{6,4},{7,5},{8,10},{9,11},{10,... | collective-permute-start | bytes 393224 | tf_op jit(solution)/shard_map/ppermute | solution.py:384
  16.1 6.1 %collective-permute-start.3 = (bf16[32,2048]{1,0:T(8,128)(2,1)S(1)}, bf16[32,2048]{1,0:T(8,128)(2,1)S(1)}, u32[]{:S(2)}, u32[]{:S(2)}) collective-permute-start(bf16[32,2048]{1,0:T(8,128)(2,1)S(1)} %add_convert_fusion.refs_0_), channel_id=1, source_target_pairs={{0,3},{1,0},{2,1},{3,2},{4,7},{5,4},{6,5},{7,6},{8,11},{9,8},{10,9... | collective-permute-start | bytes 393224 | tf_op jit(solution)/shard_map/ppermute | solution.py:384
  21.0 15.1 %copy-start.8 = (bf16[256,1024]{1,0:T(8,128)(2,1)S(1)}, bf16[256,1024]{1,0:T(8,128)(2,1)}, u32[]{:S(2)}) copy-start(bf16[256,1024]{1,0:T(8,128)(2,1)} %get-tuple-element.73) | copy-start | bytes 1572868
  21.0 16.8 %copy-start.7 = (bf16[256,1024]{1,0:T(8,128)(2,1)S(1)}, bf16[256,1024]{1,0:T(8,128)(2,1)}, u32[]{:S(2)}) copy-start(bf16[256,1024]{1,0:T(8,128)(2,1)} %get-tuple-element.74) | copy-start | bytes 1572868
  24.6 37.8 %all-to-all-start = ((bf16[32,16,2048]{2,1,0:T(8,128)(2,1)}), bf16[32,16,2048]{2,1,0:T(8,128)(2,1)}, u32[]{:S(2)}, u32[]{:S(2)}) async-start(bf16[32,16,2048]{2,1,0:T(8,128)(2,1)} %bitcast.13), calls=%async_computation | async-start | bytes 4194304 | tf_op jit(solution)/shard_map/all_to_all | solution.py:429
  34.0 41.2 %collective-permute-start.6 = (bf16[256,1024]{1,0:T(8,128)(2,1)}, bf16[256,1024]{1,0:T(8,128)(2,1)S(1)}, u32[]{:S(2)}, u32[]{:S(2)}) collective-permute-start(bf16[256,1024]{1,0:T(8,128)(2,1)} %get-tuple-element.71), channel_id=1, source_target_pairs={{0,1},{1,2},{2,3},{3,0},{4,5},{5,6},{6,7},{7,4},{8,9},{9,10},{10,1... | collective-permute-start | bytes 1572872 | tf_op jit(solution)/shard_map/ppermute | solution.py:384
  35.1 40.7 %collective-permute-start.7 = (bf16[256,1024]{1,0:T(8,128)(2,1)}, bf16[256,1024]{1,0:T(8,128)(2,1)S(1)}, u32[]{:S(2)}, u32[]{:S(2)}) collective-permute-start(bf16[256,1024]{1,0:T(8,128)(2,1)} %get-tuple-element.72), channel_id=1, source_target_pairs={{0,1},{1,2},{2,3},{3,0},{4,5},{5,6},{6,7},{7,4},{8,9},{9,10},{10,1... | collective-permute-start | bytes 1572872 | tf_op jit(solution)/shard_map/ppermute | solution.py:384
  36.1 40.8 %collective-permute-start.8 = (bf16[256,1024]{1,0:T(8,128)(2,1)S(1)}, bf16[256,1024]{1,0:T(8,128)(2,1)S(1)}, u32[]{:S(2)}, u32[]{:S(2)}) collective-permute-start(bf16[256,1024]{1,0:T(8,128)(2,1)S(1)} %copy-done.8), channel_id=1, source_target_pairs={{0,3},{1,0},{2,1},{3,2},{4,7},{5,4},{6,5},{7,6},{8,11},{9,8},{10,9... | collective-permute-start | bytes 1572872 | tf_op jit(solution)/shard_map/ppermute | solution.py:384
  37.8 40.7 %collective-permute-start.9 = (bf16[256,1024]{1,0:T(8,128)(2,1)S(1)}, bf16[256,1024]{1,0:T(8,128)(2,1)S(1)}, u32[]{:S(2)}, u32[]{:S(2)}) collective-permute-start(bf16[256,1024]{1,0:T(8,128)(2,1)S(1)} %copy-done.7), channel_id=1, source_target_pairs={{0,3},{1,0},{2,1},{3,2},{4,7},{5,4},{6,5},{7,6},{8,11},{9,8},{10,9... | collective-permute-start | bytes 1572872 | tf_op jit(solution)/shard_map/ppermute | solution.py:384
  67.5 7.7 %copy-start.9 = (bf16[128,1024]{1,0:T(8,128)(2,1)S(1)}, bf16[128,1024]{1,0:T(8,128)(2,1)}, u32[]{:S(2)}) copy-start(bf16[128,1024]{1,0:T(8,128)(2,1)} %get-tuple-element.75) | copy-start | bytes 786436
  67.6 23.7 %copy-start = (bf16[256,1024]{1,0:T(8,128)(2,1)S(1)}, bf16[256,1024]{1,0:T(8,128)(2,1)}, u32[]{:S(2)}) copy-start(bf16[256,1024]{1,0:T(8,128)(2,1)} %get-tuple-element.69.refs_3_) | copy-start | bytes 1572868
  67.6 23.7 %copy-start.1 = (bf16[256,1024]{1,0:T(8,128)(2,1)S(1)}, bf16[256,1024]{1,0:T(8,128)(2,1)}, u32[]{:S(2)}) copy-start(bf16[256,1024]{1,0:T(8,128)(2,1)} %get-tuple-element.70.refs_4_) | copy-start | bytes 1572868
  72.8 25.0 %copy-start.5 = (f32[32,8]{0,1:T(8,128)S(1)}, f32[32,8]{0,1:T(8,128)}, u32[]{:S(2)}) copy-start(f32[32,8]{0,1:T(8,128)} %param.24) | copy-start | bytes 3076
  72.8 18.5 %collective-permute-start.11 = (bf16[128,1024]{1,0:T(8,128)(2,1)}, bf16[128,1024]{1,0:T(8,128)(2,1)S(1)}, u32[]{:S(2)}, u32[]{:S(2)}) collective-permute-start(bf16[128,1024]{1,0:T(8,128)(2,1)} %get-tuple-element.76), channel_id=1, source_target_pairs={{0,2},{1,3},{2,0},{3,1},{4,6},{5,7},{6,4},{7,5},{8,10},{9,11},{10,... | collective-permute-start | bytes 786440 | tf_op jit(solution)/shard_map/ppermute | solution.py:384
  75.2 16.0 %collective-permute-start.10 = (bf16[128,1024]{1,0:T(8,128)(2,1)S(1)}, bf16[128,1024]{1,0:T(8,128)(2,1)S(1)}, u32[]{:S(2)}, u32[]{:S(2)}) collective-permute-start(bf16[128,1024]{1,0:T(8,128)(2,1)S(1)} %copy-done.9), channel_id=1, source_target_pairs={{0,2},{1,3},{2,0},{3,1},{4,6},{5,7},{6,4},{7,5},{8,10},{9,11},{10,... | collective-permute-start | bytes 786440 | tf_op jit(solution)/shard_map/ppermute | solution.py:384
  75.8 15.4 %collective-permute-start.4 = (bf16[256,256]{1,0:T(8,128)(2,1)}, bf16[256,256]{1,0:T(8,128)(2,1)S(1)}, u32[]{:S(2)}, u32[]{:S(2)}) collective-permute-start(bf16[256,256]{1,0:T(8,128)(2,1)} %get-tuple-element.68.refs_0_), channel_id=1, source_target_pairs={{0,1},{1,2},{2,3},{3,0},{4,5},{5,6},{6,7},{7,4},{8,9},{9,10},{10,1... | collective-permute-start | bytes 393224 | tf_op jit(solution)/shard_map/ppermute | solution.py:384
  76.9 14.3 %collective-permute-start.5 = (bf16[256,256]{1,0:T(8,128)(2,1)}, bf16[256,256]{1,0:T(8,128)(2,1)S(1)}, u32[]{:S(2)}, u32[]{:S(2)}) collective-permute-start(bf16[256,256]{1,0:T(8,128)(2,1)} %get-tuple-element.68.refs_0_), channel_id=1, source_target_pairs={{0,3},{1,0},{2,1},{3,2},{4,7},{5,4},{6,5},{7,6},{8,11},{9,8},{10,9... | collective-permute-start | bytes 393224 | tf_op jit(solution)/shard_map/ppermute | solution.py:384
  91.3 0.9 copy-start.2
  93.6 15.3 %all-to-all-start.1 = ((bf16[32,16,512]{2,1,0:T(8,128)(2,1)}), bf16[32,16,512]{2,1,0:T(8,128)(2,1)S(1)}, u32[]{:S(2)}, u32[]{:S(2)}) async-start(bf16[32,16,512]{2,1,0:T(8,128)(2,1)} %bitcast.16), calls=%async_computation.1 | async-start | bytes 1048576 | tf_op jit(solution)/shard_map/all_to_all | solution.py:440

commit v6 on v4

--- a/solution.py
+++ b/solution.py
@@ -82,7 +82,7 @@
     group = depth // size
     width = output_weight.shape[1]
     half = width // 2
-    step = 8
+    step = 16
     blocks = rows // step
     scale = 1.0 / math.sqrt(size)
 
@@ -110,12 +110,13 @@
         for i in range(blocks):
             copy(k_hbm, k_ref, k_sem, i).start()
             copy(v_hbm, v_ref, v_sem, i).start()
-        for weight in weights:
-            weight.start()
         for i in range(blocks):
             place = slice(i * step, (i + 1) * step)
             q = q_ref[place].reshape(step, group, size)
             copy(k_hbm, k_ref, k_sem, i).wait()
+            if i == 0:
+                for weight in weights:
+                    weight.start()
             scores = lax.dot_general(
                 q, k_ref[place], (((2,), (2,)), ((0,), (0,))), preferred_element_type=F32
             )
@@ -244,7 +245,7 @@
     return pl.pallas_call(
         body,
         out_shape=jax.ShapeDtypeStruct((slots, quarter), BF),
-        in_specs=whole(2) + [pl.BlockSpec(memory_space=pl.ANY)] * 2,
+        in_specs=whole(2) + [pl.BlockSpec(memory_space=pltpu.HBM)] * 2,
         out_specs=pl.BlockSpec(memory_space=pltpu.VMEM),
         scratch_shapes=[
             pltpu.VMEM(w_gate.shape, BF),
@@ -252,7 +253,7 @@
             pltpu.VMEM((2 * per_dev, slots // per_dev, quarter), F32),
             pltpu.SemaphoreType.DMA((2 * (width // chunk),)),
         ],
-        compiler_params=pltpu.CompilerParams(vmem_limit_bytes=57 << 20),
+        compiler_params=pltpu.CompilerParams(vmem_limit_bytes=49 << 20),
         cost_estimate=pl.CostEstimate(
             flops=4 * slots * width * quarter, bytes_accessed=10 << 20, transcendentals=0
         ),

time: 107 us -> 104 us (0.972)
  Pallas kernels: 21.1 us -> 19.2 us
    pallas_call x1, Pallas kernels: 6.23 us -> 4 us  [experts_act(): pl.pallas_call(body, out_shape=jax.ShapeDtypeStruct((slots, quarter), BF)...]
    pallas_call x1, Pallas kernels: 1.39 us -> 2.59 us  [experts_down(): pl.pallas_call(body, out_shape=jax.ShapeDtypeStruct((roles * slots, piece...]
  transfers between devices with their start and end apart: 13 -> 13, of which waited for: 5 -> 5; matrix products, arithmetic and copies ran while one was open for 1% -> 1% of each run, Pallas kernels for 10% -> 8%
where the time goes in v6:
time: 104 us
  waiting for transfers between devices  49.7 us (48%)
  starting transfers between devices  29.3 us (28%)
  Pallas kernels  19.2 us (18%)
  matrix products  3.32 us (3%)
  other arithmetic  1.39 us (1%)
    all_to_all x1, waiting for transfers between devices, per_device(): incoming = lax.all_to_all(outgoing, ('role', 'rows'), 0, 0, tiled=True)  24.2 us
    ppermute x10, starting transfers between devices, shift(): lax.ppermute(x, 'heads', [(i, (i + step) % heads_count) for i in range(he...  14.3 us
    ppermute x10, waiting for transfers between devices, shift(): lax.ppermute(x, 'heads', [(i, (i + step) % heads_count) for i in range(he...  14.2 us
    all_to_all x1, waiting for transfers between devices, per_device(): returned = lax.all_to_all(result, ('role', 'rows'), 0, 0, tiled=True)  10.7 us
    all_to_all x1, starting transfers between devices, per_device(): incoming = lax.all_to_all(outgoing, ('role', 'rows'), 0, 0, tiled=True)  9.3 us
    pallas_call x1, Pallas kernels, attend(): pl.pallas_call(body, out_shape=[jax.ShapeDtypeStruct((rows, half), BF), j...  8.52 us
    all_to_all x1, starting transfers between devices, per_device(): returned = lax.all_to_all(result, ('role', 'rows'), 0, 0, tiled=True)  4.19 us
    pallas_call x1, Pallas kernels, experts_act(): pl.pallas_call(body, out_shape=jax.ShapeDtypeStruct((slots, quarter), BF)...  4 us
  transfers between devices with their start and end apart: 13, of which 5 were waited for; matrix products, arithmetic and copies ran while one was open for 1% of the time, Pallas kernels for 8%

profile of v6, /device:TPU:1, one launch (start us, length us, event | category | flops | bytes accessed | tf_op | source)
XLA Modules:
  0.0 103.6 jit_solution(2231532009701547279)
XLA Ops:
  0.0 8.5 %attend.1 = (bf16[32,2048]{1,0:T(8,128)(2,1)}, f32[32,2048]{1,0:T(8,128)}) custom-call(s32[1]{0:T(128)} %bitcast.role_ref, s32[32]{0:T(128)} %len_ref.1, bf16[32,1024]{1,0:T(8,128)(2,1)} %bitcast.40, bf16[32,512,128]{2,1,0:T(8,128)(2,1)} %bitcast.38, bf16[32,512,128]{2,1,0:T(8,128)(2,1)} %bitcast.39, bf16[32,128]{1,0:T(8,128)(2,1)} %bitcast.41, ...), custom_call_target="tpu_custom_call" | custom-call | bytes 1048576 | tf_op jit(solution)/shard_map/attend/pallas_call | solution.py:154
  8.5 1.5 %collective-permute-start = (bf16[32,2048]{1,0:T(8,128)(2,1)}, bf16[32,2048]{1,0:T(8,128)(2,1)S(1)}, u32[]{:S(2)}, u32[]{:S(2)}) collective-permute-start(bf16[32,2048]{1,0:T(8,128)(2,1)} %get-tuple-element.27), channel_id=1, source_target_pairs={{0,64},{64,0},{1,65},{65,1},{2,66},{66,2},{3,67},{67,3},{4,68},{68... | collective-permute-start | bytes 393224 | tf_op jit(solution)/shard_map/ppermute | solution.py:379
  10.7 0.6 collective-permute-done
  11.2 1.0 add_convert_fusion
  12.2 1.4 %collective-permute-start.1 = (bf16[32,2048]{1,0:T(8,128)(2,1)S(1)}, bf16[32,2048]{1,0:T(8,128)(2,1)S(1)}, u32[]{:S(2)}, u32[]{:S(2)}) collective-permute-start(bf16[32,2048]{1,0:T(8,128)(2,1)S(1)} %add_convert_fusion), channel_id=1, source_target_pairs={{0,1},{1,2},{2,3},{3,0},{4,5},{5,6},{6,7},{7,4},{8,9},{9,10},{10,1... | collective-permute-start | bytes 393224 | tf_op jit(solution)/shard_map/ppermute | solution.py:365
  13.6 2.5 %collective-permute-start.2 = (bf16[32,2048]{1,0:T(8,128)(2,1)S(1)}, bf16[32,2048]{1,0:T(8,128)(2,1)S(1)}, u32[]{:S(2)}, u32[]{:S(2)}) collective-permute-start(bf16[32,2048]{1,0:T(8,128)(2,1)S(1)} %add_convert_fusion), channel_id=1, source_target_pairs={{0,2},{1,3},{2,0},{3,1},{4,6},{5,7},{6,4},{7,5},{8,10},{9,11},{10,... | collective-permute-start | bytes 393224 | tf_op jit(solution)/shard_map/ppermute | solution.py:365
  16.0 1.2 %collective-permute-start.3 = (bf16[32,2048]{1,0:T(8,128)(2,1)S(1)}, bf16[32,2048]{1,0:T(8,128)(2,1)S(1)}, u32[]{:S(2)}, u32[]{:S(2)}) collective-permute-start(bf16[32,2048]{1,0:T(8,128)(2,1)S(1)} %add_convert_fusion), channel_id=1, source_target_pairs={{0,3},{1,0},{2,1},{3,2},{4,7},{5,4},{6,5},{7,6},{8,11},{9,8},{10,9... | collective-permute-start | bytes 393224 | tf_op jit(solution)/shard_map/ppermute | solution.py:365
  17.2 3.8 %cut_down.1 = (bf16[256,1024]{1,0:T(8,128)(2,1)}, bf16[256,1024]{1,0:T(8,128)(2,1)}, bf16[256,1024]{1,0:T(8,128)(2,1)}, bf16[256,1024]{1,0:T(8,128)(2,1)}, bf16[...) custom-call(s32[1]{0:T(128)} %bitcast.7.head_ref, ...), custom_call_target="tpu_custom_call" | custom-call | bytes 8388608 | tf_op jit(solution)/shard_map/cut_down/pallas_call | solution.py:61
  21.0 1.1 %collective-permute-done.2 = bf16[32,2048]{1,0:T(8,128)(2,1)S(1)} collective-permute-done((bf16[32,2048]{1,0:T(8,128)(2,1)S(1)}, bf16[32,2048]{1,0:T(8,128)(2,1)S(1)}, u32[]{:S(2)}, u32[]{:S(2)}) %collective-permute-start.2) | collective-permute-done | bytes 131104 | tf_op jit(solution)/shard_map/ppermute | solution.py:365
  22.2 2.1 %convolution_convert_fusion = bf16[512,2048]{1,0:T(8,128)(2,1)} fusion(f32[32,2048]{1,0:T(8,128)S(1)} %add_add_fusion, f32[2048]{0:T(1024)S(1)} %slice_select_fusion, s32[512]{0:T(512)S(1)} %eq.64, s32[32,64]{0,1:T(8,128)S(1)} %copy.22, pred[32,64]{0,1:T(8,128)(4,1)S(1)} %copy.21), kind=kOutput, calls=%fused_computation | convolution fusion | flops 68321280 | bytes 2379776 | tf_op jit(solution)/shard_map/dot_general | solution.py:411
  24.3 9.3 %all-to-all-start = ((bf16[32,16,2048]{2,1,0:T(8,128)(2,1)}), bf16[32,16,2048]{2,1,0:T(8,128)(2,1)S(1)}, u32[]{:S(2)}, u32[]{:S(2)}) async-start(bf16[32,16,2048]{2,1,0:T(8,128)(2,1)} %bitcast.35), calls=%async_computation | async-start | bytes 4194304 | tf_op jit(solution)/shard_map/all_to_all | solution.py:415
  33.6 1.1 %collective-permute-start.6 = (bf16[256,1024]{1,0:T(8,128)(2,1)}, bf16[256,1024]{1,0:T(8,128)(2,1)S(1)}, u32[]{:S(2)}, u32[]{:S(2)}) collective-permute-start(bf16[256,1024]{1,0:T(8,128)(2,1)} %get-tuple-element.41), channel_id=1, source_target_pairs={{0,1},{1,2},{2,3},{3,0},{4,5},{5,6},{6,7},{7,4},{8,9},{9,10},{10,1... | collective-permute-start | bytes 1572872 | tf_op jit(solution)/shard_map/ppermute | solution.py:365
  34.7 1.0 collective-permute-start.7
  35.7 1.7 %collective-permute-start.8 = (bf16[256,1024]{1,0:T(8,128)(2,1)}, bf16[256,1024]{1,0:T(8,128)(2,1)}, u32[]{:S(2)}, u32[]{:S(2)}) collective-permute-start(bf16[256,1024]{1,0:T(8,128)(2,1)} %get-tuple-element.43), channel_id=1, source_target_pairs={{0,3},{1,0},{2,1},{3,2},{4,7},{5,4},{6,5},{7,6},{8,11},{9,8},{10,9... | collective-permute-start | bytes 1572872 | tf_op jit(solution)/shard_map/ppermute | solution.py:365
  37.4 0.4 collective-permute-start.9
  37.8 24.2 %all-to-all-done = bf16[32,16,2048]{2,1,0:T(8,128)(2,1)S(1)} async-done(((bf16[32,16,2048]{2,1,0:T(8,128)(2,1)}), bf16[32,16,2048]{2,1,0:T(8,128)(2,1)S(1)}, u32[]{:S(2)}, u32[]{:S(2)}) %all-to-all-start) | async-done | bytes 2097184 | tf_op jit(solution)/shard_map/all_to_all | solution.py:415
  62.0 4.0 %experts_act.1.a_ref.refs_0_ = bf16[256,256]{1,0:T(8,128)(2,1)S(1)} custom-call(bf16[2,256,2048]{2,1,0:T(8,128)(2,1)S(1)} %bitcast.32, f32[2,1,2048]{2,1,0:T(1,128)S(1)} %bitcast.33, bf16[2,4096,256]{2,1,0:T(8,128)(2,1)} %g_any.1, bf16[2,4096,256]{2,1,0:T(8,128)(2,1)} %u_any.1), custom_call_target="tpu_custom_call" | custom-call | flops 1073741824 | bytes 10485760 | tf_op jit(solution)/shard_map/experts_act/pallas_call | solution.py:245
  66.4 2.5 %collective-permute-start.10 = (bf16[256,1024]{1,0:T(8,128)(2,1)S(1)}, bf16[256,1024]{1,0:T(8,128)(2,1)S(1)}, u32[]{:S(2)}, u32[]{:S(2)}) collective-permute-start(bf16[256,1024]{1,0:T(8,128)(2,1)S(1)} %far_down.1), channel_id=1, source_target_pairs={{0,2},{1,3},{2,0},{3,1},{4,6},{5,7},{6,4},{7,5},{8,10},{9,11},{10,... | collective-permute-start | bytes 1572872 | tf_op jit(solution)/shard_map/ppermute | solution.py:365
  69.0 2.5 %collective-permute-start.5 = (bf16[256,256]{1,0:T(8,128)(2,1)S(1)}, bf16[256,256]{1,0:T(8,128)(2,1)S(1)}, u32[]{:S(2)}, u32[]{:S(2)}) collective-permute-start(bf16[256,256]{1,0:T(8,128)(2,1)S(1)} %experts_act.1.a_ref.refs_0_), channel_id=1, source_target_pairs={{0,3},{1,0},{2,1},{3,2},{4,7},{5,4},{6,5},{7,6},{8,11},{9,8},{10,9... | collective-permute-start | bytes 393224 | tf_op jit(solution)/shard_map/ppermute | solution.py:365
  71.5 13.1 %collective-permute-done.4.refs_1_ = bf16[256,256]{1,0:T(8,128)(2,1)S(1)} collective-permute-done((bf16[256,256]{1,0:T(8,128)(2,1)S(1)}, bf16[256,256]{1,0:T(8,128)(2,1)S(1)}, u32[]{:S(2)}, u32[]{:S(2)}) %collective-permute-start.4) | collective-permute-done | bytes 131104 | tf_op jit(solution)/shard_map/ppermute | solution.py:365
  84.6 2.6 %experts_down.1 = bf16[512,512]{1,0:T(8,128)(2,1)} custom-call(bf16[256,256]{1,0:T(8,128)(2,1)S(1)} %experts_act.1.a_ref.refs_0_, bf16[256,256]{1,0:T(8,128)(2,1)S(1)} %collective-permute-done.4.refs_1_, bf16[256,256]{1,0:T(8,128)(2,1)S(1)} %collective-permute-done.5.refs_2_, bf16[256,1024]{1,0:T(8,128)(2,1)S(1)} %copy-done, ...), custom_call_target="tpu_custom_call" | custom-call | flops 402653184 | bytes 5242880 | tf_op jit(solution)/shard_map/experts_down/pallas_call | solution.py:321
  87.2 4.2 %all-to-all-start.1 = ((bf16[32,16,512]{2,1,0:T(8,128)(2,1)}), bf16[32,16,512]{2,1,0:T(8,128)(2,1)S(1)}, u32[]{:S(2)}, u32[]{:S(2)}) async-start(bf16[32,16,512]{2,1,0:T(8,128)(2,1)} %bitcast.14), calls=%async_computation.1 | async-start | bytes 1048576 | tf_op jit(solution)/shard_map/all_to_all | solution.py:422
  91.8 10.7 %all-to-all-done.1 = bf16[32,16,512]{2,1,0:T(8,128)(2,1)S(1)} async-done(((bf16[32,16,512]{2,1,0:T(8,128)(2,1)}), bf16[32,16,512]{2,1,0:T(8,128)(2,1)S(1)}, u32[]{:S(2)}, u32[]{:S(2)}) %all-to-all-start.1) | async-done | bytes 524320 | tf_op jit(solution)/shard_map/all_to_all | solution.py:422
  102.8 0.9 fusion.1
  (41 shorter events, 1.8 us)
Async XLA Ops:
  0.0 10.0 %copy-start.7 = (s32[32,8]{0,1:T(8,128)S(1)}, s32[32,8]{0,1:T(8,128)}, u32[]{:S(2)}) copy-start(s32[32,8]{0,1:T(8,128)} %param.23) | copy-start | bytes 3076
  0.0 17.2 %copy-start.4 = (f32[4096]{0:T(1024)S(1)}, f32[4096]{0:T(1024)}, u32[]{:S(2)}) copy-start(f32[4096]{0:T(1024)} %param.22) | copy-start | bytes 49156
  8.5 13.6 %copy-start.5 = (bf16[32,4096]{1,0:T(8,128)(2,1)S(1)}, bf16[32,4096]{1,0:T(8,128)(2,1)}, u32[]{:S(2)}) copy-start(bf16[32,4096]{1,0:T(8,128)(2,1)} %param.21) | copy-start | bytes 786436
  8.5 2.7 %collective-permute-start = (bf16[32,2048]{1,0:T(8,128)(2,1)}, bf16[32,2048]{1,0:T(8,128)(2,1)S(1)}, u32[]{:S(2)}, u32[]{:S(2)}) collective-permute-start(bf16[32,2048]{1,0:T(8,128)(2,1)} %get-tuple-element.27), channel_id=1, source_target_pairs={{0,64},{64,0},{1,65},{65,1},{2,66},{66,2},{3,67},{67,3},{4,68},{68... | collective-permute-start | bytes 393224 | tf_op jit(solution)/shard_map/ppermute | solution.py:379
  12.2 8.8 %collective-permute-start.1 = (bf16[32,2048]{1,0:T(8,128)(2,1)S(1)}, bf16[32,2048]{1,0:T(8,128)(2,1)S(1)}, u32[]{:S(2)}, u32[]{:S(2)}) collective-permute-start(bf16[32,2048]{1,0:T(8,128)(2,1)S(1)} %add_convert_fusion), channel_id=1, source_target_pairs={{0,1},{1,2},{2,3},{3,0},{4,5},{5,6},{6,7},{7,4},{8,9},{9,10},{10,1... | collective-permute-start | bytes 393224 | tf_op jit(solution)/shard_map/ppermute | solution.py:365
  13.6 8.5 %collective-permute-start.2 = (bf16[32,2048]{1,0:T(8,128)(2,1)S(1)}, bf16[32,2048]{1,0:T(8,128)(2,1)S(1)}, u32[]{:S(2)}, u32[]{:S(2)}) collective-permute-start(bf16[32,2048]{1,0:T(8,128)(2,1)S(1)} %add_convert_fusion), channel_id=1, source_target_pairs={{0,2},{1,3},{2,0},{3,1},{4,6},{5,7},{6,4},{7,5},{8,10},{9,11},{10,... | collective-permute-start | bytes 393224 | tf_op jit(solution)/shard_map/ppermute | solution.py:365
  16.0 6.1 %collective-permute-start.3 = (bf16[32,2048]{1,0:T(8,128)(2,1)S(1)}, bf16[32,2048]{1,0:T(8,128)(2,1)S(1)}, u32[]{:S(2)}, u32[]{:S(2)}) collective-permute-start(bf16[32,2048]{1,0:T(8,128)(2,1)S(1)} %add_convert_fusion), channel_id=1, source_target_pairs={{0,3},{1,0},{2,1},{3,2},{4,7},{5,4},{6,5},{7,6},{8,11},{9,8},{10,9... | collective-permute-start | bytes 393224 | tf_op jit(solution)/shard_map/ppermute | solution.py:365
  24.3 37.7 %all-to-all-start = ((bf16[32,16,2048]{2,1,0:T(8,128)(2,1)}), bf16[32,16,2048]{2,1,0:T(8,128)(2,1)S(1)}, u32[]{:S(2)}, u32[]{:S(2)}) async-start(bf16[32,16,2048]{2,1,0:T(8,128)(2,1)} %bitcast.35), calls=%async_computation | async-start | bytes 4194304 | tf_op jit(solution)/shard_map/all_to_all | solution.py:415
  33.6 35.2 %collective-permute-start.6 = (bf16[256,1024]{1,0:T(8,128)(2,1)}, bf16[256,1024]{1,0:T(8,128)(2,1)S(1)}, u32[]{:S(2)}, u32[]{:S(2)}) collective-permute-start(bf16[256,1024]{1,0:T(8,128)(2,1)} %get-tuple-element.41), channel_id=1, source_target_pairs={{0,1},{1,2},{2,3},{3,0},{4,5},{5,6},{6,7},{7,4},{8,9},{9,10},{10,1... | collective-permute-start | bytes 1572872 | tf_op jit(solution)/shard_map/ppermute | solution.py:365
  34.7 34.3 %collective-permute-start.7 = (bf16[256,1024]{1,0:T(8,128)(2,1)}, bf16[256,1024]{1,0:T(8,128)(2,1)S(1)}, u32[]{:S(2)}, u32[]{:S(2)}) collective-permute-start(bf16[256,1024]{1,0:T(8,128)(2,1)} %get-tuple-element.42), channel_id=1, source_target_pairs={{0,1},{1,2},{2,3},{3,0},{4,5},{5,6},{6,7},{7,4},{8,9},{9,10},{10,1... | collective-permute-start | bytes 1572872 | tf_op jit(solution)/shard_map/ppermute | solution.py:365
  35.7 35.8 %collective-permute-start.8 = (bf16[256,1024]{1,0:T(8,128)(2,1)}, bf16[256,1024]{1,0:T(8,128)(2,1)}, u32[]{:S(2)}, u32[]{:S(2)}) collective-permute-start(bf16[256,1024]{1,0:T(8,128)(2,1)} %get-tuple-element.43), channel_id=1, source_target_pairs={{0,3},{1,0},{2,1},{3,2},{4,7},{5,4},{6,5},{7,6},{8,11},{9,8},{10,9... | collective-permute-start | bytes 1572872 | tf_op jit(solution)/shard_map/ppermute | solution.py:365
  37.4 34.1 %collective-permute-start.9 = (bf16[256,1024]{1,0:T(8,128)(2,1)}, bf16[256,1024]{1,0:T(8,128)(2,1)}, u32[]{:S(2)}, u32[]{:S(2)}) collective-permute-start(bf16[256,1024]{1,0:T(8,128)(2,1)} %get-tuple-element.44), channel_id=1, source_target_pairs={{0,3},{1,0},{2,1},{3,2},{4,7},{5,4},{6,5},{7,6},{8,11},{9,8},{10,9... | collective-permute-start | bytes 1572872 | tf_op jit(solution)/shard_map/ppermute | solution.py:365
  62.0 4.0 %copy-start.2 = (bf16[256,1024]{1,0:T(8,128)(2,1)S(1)}, bf16[256,1024]{1,0:T(8,128)(2,1)}, u32[]{:S(2)}) copy-start(bf16[256,1024]{1,0:T(8,128)(2,1)} %get-tuple-element.45.refs_0_) | copy-start | bytes 1572868
  62.0 4.0 %copy-start.3 = (bf16[256,1024]{1,0:T(8,128)(2,1)S(1)}, bf16[256,1024]{1,0:T(8,128)(2,1)}, u32[]{:S(2)}) copy-start(bf16[256,1024]{1,0:T(8,128)(2,1)} %get-tuple-element.46.refs_1_) | copy-start | bytes 1572868
  62.0 22.6 %copy-start = (bf16[256,1024]{1,0:T(8,128)(2,1)S(1)}, bf16[256,1024]{1,0:T(8,128)(2,1)}, u32[]{:S(2)}) copy-start(bf16[256,1024]{1,0:T(8,128)(2,1)} %get-tuple-element.39.refs_3_) | copy-start | bytes 1572868
  62.0 22.6 %copy-start.1 = (bf16[256,1024]{1,0:T(8,128)(2,1)S(1)}, bf16[256,1024]{1,0:T(8,128)(2,1)}, u32[]{:S(2)}) copy-start(bf16[256,1024]{1,0:T(8,128)(2,1)} %get-tuple-element.40.refs_4_) | copy-start | bytes 1572868
  66.0 25.4 %copy-start.6 = (f32[32,8]{0,1:T(8,128)S(1)}, f32[32,8]{0,1:T(8,128)}, u32[]{:S(2)}) copy-start(f32[32,8]{0,1:T(8,128)} %param.24) | copy-start | bytes 3076
  66.4 18.2 %collective-permute-start.10 = (bf16[256,1024]{1,0:T(8,128)(2,1)S(1)}, bf16[256,1024]{1,0:T(8,128)(2,1)S(1)}, u32[]{:S(2)}, u32[]{:S(2)}) collective-permute-start(bf16[256,1024]{1,0:T(8,128)(2,1)S(1)} %far_down.1), channel_id=1, source_target_pairs={{0,2},{1,3},{2,0},{3,1},{4,6},{5,7},{6,4},{7,5},{8,10},{9,11},{10,... | collective-permute-start | bytes 1572872 | tf_op jit(solution)/shard_map/ppermute | solution.py:365
  68.8 15.8 %collective-permute-start.4 = (bf16[256,256]{1,0:T(8,128)(2,1)S(1)}, bf16[256,256]{1,0:T(8,128)(2,1)S(1)}, u32[]{:S(2)}, u32[]{:S(2)}) collective-permute-start(bf16[256,256]{1,0:T(8,128)(2,1)S(1)} %experts_act.1.a_ref.refs_0_), channel_id=1, source_target_pairs={{0,1},{1,2},{2,3},{3,0},{4,5},{5,6},{6,7},{7,4},{8,9},{9,10},{10,1... | collective-permute-start | bytes 393224 | tf_op jit(solution)/shard_map/ppermute | solution.py:365
  69.0 15.6 %collective-permute-start.5 = (bf16[256,256]{1,0:T(8,128)(2,1)S(1)}, bf16[256,256]{1,0:T(8,128)(2,1)S(1)}, u32[]{:S(2)}, u32[]{:S(2)}) collective-permute-start(bf16[256,256]{1,0:T(8,128)(2,1)S(1)} %experts_act.1.a_ref.refs_0_), channel_id=1, source_target_pairs={{0,3},{1,0},{2,1},{3,2},{4,7},{5,4},{6,5},{7,6},{8,11},{9,8},{10,9... | collective-permute-start | bytes 393224 | tf_op jit(solution)/shard_map/ppermute | solution.py:365
  87.2 15.3 %all-to-all-start.1 = ((bf16[32,16,512]{2,1,0:T(8,128)(2,1)}), bf16[32,16,512]{2,1,0:T(8,128)(2,1)S(1)}, u32[]{:S(2)}, u32[]{:S(2)}) async-start(bf16[32,16,512]{2,1,0:T(8,128)(2,1)} %bitcast.14), calls=%async_computation.1 | async-start | bytes 1048576 | tf_op jit(solution)/shard_map/all_to_all | solution.py:422

commit v7 on v6

--- a/solution.py
+++ b/solution.py
@@ -289,46 +289,83 @@
     )(act, *downs)
 
 
-def experts_down(acts, downs, far, capacity, roles):
+def own_down(act, own, others, capacity):
+    slots, _ = act.shape
+    per_dev = len(own)
+    rows = slots // per_dev
+    columns = own[0].shape[1]
+    count = len(others)
+
+    def body(a_ref, *refs):
+        w_refs, sources = refs[:per_dev], refs[per_dev : per_dev + count]
+        out_ref, targets, sems = refs[per_dev + count], refs[per_dev + count + 1 : -1], refs[-1]
+        copies = [
+            pltpu.make_async_copy(source, target, sems.at[i])
+            for i, (source, target) in enumerate(zip(sources, targets))
+        ]
+        for copy in copies:
+            copy.start()
+        value = a_ref[...].astype(F32)
+        for e in range(per_dev):
+            out_ref[e * rows : (e + 1) * rows] = jnp.dot(
+                of_expert(value, e, per_dev, capacity).astype(BF),
+                w_refs[e][...],
+                preferred_element_type=F32,
+            )
+        for copy in copies:
+            copy.wait()
+
+    return pl.pallas_call(
+        body,
+        out_shape=[jax.ShapeDtypeStruct((slots, columns), F32)]
+        + [jax.ShapeDtypeStruct(w.shape, BF) for w in others],
+        in_specs=whole(1 + per_dev) + [pl.BlockSpec(memory_space=pltpu.HBM)] * count,
+        out_specs=whole(1 + count),
+        scratch_shapes=[pltpu.SemaphoreType.DMA((count,))],
+        compiler_params=pltpu.CompilerParams(vmem_limit_bytes=44 << 20),
+        name="own_down",
+    )(act, *own, *others)
+
+
+def experts_down(acts, downs, own, far, capacity, roles):
     count = len(acts)
-    slots, quarter = acts[0].shape
+    slots, _ = acts[0].shape
     per_dev = len(downs[0])
-    columns = downs[0][0].shape[1]
+    rows = slots // per_dev
+    columns = far.shape[1]
     piece = columns // roles
 
     def body(*refs):
-        a_refs, w_refs, (far_ref, out_ref) = refs[:count], refs[count:-2], refs[-2:]
+        a_refs, w_refs = refs[:count], refs[count:-3]
+        own_ref, far_ref, out_ref = refs[-3:]
         ones = [
             [of_expert(a[...].astype(F32), e, per_dev, capacity).astype(BF) for e in range(per_dev)]
             for a in a_refs
         ]
         for s in range(roles):
+            place = slice(s * piece, (s + 1) * piece)
             totals = []
             for e in range(per_dev):
-                total = None
+                total = own_ref[e * rows : (e + 1) * rows, place]
                 for i in range(count):
-                    product = jnp.dot(
+                    total = total + jnp.dot(
                         ones[i][e],
-                        w_refs[i * per_dev + e][:, s * piece : (s + 1) * piece],
+                        w_refs[i * per_dev + e][:, place],
                         preferred_element_type=F32,
                     )
-                    total = product if total is None else total + product
                 totals.append(total)
-            total = of_all(totals, capacity) + far_ref[:, s * piece : (s + 1) * piece].astype(F32)
+            total = of_all(totals, capacity) + far_ref[:, place].astype(F32)
             out_ref[s * slots : (s + 1) * slots] = total.astype(BF)
 
     flat = [w for each in downs for w in each]
     return pl.pallas_call(
         body,
         out_shape=jax.ShapeDtypeStruct((roles * slots, piece), BF),
-        in_specs=whole(count + len(flat) + 1),
+        in_specs=whole(count + len(flat) + 2),
         out_specs=pl.BlockSpec(memory_space=pltpu.VMEM),
         compiler_params=pltpu.CompilerParams(vmem_limit_bytes=24 << 20),
-        cost_estimate=pl.CostEstimate(
-            flops=2 * slots * count * quarter * columns, bytes_accessed=5 << 20, transcendentals=0
-        ),
         name="experts_down",
-    )(*acts, *flat, far)
+    )(*acts, *flat, own, far)
 
 
 def per_device(
@@ -416,8 +453,12 @@
     tokens = incoming.reshape(roles, shards * per_dev * capacity, half)
     act = experts_act(tokens, norm_gain.reshape(roles, 1, half), w_gate, w_up, capacity)
     far = shift(far_down(act, rest[len(near) * per_dev :], capacity), across)
-    acts = [shift(act, step) if step else act for step in near]
-    result = experts_down(acts, downs, far, capacity, roles)
+    acts = [shift(act, step) for step in near[1:]]
+    others = [w for each in downs[1:] for w in each]
+    act, *others = lax.optimization_barrier((act, *others))
+    own, *others = own_down(act, downs[0], others, capacity)
+    others = [others[i : i + per_dev] for i in range(0, len(others), per_dev)]
+    result = experts_down(acts, others, own, far, capacity, roles)
     result = result.reshape(roles * shards, per_dev * capacity, piece)
     returned = lax.all_to_all(result, ("role", "rows"), 0, 0, tiled=True)
     returned = returned.reshape(slots, piece)

time: 104 us -> 103 us (level)
  waiting for transfers between devices: 49.7 us -> 48.3 us
    ppermute x10, waiting for transfers between devices: 14.2 us -> 12.8 us  [shift(): lax.ppermute(x, 'heads', [(i, (i + step) % heads_count) for i in range(he...]
    pallas_call x0 -> x1, Pallas kernels: none -> 1.37 us  [own_down(): pl.pallas_call(body, out_shape=[jax.ShapeDtypeStruct((slots, columns), F3...]
    pallas_call x1, Pallas kernels: 2.59 us -> 1.25 us  [experts_down(): pl.pallas_call(body, out_shape=jax.ShapeDtypeStruct((roles * slots, piece...]
  transfers between devices with their start and end apart: 13 -> 13, of which waited for: 5 -> 5; matrix products, arithmetic and copies ran while one was open for 1% -> 1% of each run, Pallas kernels for 8% -> 9%
where the time goes in v7:
time: 103 us; the launch traced here: 102 us
  waiting for transfers between devices  48.3 us (47%)
  starting transfers between devices  29.3 us (28%)
  Pallas kernels  19.2 us (19%)
  matrix products  3.33 us (3%)
  other arithmetic  1.39 us (1%)
    all_to_all x1, waiting for transfers between devices, per_device(): incoming = lax.all_to_all(outgoing, ('role', 'rows'), 0, 0, tiled=True)  24.2 us
    ppermute x10, starting transfers between devices, shift(): lax.ppermute(x, 'heads', [(i, (i + step) % heads_count) for i in range(he...  14.3 us
    ppermute x10, waiting for transfers between devices, shift(): lax.ppermute(x, 'heads', [(i, (i + step) % heads_count) for i in range(he...  12.8 us
    all_to_all x1, waiting for transfers between devices, per_device(): returned = lax.all_to_all(result, ('role', 'rows'), 0, 0, tiled=True)  10.7 us
    all_to_all x1, starting transfers between devices, per_device(): incoming = lax.all_to_all(outgoing, ('role', 'rows'), 0, 0, tiled=True)  9.3 us
    pallas_call x1, Pallas kernels, attend(): pl.pallas_call(body, out_shape=[jax.ShapeDtypeStruct((rows, half), BF), j...  8.51 us
    all_to_all x1, starting transfers between devices, per_device(): returned = lax.all_to_all(result, ('role', 'rows'), 0, 0, tiled=True)  4.2 us
    pallas_call x1, Pallas kernels, experts_act(): pl.pallas_call(body, out_shape=jax.ShapeDtypeStruct((slots, quarter), BF)...  4 us
  transfers between devices with their start and end apart: 13, of which 5 were waited for; matrix products, arithmetic and copies ran while one was open for 1% of the time, Pallas kernels for 9%

profile of v7, /device:TPU:1, one launch (start us, length us, event | category | flops | bytes accessed | tf_op | source)
XLA Modules:
  0.0 102.3 jit_solution(5397670365354620243)
XLA Ops:
  0.0 8.5 %attend.1 = (bf16[32,2048]{1,0:T(8,128)(2,1)}, f32[32,2048]{1,0:T(8,128)}) custom-call(s32[1]{0:T(128)} %bitcast.role_ref, s32[32]{0:T(128)} %len_ref.1, bf16[32,1024]{1,0:T(8,128)(2,1)} %bitcast.40, bf16[32,512,128]{2,1,0:T(8,128)(2,1)} %bitcast.38, bf16[32,512,128]{2,1,0:T(8,128)(2,1)} %bitcast.39, bf16[32,128]{1,0:T(8,128)(2,1)} %bitcast.41, ...), custom_call_target="tpu_custom_call" | custom-call | bytes 1048576 | tf_op jit(solution)/shard_map/attend/pallas_call | solution.py:154
  8.5 1.5 %collective-permute-start = (bf16[32,2048]{1,0:T(8,128)(2,1)}, bf16[32,2048]{1,0:T(8,128)(2,1)S(1)}, u32[]{:S(2)}, u32[]{:S(2)}) collective-permute-start(bf16[32,2048]{1,0:T(8,128)(2,1)} %get-tuple-element.37), channel_id=1, source_target_pairs={{0,64},{64,0},{1,65},{65,1},{2,66},{66,2},{3,67},{67,3},{4,68},{68... | collective-permute-start | bytes 393224 | tf_op jit(solution)/shard_map/ppermute | solution.py:416
  10.7 0.6 collective-permute-done
  11.2 1.0 add_convert_fusion
  12.2 1.4 %collective-permute-start.1 = (bf16[32,2048]{1,0:T(8,128)(2,1)S(1)}, bf16[32,2048]{1,0:T(8,128)(2,1)S(1)}, u32[]{:S(2)}, u32[]{:S(2)}) collective-permute-start(bf16[32,2048]{1,0:T(8,128)(2,1)S(1)} %add_convert_fusion), channel_id=1, source_target_pairs={{0,1},{1,2},{2,3},{3,0},{4,5},{5,6},{6,7},{7,4},{8,9},{9,10},{10,1... | collective-permute-start | bytes 393224 | tf_op jit(solution)/shard_map/ppermute | solution.py:402
  13.6 2.5 %collective-permute-start.2 = (bf16[32,2048]{1,0:T(8,128)(2,1)S(1)}, bf16[32,2048]{1,0:T(8,128)(2,1)S(1)}, u32[]{:S(2)}, u32[]{:S(2)}) collective-permute-start(bf16[32,2048]{1,0:T(8,128)(2,1)S(1)} %add_convert_fusion), channel_id=1, source_target_pairs={{0,2},{1,3},{2,0},{3,1},{4,6},{5,7},{6,4},{7,5},{8,10},{9,11},{10,... | collective-permute-start | bytes 393224 | tf_op jit(solution)/shard_map/ppermute | solution.py:402
  16.0 1.2 %collective-permute-start.3 = (bf16[32,2048]{1,0:T(8,128)(2,1)S(1)}, bf16[32,2048]{1,0:T(8,128)(2,1)S(1)}, u32[]{:S(2)}, u32[]{:S(2)}) collective-permute-start(bf16[32,2048]{1,0:T(8,128)(2,1)S(1)} %add_convert_fusion), channel_id=1, source_target_pairs={{0,3},{1,0},{2,1},{3,2},{4,7},{5,4},{6,5},{7,6},{8,11},{9,8},{10,9... | collective-permute-start | bytes 393224 | tf_op jit(solution)/shard_map/ppermute | solution.py:402
  17.2 3.8 %cut_down.1 = (bf16[256,1024]{1,0:T(8,128)(2,1)}, bf16[256,1024]{1,0:T(8,128)(2,1)}, bf16[256,1024]{1,0:T(8,128)(2,1)}, bf16[256,1024]{1,0:T(8,128)(2,1)}, bf16[...) custom-call(s32[1]{0:T(128)} %bitcast.7.head_ref, ...), custom_call_target="tpu_custom_call" | custom-call | bytes 8388608 | tf_op jit(solution)/shard_map/cut_down/pallas_call | solution.py:61
  21.0 1.1 %collective-permute-done.2 = bf16[32,2048]{1,0:T(8,128)(2,1)S(1)} collective-permute-done((bf16[32,2048]{1,0:T(8,128)(2,1)S(1)}, bf16[32,2048]{1,0:T(8,128)(2,1)S(1)}, u32[]{:S(2)}, u32[]{:S(2)}) %collective-permute-start.2) | collective-permute-done | bytes 131104 | tf_op jit(solution)/shard_map/ppermute | solution.py:402
  22.2 2.1 %convolution_convert_fusion = bf16[512,2048]{1,0:T(8,128)(2,1)} fusion(f32[32,2048]{1,0:T(8,128)S(1)} %add_add_fusion, f32[2048]{0:T(1024)S(1)} %slice_select_fusion, s32[512]{0:T(512)S(1)} %eq.64, s32[32,64]{0,1:T(8,128)S(1)} %copy.22, pred[32,64]{0,1:T(8,128)(4,1)S(1)} %copy.21), kind=kOutput, calls=%fused_computation | convolution fusion | flops 68321280 | bytes 2379776 | tf_op jit(solution)/shard_map/dot_general | solution.py:448
  24.3 9.3 %all-to-all-start = ((bf16[32,16,2048]{2,1,0:T(8,128)(2,1)}), bf16[32,16,2048]{2,1,0:T(8,128)(2,1)S(1)}, u32[]{:S(2)}, u32[]{:S(2)}) async-start(bf16[32,16,2048]{2,1,0:T(8,128)(2,1)} %bitcast.35), calls=%async_computation | async-start | bytes 4194304 | tf_op jit(solution)/shard_map/all_to_all | solution.py:452
  33.6 1.1 %collective-permute-start.6 = (bf16[256,1024]{1,0:T(8,128)(2,1)}, bf16[256,1024]{1,0:T(8,128)(2,1)S(1)}, u32[]{:S(2)}, u32[]{:S(2)}) collective-permute-start(bf16[256,1024]{1,0:T(8,128)(2,1)} %get-tuple-element.49), channel_id=1, source_target_pairs={{0,1},{1,2},{2,3},{3,0},{4,5},{5,6},{6,7},{7,4},{8,9},{9,10},{10,1... | collective-permute-start | bytes 1572872 | tf_op jit(solution)/shard_map/ppermute | solution.py:402
  34.7 1.0 collective-permute-start.7
  35.7 1.7 %collective-permute-start.8 = (bf16[256,1024]{1,0:T(8,128)(2,1)}, bf16[256,1024]{1,0:T(8,128)(2,1)}, u32[]{:S(2)}, u32[]{:S(2)}) collective-permute-start(bf16[256,1024]{1,0:T(8,128)(2,1)} %get-tuple-element.51), channel_id=1, source_target_pairs={{0,3},{1,0},{2,1},{3,2},{4,7},{5,4},{6,5},{7,6},{8,11},{9,8},{10,9... | collective-permute-start | bytes 1572872 | tf_op jit(solution)/shard_map/ppermute | solution.py:402
  37.8 24.2 %all-to-all-done = bf16[32,16,2048]{2,1,0:T(8,128)(2,1)S(1)} async-done(((bf16[32,16,2048]{2,1,0:T(8,128)(2,1)}), bf16[32,16,2048]{2,1,0:T(8,128)(2,1)S(1)}, u32[]{:S(2)}, u32[]{:S(2)}) %all-to-all-start) | async-done | bytes 2097184 | tf_op jit(solution)/shard_map/all_to_all | solution.py:452
  62.0 4.0 %experts_act.1.a_ref = bf16[256,256]{1,0:T(8,128)(2,1)S(1)} custom-call(bf16[2,256,2048]{2,1,0:T(8,128)(2,1)S(1)} %bitcast.32, f32[2,1,2048]{2,1,0:T(1,128)S(1)} %bitcast.33, bf16[2,4096,256]{2,1,0:T(8,128)(2,1)} %g_any.1, bf16[2,4096,256]{2,1,0:T(8,128)(2,1)} %u_any.1), custom_call_target="tpu_custom_call" | custom-call | flops 1073741824 | bytes 10485760 | tf_op jit(solution)/shard_map/experts_act/pallas_call | solution.py:245
  66.4 2.5 %collective-permute-start.10 = (bf16[256,1024]{1,0:T(8,128)(2,1)S(1)}, bf16[256,1024]{1,0:T(8,128)(2,1)S(1)}, u32[]{:S(2)}, u32[]{:S(2)}) collective-permute-start(bf16[256,1024]{1,0:T(8,128)(2,1)S(1)} %far_down.1), channel_id=1, source_target_pairs={{0,2},{1,3},{2,0},{3,1},{4,6},{5,7},{6,4},{7,5},{8,10},{9,11},{10,... | collective-permute-start | bytes 1572872 | tf_op jit(solution)/shard_map/ppermute | solution.py:402
  69.0 2.5 %collective-permute-start.5 = (bf16[256,256]{1,0:T(8,128)(2,1)S(1)}, bf16[256,256]{1,0:T(8,128)(2,1)S(1)}, u32[]{:S(2)}, u32[]{:S(2)}) collective-permute-start(bf16[256,256]{1,0:T(8,128)(2,1)S(1)} %experts_act.1.a_ref), channel_id=1, source_target_pairs={{0,3},{1,0},{2,1},{3,2},{4,7},{5,4},{6,5},{7,6},{8,11},{9,8},{10,9... | collective-permute-start | bytes 393224 | tf_op jit(solution)/shard_map/ppermute | solution.py:402
  71.5 1.4 %own_down.1 = (f32[256,1024]{1,0:T(8,128)S(1)}, bf16[256,1024]{1,0:T(8,128)(2,1)S(1)}, bf16[256,1024]{1,0:T(8,128)(2,1)S(1)}, bf16[256,1024]{1,0:T(8,128)(2,1)S(1)}, bf16[256,1024]{1,0:T(8,128)(2,1)S(1)}) custom-call(bf16[256,256]{1,0:T(8,128)(2,1)S(1)} %experts_act.1.a_ref, bf16[256,1024]{1,0:T(8,128)(2,1)S(1)} %copy-done, bf16[256,1024]{1,0:T(8,128)(2,1)S(1)} %copy-done.1, ...), custom_call_target="tpu_custom_call" | custom-call | tf_op jit(solution)/shard_map/own_down/pallas_call | solution.py:318
  72.9 11.7 %collective-permute-done.4.refs_0_ = bf16[256,256]{1,0:T(8,128)(2,1)S(1)} collective-permute-done((bf16[256,256]{1,0:T(8,128)(2,1)S(1)}, bf16[256,256]{1,0:T(8,128)(2,1)S(1)}, u32[]{:S(2)}, u32[]{:S(2)}) %collective-permute-start.4) | collective-permute-done | bytes 131104 | tf_op jit(solution)/shard_map/ppermute | solution.py:402
  84.6 1.3 %experts_down.1 = bf16[512,512]{1,0:T(8,128)(2,1)} custom-call(bf16[256,256]{1,0:T(8,128)(2,1)S(1)} %collective-permute-done.4.refs_0_, bf16[256,256]{1,0:T(8,128)(2,1)S(1)} %collective-permute-done.5.refs_1_, bf16[256,1024]{1,0:T(8,128)(2,1)S(1)} %get-tuple-element.60.refs_2_, bf16[256,1024]{1,0:T(8,128)(2,1)S(1)} %get-tuple-element.61.refs_3_, ...), custom_call_target="tpu_custom_call" | custom-call | tf_op jit(solution)/shard_map/experts_down/pallas_call | solution.py:361
  85.9 4.2 %all-to-all-start.1 = ((bf16[32,16,512]{2,1,0:T(8,128)(2,1)}), bf16[32,16,512]{2,1,0:T(8,128)(2,1)S(1)}, u32[]{:S(2)}, u32[]{:S(2)}) async-start(bf16[32,16,512]{2,1,0:T(8,128)(2,1)} %bitcast.14), calls=%async_computation.1 | async-start | bytes 1048576 | tf_op jit(solution)/shard_map/all_to_all | solution.py:463
  90.4 10.7 %all-to-all-done.1 = bf16[32,16,512]{2,1,0:T(8,128)(2,1)S(1)} async-done(((bf16[32,16,512]{2,1,0:T(8,128)(2,1)}), bf16[32,16,512]{2,1,0:T(8,128)(2,1)S(1)}, u32[]{:S(2)}, u32[]{:S(2)}) %all-to-all-start.1) | async-done | bytes 524320 | tf_op jit(solution)/shard_map/all_to_all | solution.py:463
  101.4 0.9 fusion.1
  (42 shorter events, 2.2 us)
Async XLA Ops:
  0.0 10.0 %copy-start.7 = (s32[32,8]{0,1:T(8,128)S(1)}, s32[32,8]{0,1:T(8,128)}, u32[]{:S(2)}) copy-start(s32[32,8]{0,1:T(8,128)} %param.23) | copy-start | bytes 3076
  0.0 17.2 %copy-start.4 = (f32[4096]{0:T(1024)S(1)}, f32[4096]{0:T(1024)}, u32[]{:S(2)}) copy-start(f32[4096]{0:T(1024)} %param.22) | copy-start | bytes 49156
  8.5 13.6 %copy-start.5 = (bf16[32,4096]{1,0:T(8,128)(2,1)S(1)}, bf16[32,4096]{1,0:T(8,128)(2,1)}, u32[]{:S(2)}) copy-start(bf16[32,4096]{1,0:T(8,128)(2,1)} %param.21) | copy-start | bytes 786436
  8.5 2.7 %collective-permute-start = (bf16[32,2048]{1,0:T(8,128)(2,1)}, bf16[32,2048]{1,0:T(8,128)(2,1)S(1)}, u32[]{:S(2)}, u32[]{:S(2)}) collective-permute-start(bf16[32,2048]{1,0:T(8,128)(2,1)} %get-tuple-element.37), channel_id=1, source_target_pairs={{0,64},{64,0},{1,65},{65,1},{2,66},{66,2},{3,67},{67,3},{4,68},{68... | collective-permute-start | bytes 393224 | tf_op jit(solution)/shard_map/ppermute | solution.py:416
  12.2 8.8 %collective-permute-start.1 = (bf16[32,2048]{1,0:T(8,128)(2,1)S(1)}, bf16[32,2048]{1,0:T(8,128)(2,1)S(1)}, u32[]{:S(2)}, u32[]{:S(2)}) collective-permute-start(bf16[32,2048]{1,0:T(8,128)(2,1)S(1)} %add_convert_fusion), channel_id=1, source_target_pairs={{0,1},{1,2},{2,3},{3,0},{4,5},{5,6},{6,7},{7,4},{8,9},{9,10},{10,1... | collective-permute-start | bytes 393224 | tf_op jit(solution)/shard_map/ppermute | solution.py:402
  13.6 8.5 %collective-permute-start.2 = (bf16[32,2048]{1,0:T(8,128)(2,1)S(1)}, bf16[32,2048]{1,0:T(8,128)(2,1)S(1)}, u32[]{:S(2)}, u32[]{:S(2)}) collective-permute-start(bf16[32,2048]{1,0:T(8,128)(2,1)S(1)} %add_convert_fusion), channel_id=1, source_target_pairs={{0,2},{1,3},{2,0},{3,1},{4,6},{5,7},{6,4},{7,5},{8,10},{9,11},{10,... | collective-permute-start | bytes 393224 | tf_op jit(solution)/shard_map/ppermute | solution.py:402
  16.0 6.1 %collective-permute-start.3 = (bf16[32,2048]{1,0:T(8,128)(2,1)S(1)}, bf16[32,2048]{1,0:T(8,128)(2,1)S(1)}, u32[]{:S(2)}, u32[]{:S(2)}) collective-permute-start(bf16[32,2048]{1,0:T(8,128)(2,1)S(1)} %add_convert_fusion), channel_id=1, source_target_pairs={{0,3},{1,0},{2,1},{3,2},{4,7},{5,4},{6,5},{7,6},{8,11},{9,8},{10,9... | collective-permute-start | bytes 393224 | tf_op jit(solution)/shard_map/ppermute | solution.py:402
  24.3 37.7 %all-to-all-start = ((bf16[32,16,2048]{2,1,0:T(8,128)(2,1)}), bf16[32,16,2048]{2,1,0:T(8,128)(2,1)S(1)}, u32[]{:S(2)}, u32[]{:S(2)}) async-start(bf16[32,16,2048]{2,1,0:T(8,128)(2,1)} %bitcast.35), calls=%async_computation | async-start | bytes 4194304 | tf_op jit(solution)/shard_map/all_to_all | solution.py:452
  33.6 35.2 %collective-permute-start.6 = (bf16[256,1024]{1,0:T(8,128)(2,1)}, bf16[256,1024]{1,0:T(8,128)(2,1)S(1)}, u32[]{:S(2)}, u32[]{:S(2)}) collective-permute-start(bf16[256,1024]{1,0:T(8,128)(2,1)} %get-tuple-element.49), channel_id=1, source_target_pairs={{0,1},{1,2},{2,3},{3,0},{4,5},{5,6},{6,7},{7,4},{8,9},{9,10},{10,1... | collective-permute-start | bytes 1572872 | tf_op jit(solution)/shard_map/ppermute | solution.py:402
  34.7 34.3 %collective-permute-start.7 = (bf16[256,1024]{1,0:T(8,128)(2,1)}, bf16[256,1024]{1,0:T(8,128)(2,1)S(1)}, u32[]{:S(2)}, u32[]{:S(2)}) collective-permute-start(bf16[256,1024]{1,0:T(8,128)(2,1)} %get-tuple-element.50), channel_id=1, source_target_pairs={{0,1},{1,2},{2,3},{3,0},{4,5},{5,6},{6,7},{7,4},{8,9},{9,10},{10,1... | collective-permute-start | bytes 1572872 | tf_op jit(solution)/shard_map/ppermute | solution.py:402
  35.7 35.8 %collective-permute-start.8 = (bf16[256,1024]{1,0:T(8,128)(2,1)}, bf16[256,1024]{1,0:T(8,128)(2,1)}, u32[]{:S(2)}, u32[]{:S(2)}) collective-permute-start(bf16[256,1024]{1,0:T(8,128)(2,1)} %get-tuple-element.51), channel_id=1, source_target_pairs={{0,3},{1,0},{2,1},{3,2},{4,7},{5,4},{6,5},{7,6},{8,11},{9,8},{10,9... | collective-permute-start | bytes 1572872 | tf_op jit(solution)/shard_map/ppermute | solution.py:402
  37.4 34.1 %collective-permute-start.9 = (bf16[256,1024]{1,0:T(8,128)(2,1)}, bf16[256,1024]{1,0:T(8,128)(2,1)}, u32[]{:S(2)}, u32[]{:S(2)}) collective-permute-start(bf16[256,1024]{1,0:T(8,128)(2,1)} %get-tuple-element.52), channel_id=1, source_target_pairs={{0,3},{1,0},{2,1},{3,2},{4,7},{5,4},{6,5},{7,6},{8,11},{9,8},{10,9... | collective-permute-start | bytes 1572872 | tf_op jit(solution)/shard_map/ppermute | solution.py:402
  62.0 4.0 %copy-start.2 = (bf16[256,1024]{1,0:T(8,128)(2,1)S(1)}, bf16[256,1024]{1,0:T(8,128)(2,1)}, u32[]{:S(2)}) copy-start(bf16[256,1024]{1,0:T(8,128)(2,1)} %get-tuple-element.65.refs_0_) | copy-start | bytes 1572868
  62.0 4.0 %copy-start.3 = (bf16[256,1024]{1,0:T(8,128)(2,1)S(1)}, bf16[256,1024]{1,0:T(8,128)(2,1)}, u32[]{:S(2)}) copy-start(bf16[256,1024]{1,0:T(8,128)(2,1)} %get-tuple-element.66.refs_1_) | copy-start | bytes 1572868
  62.0 9.5 %copy-start = (bf16[256,1024]{1,0:T(8,128)(2,1)S(1)}, bf16[256,1024]{1,0:T(8,128)(2,1)}, u32[]{:S(2)}) copy-start(bf16[256,1024]{1,0:T(8,128)(2,1)} %get-tuple-element.54.refs_0_) | copy-start | bytes 1572868
  62.0 9.5 %copy-start.1 = (bf16[256,1024]{1,0:T(8,128)(2,1)S(1)}, bf16[256,1024]{1,0:T(8,128)(2,1)}, u32[]{:S(2)}) copy-start(bf16[256,1024]{1,0:T(8,128)(2,1)} %get-tuple-element.55.refs_1_) | copy-start | bytes 1572868
  66.4 23.7 %copy-start.6 = (f32[32,8]{0,1:T(8,128)S(1)}, f32[32,8]{0,1:T(8,128)}, u32[]{:S(2)}) copy-start(f32[32,8]{0,1:T(8,128)} %param.24) | copy-start | bytes 3076
  66.4 18.2 %collective-permute-start.10 = (bf16[256,1024]{1,0:T(8,128)(2,1)S(1)}, bf16[256,1024]{1,0:T(8,128)(2,1)S(1)}, u32[]{:S(2)}, u32[]{:S(2)}) collective-permute-start(bf16[256,1024]{1,0:T(8,128)(2,1)S(1)} %far_down.1), channel_id=1, source_target_pairs={{0,2},{1,3},{2,0},{3,1},{4,6},{5,7},{6,4},{7,5},{8,10},{9,11},{10,... | collective-permute-start | bytes 1572872 | tf_op jit(solution)/shard_map/ppermute | solution.py:402
  68.8 15.8 %collective-permute-start.4 = (bf16[256,256]{1,0:T(8,128)(2,1)S(1)}, bf16[256,256]{1,0:T(8,128)(2,1)S(1)}, u32[]{:S(2)}, u32[]{:S(2)}) collective-permute-start(bf16[256,256]{1,0:T(8,128)(2,1)S(1)} %experts_act.1.a_ref), channel_id=1, source_target_pairs={{0,1},{1,2},{2,3},{3,0},{4,5},{5,6},{6,7},{7,4},{8,9},{9,10},{10,1... | collective-permute-start | bytes 393224 | tf_op jit(solution)/shard_map/ppermute | solution.py:402
  69.0 15.6 %collective-permute-start.5 = (bf16[256,256]{1,0:T(8,128)(2,1)S(1)}, bf16[256,256]{1,0:T(8,128)(2,1)S(1)}, u32[]{:S(2)}, u32[]{:S(2)}) collective-permute-start(bf16[256,256]{1,0:T(8,128)(2,1)S(1)} %experts_act.1.a_ref), channel_id=1, source_target_pairs={{0,3},{1,0},{2,1},{3,2},{4,7},{5,4},{6,5},{7,6},{8,11},{9,8},{10,9... | collective-permute-start | bytes 393224 | tf_op jit(solution)/shard_map/ppermute | solution.py:402
  85.9 15.3 %all-to-all-start.1 = ((bf16[32,16,512]{2,1,0:T(8,128)(2,1)}), bf16[32,16,512]{2,1,0:T(8,128)(2,1)S(1)}, u32[]{:S(2)}, u32[]{:S(2)}) async-start(bf16[32,16,512]{2,1,0:T(8,128)(2,1)} %bitcast.14), calls=%async_computation.1 | async-start | bytes 1048576 | tf_op jit(solution)/shard_map/all_to_all | solution.py:463

commit v8 on v7

--- a/solution.py
+++ b/solution.py
@@ -200,118 +200,98 @@
     return jnp.concatenate(parts, axis=1).reshape(len(values) * rows, columns)
 
 
-def experts_act(tokens, gain, w_gate, w_up, capacity):
+def expert_act(tokens, gain, w_gate, w_up, across, e, before, capacity):
     roles, slots, half = tokens.shape
     per_dev, width, quarter = w_gate.shape
+    columns = across.shape[1]
     chunk = 512
-
-    def body(x_ref, gain_ref, g_any, u_any, act_ref, g_ref, u_ref, sums, sems):
+    rows = slots // per_dev
+    done = e * rows
+
+    def body(x_ref, gain_ref, g_hbm, u_hbm, w_ref, *rest):
+        before_ref = rest[0] if e else None
+        act_ref, far_ref, g_ref, u_ref, sums, sems = rest[1 if e else 0 :]
         copies = []
         for k in range(width // chunk):
-            rows = pl.ds(k * chunk, chunk)
+            place = pl.ds(k * chunk, chunk)
             copies.append(
                 [
-                    pltpu.make_async_copy(
-                        source.at[:, rows], target.at[:, rows], sems.at[2 * k + i]
-                    )
-                    for i, (source, target) in enumerate(((g_any, g_ref), (u_any, u_ref)))
+                    pltpu.make_async_copy(hbm.at[e, place], ref.at[place], sems.at[2 * k + i])
+                    for i, (hbm, ref) in enumerate(((g_hbm, g_ref), (u_hbm, u_ref)))
                 ]
             )
         for pair in copies:
             for copy in pair:
                 copy.start()
-        square = jnp.zeros((slots, 1), F32)
+        square = jnp.zeros((rows, 1), F32)
         for k in range(width // chunk):
             s, place = divmod(k * chunk, half)
             x = x_ref[s, :, place : place + chunk].astype(F32)
+            x = of_expert(x, e, per_dev, capacity)
             plain = x * (1.0 / gain_ref[s, :, place : place + chunk])
             square = square + jnp.sum(plain * plain, axis=1, keepdims=True)
+            x = x.astype(BF)
             for copy in copies[k]:
                 copy.wait()
-            for e in range(per_dev):
-                one = of_expert(x, e, per_dev, capacity).astype(BF)
-                for i, w_ref in enumerate((g_ref, u_ref)):
-                    product = jnp.dot(
-                        one, w_ref[e, k * chunk : (k + 1) * chunk], preferred_element_type=F32
-                    )
-                    if k:
-                        product = product + sums[2 * e + i]
-                    sums[2 * e + i] = product
+            for i, ref in enumerate((g_ref, u_ref)):
+                product = jnp.dot(
+                    x, ref[k * chunk : (k + 1) * chunk], preferred_element_type=F32
+                )
+                sums[i] = product + sums[i] if k else product
         inverse = lax.rsqrt(square / width + EPS)
-        gate = of_all([sums[2 * e] for e in range(per_dev)], capacity) * inverse
-        upper = of_all([sums[2 * e + 1] for e in range(per_dev)], capacity) * inverse
-        act_ref[...] = (gate / (1.0 + jnp.exp(-gate)) * upper).astype(BF)
+        gate, upper = sums[0] * inverse, sums[1] * inverse
+        act = (gate / (1.0 + jnp.exp(-gate)) * upper).astype(BF)
+        if e:
+            act_ref[:done] = before_ref[...]
+        act_ref[done:] = act
+        far_ref[...] = jnp.dot(act, w_ref[...], preferred_element_type=F32).astype(BF)
 
     return pl.pallas_call(
         body,
-        out_shape=jax.ShapeDtypeStruct((slots, quarter), BF),
-        in_specs=whole(2) + [pl.BlockSpec(memory_space=pltpu.HBM)] * 2,
-        out_specs=pl.BlockSpec(memory_space=pltpu.VMEM),
+        out_shape=[
+            jax.ShapeDtypeStruct((done + rows, quarter), BF),
+            jax.ShapeDtypeStruct((rows, columns), BF),
+        ],
+        in_specs=whole(2)
+        + [pl.BlockSpec(memory_space=pltpu.HBM)] * 2
+        + whole(2 if e else 1),
+        out_specs=whole(2),
         scratch_shapes=[
-            pltpu.VMEM(w_gate.shape, BF),
-            pltpu.VMEM(w_up.shape, BF),
-            pltpu.VMEM((2 * per_dev, slots // per_dev, quarter), F32),
+            pltpu.VMEM((width, quarter), BF),
+            pltpu.VMEM((width, quarter), BF),
+            pltpu.VMEM((2, rows, quarter), F32),
             pltpu.SemaphoreType.DMA((2 * (width // chunk),)),
         ],
         compiler_params=pltpu.CompilerParams(vmem_limit_bytes=49 << 20),
         cost_estimate=pl.CostEstimate(
-            flops=4 * slots * width * quarter, bytes_accessed=10 << 20, transcendentals=0
+            flops=4 * rows * width * quarter, bytes_accessed=6 << 20, transcendentals=0
         ),
-        name="experts_act",
-    )(tokens, gain, w_gate, w_up)
-
-
-def far_down(act, downs, capacity):
-    slots, _ = act.shape
-    per_dev = len(downs)
-    columns = downs[0].shape[1]
-
-    def body(a_ref, *refs):
-        w_refs, out_ref = refs[:-1], refs[-1]
-        value = a_ref[...].astype(F32)
-        products = [
-            jnp.dot(
-                of_expert(value, e, per_dev, capacity).astype(BF),
-                w_ref[...],
-                preferred_element_type=F32,
-            )
-            for e, w_ref in enumerate(w_refs)
-        ]
-        out_ref[...] = of_all(products, capacity).astype(BF)
-
-    return pl.pallas_call(
-        body,
-        out_shape=jax.ShapeDtypeStruct((slots, columns), BF),
-        in_specs=whole(1 + per_dev),
-        out_specs=pl.BlockSpec(memory_space=pltpu.VMEM),
-        compiler_params=pltpu.CompilerParams(vmem_limit_bytes=24 << 20),
-        name="far_down",
-    )(act, *downs)
-
-
-def own_down(act, own, others, capacity):
+        name=f"expert_act_{e}",
+    )(tokens, gain, w_gate, w_up, across, *([before] if e else []))
+
+
+def own_down(act, own, others, fars):
     slots, _ = act.shape
     per_dev = len(own)
     rows = slots // per_dev
     columns = own[0].shape[1]
-    count = len(others)
+    count, early = len(others), len(fars)
 
     def body(a_ref, *refs):
         w_refs, sources = refs[:per_dev], refs[per_dev : per_dev + count]
-        out_ref, targets, sems = refs[per_dev + count], refs[per_dev + count + 1 : -1], refs[-1]
+        far_refs, (out_ref, *targets, sems) = refs[per_dev + count :][:early], refs[per_dev + count + early :]
         copies = [
             pltpu.make_async_copy(source, target, sems.at[i])
             for i, (source, target) in enumerate(zip(sources, targets))
         ]
         for copy in copies:
             copy.start()
-        value = a_ref[...].astype(F32)
         for e in range(per_dev):
-            out_ref[e * rows : (e + 1) * rows] = jnp.dot(
-                of_expert(value, e, per_dev, capacity).astype(BF),
-                w_refs[e][...],
-                preferred_element_type=F32,
-            )
+            place = slice(e * rows, (e + 1) * rows)
+            value = jnp.dot(a_ref[place], w_refs[e][...], preferred_element_type=F32)
+            if e < early:
+                value = value + far_refs[e][...].astype(F32)
+            out_ref[place] = value
         for copy in copies:
             copy.wait()
 
@@ -319,12 +299,15 @@
         body,
         out_shape=[jax.ShapeDtypeStruct((slots, columns), F32)]
         + [jax.ShapeDtypeStruct(w.shape, BF) for w in others],
-        in_specs=whole(1 + per_dev) + [pl.BlockSpec(memory_space=pltpu.HBM)] * count,
+        in_specs=whole(1 + per_dev)
+        + [pl.BlockSpec(memory_space=pltpu.HBM)] * count
+        + whole(early),
         out_specs=whole(1 + count),
         scratch_shapes=[pltpu.SemaphoreType.DMA((count,))],
         compiler_params=pltpu.CompilerParams(vmem_limit_bytes=44 << 20),
+        cost_estimate=pl.CostEstimate(flops=0, bytes_accessed=8 << 20, transcendentals=0),
         name="own_down",
-    )(act, *own, *others)
+    )(act, *own, *others, *fars)
 
 
 def experts_down(acts, downs, own, far, capacity, roles):
@@ -338,10 +321,6 @@
     def body(*refs):
         a_refs, w_refs = refs[:count], refs[count:-3]
         own_ref, far_ref, out_ref = refs[-3:]
-        ones = [
-            [of_expert(a[...].astype(F32), e, per_dev, capacity).astype(BF) for e in range(per_dev)]
-            for a in a_refs
-        ]
         for s in range(roles):
             place = slice(s * piece, (s + 1) * piece)
             totals = []
@@ -349,13 +328,14 @@
                 total = own_ref[e * rows : (e + 1) * rows, place]
                 for i in range(count):
                     total = total + jnp.dot(
-                        ones[i][e],
+                        a_refs[i][e * rows : (e + 1) * rows],
                         w_refs[i * per_dev + e][:, place],
                         preferred_element_type=F32,
                     )
+                if e == per_dev - 1:
+                    total = total + far_ref[:, place].astype(F32)
                 totals.append(total)
-            total = of_all(totals, capacity) + far_ref[:, place].astype(F32)
-            out_ref[s * slots : (s + 1) * slots] = total.astype(BF)
+            out_ref[s * slots : (s + 1) * slots] = of_all(totals, capacity).astype(BF)
 
     flat = [w for each in downs for w in each]
     return pl.pallas_call(
@@ -451,14 +431,18 @@
     outgoing = outgoing.reshape(roles * shards, per_dev * capacity, half)
     incoming = lax.all_to_all(outgoing, ("role", "rows"), 0, 0, tiled=True)
     tokens = incoming.reshape(roles, shards * per_dev * capacity, half)
-    act = experts_act(tokens, norm_gain.reshape(roles, 1, half), w_gate, w_up, capacity)
-    far = shift(far_down(act, rest[len(near) * per_dev :], capacity), across)
+    flat_gain = norm_gain.reshape(roles, 1, half)
+    act, fars = None, []
+    for e in range(per_dev):
+        opposite = rest[len(near) * per_dev + e]
+        act, far = expert_act(tokens, flat_gain, w_gate, w_up, opposite, e, act, capacity)
+        fars.append(shift(far, across))
     acts = [shift(act, step) for step in near[1:]]
     others = [w for each in downs[1:] for w in each]
     act, *others = lax.optimization_barrier((act, *others))
-    own, *others = own_down(act, downs[0], others, capacity)
+    own, *others = own_down(act, downs[0], others, fars[:-1])
     others = [others[i : i + per_dev] for i in range(0, len(others), per_dev)]
-    result = experts_down(acts, others, own, far, capacity, roles)
+    result = experts_down(acts, others, own, fars[-1], capacity, roles)
     result = result.reshape(roles * shards, per_dev * capacity, piece)
     returned = lax.all_to_all(result, ("role", "rows"), 0, 0, tiled=True)
     returned = returned.reshape(slots, piece)

time: 103 us -> 102 us (level)
  waiting for transfers between devices: 48.3 us -> 44.8 us
  Pallas kernels: 19.2 us -> 20.5 us
  local copies, waits for them, and re-layouts: 0.55 us -> 1.58 us
    ppermute x10 -> x11, waiting for transfers between devices: 12.8 us -> 9.34 us  [shift(): lax.ppermute(x, 'heads', [(i, (i + step) % heads_count) for i in range(he...]
    pallas_call x2, Pallas kernels: 4.31 us -> 5.56 us  [expert_act(): pl.pallas_call(body, out_shape=[jax.ShapeDtypeStruct((done + rows, quarte...]
    unnamed x17, local copies, waits for them, and re-layouts: 0.11 us -> 1.15 us
    ppermute x10 -> x11, starting transfers between devices: 14.3 us -> 15 us  [shift(): lax.ppermute(x, 'heads', [(i, (i + step) % heads_count) for i in range(he...]
  transfers between devices with their start and end apart: 13 -> 14, of which waited for: 5 -> 5; matrix products, arithmetic and copies ran while one was open for 1% -> 1% of each run, Pallas kernels for 9% -> 11%
where the time goes in v8:
time: 102 us
  waiting for transfers between devices  44.8 us (44%)
  starting transfers between devices  30 us (29%)
  Pallas kernels  20.5 us (20%)
  matrix products  3.32 us (3%)
  local copies, waits for them, and re-layouts  1.58 us (2%)
  other arithmetic  1.39 us (1%)
    all_to_all x1, waiting for transfers between devices, per_device(): incoming = lax.all_to_all(outgoing, ('role', 'rows'), 0, 0, tiled=True)  24.2 us
    ppermute x11, starting transfers between devices, shift(): lax.ppermute(x, 'heads', [(i, (i + step) % heads_count) for i in range(he...  15 us
    all_to_all x1, waiting for transfers between devices, per_device(): returned = lax.all_to_all(result, ('role', 'rows'), 0, 0, tiled=True)  10.7 us
    ppermute x11, waiting for transfers between devices, shift(): lax.ppermute(x, 'heads', [(i, (i + step) % heads_count) for i in range(he...  9.34 us
    all_to_all x1, starting transfers between devices, per_device(): incoming = lax.all_to_all(outgoing, ('role', 'rows'), 0, 0, tiled=True)  9.29 us
    pallas_call x1, Pallas kernels, attend(): pl.pallas_call(body, out_shape=[jax.ShapeDtypeStruct((rows, half), BF), j...  8.52 us
    pallas_call x2, Pallas kernels, expert_act(): pl.pallas_call(body, out_shape=[jax.ShapeDtypeStruct((done + rows, quarte...  5.56 us
    all_to_all x1, starting transfers between devices, per_device(): returned = lax.all_to_all(result, ('role', 'rows'), 0, 0, tiled=True)  4.2 us
  transfers between devices with their start and end apart: 14, of which 5 were waited for; matrix products, arithmetic and copies ran while one was open for 1% of the time, Pallas kernels for 11%

profile of v8, /device:TPU:1, one launch (start us, length us, event | category | flops | bytes accessed | tf_op | source)
XLA Modules:
  0.0 101.7 jit_solution(17596772801442358920)
XLA Ops:
  0.0 8.5 %attend.1 = (bf16[32,2048]{1,0:T(8,128)(2,1)}, f32[32,2048]{1,0:T(8,128)}) custom-call(s32[1]{0:T(128)} %bitcast.role_ref, s32[32]{0:T(128)} %len_ref.1, bf16[32,1024]{1,0:T(8,128)(2,1)} %bitcast.42, bf16[32,512,128]{2,1,0:T(8,128)(2,1)} %bitcast.40, bf16[32,512,128]{2,1,0:T(8,128)(2,1)} %bitcast.41, bf16[32,128]{1,0:T(8,128)(2,1)} %bitcast.43, ...), custom_call_target="tpu_custom_call" | custom-call | bytes 1048576 | tf_op jit(solution)/shard_map/attend/pallas_call | solution.py:154
  8.5 1.5 %collective-permute-start = (bf16[32,2048]{1,0:T(8,128)(2,1)}, bf16[32,2048]{1,0:T(8,128)(2,1)S(1)}, u32[]{:S(2)}, u32[]{:S(2)}) collective-permute-start(bf16[32,2048]{1,0:T(8,128)(2,1)} %get-tuple-element.41), channel_id=1, source_target_pairs={{0,64},{64,0},{1,65},{65,1},{2,66},{66,2},{3,67},{67,3},{4,68},{68... | collective-permute-start | bytes 393224 | tf_op jit(solution)/shard_map/ppermute | solution.py:396
  12.2 1.4 %collective-permute-start.1 = (bf16[32,2048]{1,0:T(8,128)(2,1)S(1)}, bf16[32,2048]{1,0:T(8,128)(2,1)S(1)}, u32[]{:S(2)}, u32[]{:S(2)}) collective-permute-start(bf16[32,2048]{1,0:T(8,128)(2,1)S(1)} %add_convert_fusion), channel_id=1, source_target_pairs={{0,1},{1,2},{2,3},{3,0},{4,5},{5,6},{6,7},{7,4},{8,9},{9,10},{10,1... | collective-permute-start | bytes 393224 | tf_op jit(solution)/shard_map/ppermute | solution.py:382
  13.6 2.5 %collective-permute-start.2 = (bf16[32,2048]{1,0:T(8,128)(2,1)S(1)}, bf16[32,2048]{1,0:T(8,128)(2,1)S(1)}, u32[]{:S(2)}, u32[]{:S(2)}) collective-permute-start(bf16[32,2048]{1,0:T(8,128)(2,1)S(1)} %add_convert_fusion), channel_id=1, source_target_pairs={{0,2},{1,3},{2,0},{3,1},{4,6},{5,7},{6,4},{7,5},{8,10},{9,11},{10,... | collective-permute-start | bytes 393224 | tf_op jit(solution)/shard_map/ppermute | solution.py:382
  16.0 1.2 %collective-permute-start.3 = (bf16[32,2048]{1,0:T(8,128)(2,1)S(1)}, bf16[32,2048]{1,0:T(8,128)(2,1)S(1)}, u32[]{:S(2)}, u32[]{:S(2)}) collective-permute-start(bf16[32,2048]{1,0:T(8,128)(2,1)S(1)} %add_convert_fusion), channel_id=1, source_target_pairs={{0,3},{1,0},{2,1},{3,2},{4,7},{5,4},{6,5},{7,6},{8,11},{9,8},{10,9... | collective-permute-start | bytes 393224 | tf_op jit(solution)/shard_map/ppermute | solution.py:382
  17.2 3.8 %cut_down.1 = (bf16[256,1024]{1,0:T(8,128)(2,1)}, bf16[256,1024]{1,0:T(8,128)(2,1)}, bf16[256,1024]{1,0:T(8,128)(2,1)}, bf16[256,1024]{1,0:T(8,128)(2,1)}, bf16[...) custom-call(s32[1]{0:T(128)} %bitcast.7.head_ref, ...), custom_call_target="tpu_custom_call" | custom-call | bytes 8388608 | tf_op jit(solution)/shard_map/cut_down/pallas_call | solution.py:61
  21.0 1.1 %collective-permute-done.2 = bf16[32,2048]{1,0:T(8,128)(2,1)S(1)} collective-permute-done((bf16[32,2048]{1,0:T(8,128)(2,1)S(1)}, bf16[32,2048]{1,0:T(8,128)(2,1)S(1)}, u32[]{:S(2)}, u32[]{:S(2)}) %collective-permute-start.2) | collective-permute-done | bytes 131104 | tf_op jit(solution)/shard_map/ppermute | solution.py:382
  22.2 2.1 %convolution_convert_fusion = bf16[512,2048]{1,0:T(8,128)(2,1)} fusion(f32[32,2048]{1,0:T(8,128)S(1)} %add_add_fusion, f32[2048]{0:T(1024)S(1)} %slice_select_fusion, s32[512]{0:T(512)S(1)} %eq.64, s32[32,64]{0,1:T(8,128)S(1)} %copy.22, pred[32,64]{0,1:T(8,128)(4,1)S(1)} %copy.21), kind=kOutput, calls=%fused_computation | convolution fusion | flops 68321280 | bytes 2379776 | tf_op jit(solution)/shard_map/dot_general | solution.py:428
  24.3 9.3 %all-to-all-start = ((bf16[32,16,2048]{2,1,0:T(8,128)(2,1)}), bf16[32,16,2048]{2,1,0:T(8,128)(2,1)S(1)}, u32[]{:S(2)}, u32[]{:S(2)}) async-start(bf16[32,16,2048]{2,1,0:T(8,128)(2,1)} %bitcast.37), calls=%async_computation | async-start | bytes 4194304 | tf_op jit(solution)/shard_map/all_to_all | solution.py:432
  33.6 1.1 %collective-permute-start.6 = (bf16[256,1024]{1,0:T(8,128)(2,1)}, bf16[256,1024]{1,0:T(8,128)(2,1)S(1)}, u32[]{:S(2)}, u32[]{:S(2)}) collective-permute-start(bf16[256,1024]{1,0:T(8,128)(2,1)} %get-tuple-element.57), channel_id=1, source_target_pairs={{0,1},{1,2},{2,3},{3,0},{4,5},{5,6},{6,7},{7,4},{8,9},{9,10},{10,1... | collective-permute-start | bytes 1572872 | tf_op jit(solution)/shard_map/ppermute | solution.py:382
  34.7 1.0 collective-permute-start.7
  35.7 1.7 %collective-permute-start.8 = (bf16[256,1024]{1,0:T(8,128)(2,1)}, bf16[256,1024]{1,0:T(8,128)(2,1)}, u32[]{:S(2)}, u32[]{:S(2)}) collective-permute-start(bf16[256,1024]{1,0:T(8,128)(2,1)} %get-tuple-element.59), channel_id=1, source_target_pairs={{0,3},{1,0},{2,1},{3,2},{4,7},{5,4},{6,5},{7,6},{8,11},{9,8},{10,9... | collective-permute-start | bytes 1572872 | tf_op jit(solution)/shard_map/ppermute | solution.py:382
  37.8 24.2 %all-to-all-done = bf16[32,16,2048]{2,1,0:T(8,128)(2,1)S(1)} async-done(((bf16[32,16,2048]{2,1,0:T(8,128)(2,1)}), bf16[32,16,2048]{2,1,0:T(8,128)(2,1)S(1)}, u32[]{:S(2)}, u32[]{:S(2)}) %all-to-all-start) | async-done | bytes 2097184 | tf_op jit(solution)/shard_map/all_to_all | solution.py:432
  62.0 1.0 %copy-done.3 = bf16[256,1024]{1,0:T(8,128)(2,1)S(1)} copy-done((bf16[256,1024]{1,0:T(8,128)(2,1)S(1)}, bf16[256,1024]{1,0:T(8,128)(2,1)}, u32[]{:S(2)}) %copy-start.3) | copy-done | bytes 524312
  63.1 2.8 %expert_act_0.1 = (bf16[128,256]{1,0:T(8,128)(2,1)S(1)}, bf16[128,1024]{1,0:T(8,128)(2,1)S(1)}) custom-call(bf16[2,256,2048]{2,1,0:T(8,128)(2,1)S(1)} %bitcast.32, f32[2,1,2048]{2,1,0:T(1,128)S(1)} %bitcast.34, bf16[2,4096,256]{2,1,0:T(8,128)(2,1)} %g_hbm.3, bf16[2,4096,256]{2,1,0:T(8,128)(2,1)} %u_hbm.3, bf16[256,1024]{1,0:T(8,128)(2,1)S(1)} %copy-done.3), custom_call_target="tpu_custom_call" | custom-call | flops 536870912 | bytes 6291456 | tf_op jit(solution)/shard_map/expert_act_0/pallas_call | solution.py:249
  65.8 2.5 %collective-permute-start.10 = (bf16[128,1024]{1,0:T(8,128)(2,1)S(1)}, bf16[128,1024]{1,0:T(8,128)(2,1)S(1)}, u32[]{:S(2)}, u32[]{:S(2)}) collective-permute-start(bf16[128,1024]{1,0:T(8,128)(2,1)S(1)} %get-tuple-element.68), channel_id=1, source_target_pairs={{0,2},{1,3},{2,0},{3,1},{4,6},{5,7},{6,4},{7,5},{8,10},{9,11},{10,... | collective-permute-start | bytes 786440 | tf_op jit(solution)/shard_map/ppermute | solution.py:382
  68.3 2.8 %expert_act_1.1 = (bf16[256,256]{1,0:T(8,128)(2,1)S(1)}, bf16[128,1024]{1,0:T(8,128)(2,1)S(1)}) custom-call(bf16[2,256,2048]{2,1,0:T(8,128)(2,1)S(1)} %bitcast.33, f32[2,1,2048]{2,1,0:T(1,128)S(1)} %bitcast.35, bf16[2,4096,256]{2,1,0:T(8,128)(2,1)} %g_hbm.3, bf16[2,4096,256]{2,1,0:T(8,128)(2,1)} %u_hbm.3, bf16[256,1024]{1,0:T(8,128)(2,1)S(1)} %copy-done.2, ...), custom_call_target="tpu_custom_call" | custom-call | flops 536870912 | bytes 6291456 | tf_op jit(solution)/shard_map/expert_act_1/pallas_call | solution.py:249
  71.8 1.0 %collective-permute-start.4 = (bf16[256,256]{1,0:T(8,128)(2,1)S(1)}, bf16[256,256]{1,0:T(8,128)(2,1)S(1)}, u32[]{:S(2)}, u32[]{:S(2)}) collective-permute-start(bf16[256,256]{1,0:T(8,128)(2,1)S(1)} %get-tuple-element.61.a_ref), channel_id=1, source_target_pairs={{0,1},{1,2},{2,3},{3,0},{4,5},{5,6},{6,7},{7,4},{8,9},{9,10},{10,1... | collective-permute-start | bytes 393224 | tf_op jit(solution)/shard_map/ppermute | solution.py:382
  72.8 1.6 %collective-permute-start.5 = (bf16[256,256]{1,0:T(8,128)(2,1)S(1)}, bf16[256,256]{1,0:T(8,128)(2,1)S(1)}, u32[]{:S(2)}, u32[]{:S(2)}) collective-permute-start(bf16[256,256]{1,0:T(8,128)(2,1)S(1)} %get-tuple-element.61.a_ref), channel_id=1, source_target_pairs={{0,3},{1,0},{2,1},{3,2},{4,7},{5,4},{6,5},{7,6},{8,11},{9,8},{10,9... | collective-permute-start | bytes 393224 | tf_op jit(solution)/shard_map/ppermute | solution.py:382
  74.5 1.4 %own_down.1 = (f32[256,1024]{1,0:T(8,128)S(1)}, bf16[256,1024]{1,0:T(8,128)(2,1)S(1)}, bf16[256,1024]{1,0:T(8,128)(2,1)S(1)}, bf16[256,1024]{1,0:T(8,128)(2,1)S(1)}, bf16[256,1024]{1,0:T(8,128)(2,1)S(1)}) custom-call(bf16[256,256]{1,0:T(8,128)(2,1)S(1)} %get-tuple-element.61.a_ref, bf16[256,1024]{1,0:T(8,128)(2,1)S(1)} %copy-done, ...), custom_call_target="tpu_custom_call" | custom-call | bytes 8388608 | tf_op jit(solution)/shard_map/own_down/pallas_call | solution.py:298
  75.9 8.2 %collective-permute-done.4.refs_0_ = bf16[256,256]{1,0:T(8,128)(2,1)S(1)} collective-permute-done((bf16[256,256]{1,0:T(8,128)(2,1)S(1)}, bf16[256,256]{1,0:T(8,128)(2,1)S(1)}, u32[]{:S(2)}, u32[]{:S(2)}) %collective-permute-start.4) | collective-permute-done | bytes 131104 | tf_op jit(solution)/shard_map/ppermute | solution.py:382
  84.1 1.3 %experts_down.1 = bf16[512,512]{1,0:T(8,128)(2,1)} custom-call(bf16[256,256]{1,0:T(8,128)(2,1)S(1)} %collective-permute-done.4.refs_0_, bf16[256,256]{1,0:T(8,128)(2,1)S(1)} %collective-permute-done.5.refs_1_, bf16[256,1024]{1,0:T(8,128)(2,1)S(1)} %get-tuple-element.69.refs_2_, bf16[256,1024]{1,0:T(8,128)(2,1)S(1)} %get-tuple-element.70.refs_3_, ...), custom_call_target="tpu_custom_call" | custom-call | tf_op jit(solution)/shard_map/experts_down/pallas_call | solution.py:341
  85.3 4.2 %all-to-all-start.1 = ((bf16[32,16,512]{2,1,0:T(8,128)(2,1)}), bf16[32,16,512]{2,1,0:T(8,128)(2,1)S(1)}, u32[]{:S(2)}, u32[]{:S(2)}) async-start(bf16[32,16,512]{2,1,0:T(8,128)(2,1)} %bitcast.14), calls=%async_computation.1 | async-start | bytes 1048576 | tf_op jit(solution)/shard_map/all_to_all | solution.py:447
  89.9 10.7 %all-to-all-done.1 = bf16[32,16,512]{2,1,0:T(8,128)(2,1)S(1)} async-done(((bf16[32,16,512]{2,1,0:T(8,128)(2,1)}), bf16[32,16,512]{2,1,0:T(8,128)(2,1)S(1)}, u32[]{:S(2)}, u32[]{:S(2)}) %all-to-all-start.1) | async-done | bytes 524320 | tf_op jit(solution)/shard_map/all_to_all | solution.py:447
  (44 shorter events, 4.8 us)
Async XLA Ops:
  0.0 10.1 %copy-start.7 = (s32[32,8]{0,1:T(8,128)S(1)}, s32[32,8]{0,1:T(8,128)}, u32[]{:S(2)}) copy-start(s32[32,8]{0,1:T(8,128)} %param.23) | copy-start | bytes 3076
  0.0 17.2 %copy-start.4 = (f32[4096]{0:T(1024)S(1)}, f32[4096]{0:T(1024)}, u32[]{:S(2)}) copy-start(f32[4096]{0:T(1024)} %param.22) | copy-start | bytes 49156
  8.5 13.6 %copy-start.5 = (bf16[32,4096]{1,0:T(8,128)(2,1)S(1)}, bf16[32,4096]{1,0:T(8,128)(2,1)}, u32[]{:S(2)}) copy-start(bf16[32,4096]{1,0:T(8,128)(2,1)} %param.21) | copy-start | bytes 786436
  8.5 2.7 %collective-permute-start = (bf16[32,2048]{1,0:T(8,128)(2,1)}, bf16[32,2048]{1,0:T(8,128)(2,1)S(1)}, u32[]{:S(2)}, u32[]{:S(2)}) collective-permute-start(bf16[32,2048]{1,0:T(8,128)(2,1)} %get-tuple-element.41), channel_id=1, source_target_pairs={{0,64},{64,0},{1,65},{65,1},{2,66},{66,2},{3,67},{67,3},{4,68},{68... | collective-permute-start | bytes 393224 | tf_op jit(solution)/shard_map/ppermute | solution.py:396
  12.2 8.7 %collective-permute-start.1 = (bf16[32,2048]{1,0:T(8,128)(2,1)S(1)}, bf16[32,2048]{1,0:T(8,128)(2,1)S(1)}, u32[]{:S(2)}, u32[]{:S(2)}) collective-permute-start(bf16[32,2048]{1,0:T(8,128)(2,1)S(1)} %add_convert_fusion), channel_id=1, source_target_pairs={{0,1},{1,2},{2,3},{3,0},{4,5},{5,6},{6,7},{7,4},{8,9},{9,10},{10,1... | collective-permute-start | bytes 393224 | tf_op jit(solution)/shard_map/ppermute | solution.py:382
  13.6 8.5 %collective-permute-start.2 = (bf16[32,2048]{1,0:T(8,128)(2,1)S(1)}, bf16[32,2048]{1,0:T(8,128)(2,1)S(1)}, u32[]{:S(2)}, u32[]{:S(2)}) collective-permute-start(bf16[32,2048]{1,0:T(8,128)(2,1)S(1)} %add_convert_fusion), channel_id=1, source_target_pairs={{0,2},{1,3},{2,0},{3,1},{4,6},{5,7},{6,4},{7,5},{8,10},{9,11},{10,... | collective-permute-start | bytes 393224 | tf_op jit(solution)/shard_map/ppermute | solution.py:382
  16.0 6.1 %collective-permute-start.3 = (bf16[32,2048]{1,0:T(8,128)(2,1)S(1)}, bf16[32,2048]{1,0:T(8,128)(2,1)S(1)}, u32[]{:S(2)}, u32[]{:S(2)}) collective-permute-start(bf16[32,2048]{1,0:T(8,128)(2,1)S(1)} %add_convert_fusion), channel_id=1, source_target_pairs={{0,3},{1,0},{2,1},{3,2},{4,7},{5,4},{6,5},{7,6},{8,11},{9,8},{10,9... | collective-permute-start | bytes 393224 | tf_op jit(solution)/shard_map/ppermute | solution.py:382
  24.3 37.7 %all-to-all-start = ((bf16[32,16,2048]{2,1,0:T(8,128)(2,1)}), bf16[32,16,2048]{2,1,0:T(8,128)(2,1)S(1)}, u32[]{:S(2)}, u32[]{:S(2)}) async-start(bf16[32,16,2048]{2,1,0:T(8,128)(2,1)} %bitcast.37), calls=%async_computation | async-start | bytes 4194304 | tf_op jit(solution)/shard_map/all_to_all | solution.py:432
  33.6 37.5 %collective-permute-start.6 = (bf16[256,1024]{1,0:T(8,128)(2,1)}, bf16[256,1024]{1,0:T(8,128)(2,1)S(1)}, u32[]{:S(2)}, u32[]{:S(2)}) collective-permute-start(bf16[256,1024]{1,0:T(8,128)(2,1)} %get-tuple-element.57), channel_id=1, source_target_pairs={{0,1},{1,2},{2,3},{3,0},{4,5},{5,6},{6,7},{7,4},{8,9},{9,10},{10,1... | collective-permute-start | bytes 1572872 | tf_op jit(solution)/shard_map/ppermute | solution.py:382
  34.7 37.0 %collective-permute-start.7 = (bf16[256,1024]{1,0:T(8,128)(2,1)}, bf16[256,1024]{1,0:T(8,128)(2,1)S(1)}, u32[]{:S(2)}, u32[]{:S(2)}) collective-permute-start(bf16[256,1024]{1,0:T(8,128)(2,1)} %get-tuple-element.58), channel_id=1, source_target_pairs={{0,1},{1,2},{2,3},{3,0},{4,5},{5,6},{6,7},{7,4},{8,9},{9,10},{10,1... | collective-permute-start | bytes 1572872 | tf_op jit(solution)/shard_map/ppermute | solution.py:382
  35.7 37.1 %collective-permute-start.8 = (bf16[256,1024]{1,0:T(8,128)(2,1)}, bf16[256,1024]{1,0:T(8,128)(2,1)}, u32[]{:S(2)}, u32[]{:S(2)}) collective-permute-start(bf16[256,1024]{1,0:T(8,128)(2,1)} %get-tuple-element.59), channel_id=1, source_target_pairs={{0,3},{1,0},{2,1},{3,2},{4,7},{5,4},{6,5},{7,6},{8,11},{9,8},{10,9... | collective-permute-start | bytes 1572872 | tf_op jit(solution)/shard_map/ppermute | solution.py:382
  37.4 37.0 %collective-permute-start.9 = (bf16[256,1024]{1,0:T(8,128)(2,1)}, bf16[256,1024]{1,0:T(8,128)(2,1)}, u32[]{:S(2)}, u32[]{:S(2)}) collective-permute-start(bf16[256,1024]{1,0:T(8,128)(2,1)} %get-tuple-element.60), channel_id=1, source_target_pairs={{0,3},{1,0},{2,1},{3,2},{4,7},{5,4},{6,5},{7,6},{8,11},{9,8},{10,9... | collective-permute-start | bytes 1572872 | tf_op jit(solution)/shard_map/ppermute | solution.py:382
  62.0 1.0 %copy-start.3 = (bf16[256,1024]{1,0:T(8,128)(2,1)S(1)}, bf16[256,1024]{1,0:T(8,128)(2,1)}, u32[]{:S(2)}) copy-start(bf16[256,1024]{1,0:T(8,128)(2,1)} %get-tuple-element.54.w_ref) | copy-start | bytes 1572868
  63.1 5.2 %copy-start.2 = (bf16[256,1024]{1,0:T(8,128)(2,1)S(1)}, bf16[256,1024]{1,0:T(8,128)(2,1)}, u32[]{:S(2)}) copy-start(bf16[256,1024]{1,0:T(8,128)(2,1)} %get-tuple-element.53.w_ref) | copy-start | bytes 1572868
  65.8 8.7 %collective-permute-start.10 = (bf16[128,1024]{1,0:T(8,128)(2,1)S(1)}, bf16[128,1024]{1,0:T(8,128)(2,1)S(1)}, u32[]{:S(2)}, u32[]{:S(2)}) collective-permute-start(bf16[128,1024]{1,0:T(8,128)(2,1)S(1)} %get-tuple-element.68), channel_id=1, source_target_pairs={{0,2},{1,3},{2,0},{3,1},{4,6},{5,7},{6,4},{7,5},{8,10},{9,11},{10,... | collective-permute-start | bytes 786440 | tf_op jit(solution)/shard_map/ppermute | solution.py:382
  68.3 6.2 %copy-start = (bf16[256,1024]{1,0:T(8,128)(2,1)S(1)}, bf16[256,1024]{1,0:T(8,128)(2,1)}, u32[]{:S(2)}) copy-start(bf16[256,1024]{1,0:T(8,128)(2,1)} %get-tuple-element.62.refs_0_) | copy-start | bytes 1572868
  68.3 6.2 %copy-start.1 = (bf16[256,1024]{1,0:T(8,128)(2,1)S(1)}, bf16[256,1024]{1,0:T(8,128)(2,1)}, u32[]{:S(2)}) copy-start(bf16[256,1024]{1,0:T(8,128)(2,1)} %get-tuple-element.63.refs_1_) | copy-start | bytes 1572868
  71.1 13.0 %collective-permute-start.11 = (bf16[128,1024]{1,0:T(8,128)(2,1)S(1)}, bf16[128,1024]{1,0:T(8,128)(2,1)S(1)}, u32[]{:S(2)}, u32[]{:S(2)}) collective-permute-start(bf16[128,1024]{1,0:T(8,128)(2,1)S(1)} %get-tuple-element.74), channel_id=1, source_target_pairs={{0,2},{1,3},{2,0},{3,1},{4,6},{5,7},{6,4},{7,5},{8,10},{9,11},{10,... | collective-permute-start | bytes 786440 | tf_op jit(solution)/shard_map/ppermute | solution.py:382
  71.8 17.7 %copy-start.6 = (f32[32,8]{0,1:T(8,128)S(1)}, f32[32,8]{0,1:T(8,128)}, u32[]{:S(2)}) copy-start(f32[32,8]{0,1:T(8,128)} %param.24) | copy-start | bytes 3076
  71.8 12.3 %collective-permute-start.4 = (bf16[256,256]{1,0:T(8,128)(2,1)S(1)}, bf16[256,256]{1,0:T(8,128)(2,1)S(1)}, u32[]{:S(2)}, u32[]{:S(2)}) collective-permute-start(bf16[256,256]{1,0:T(8,128)(2,1)S(1)} %get-tuple-element.61.a_ref), channel_id=1, source_target_pairs={{0,1},{1,2},{2,3},{3,0},{4,5},{5,6},{6,7},{7,4},{8,9},{9,10},{10,1... | collective-permute-start | bytes 393224 | tf_op jit(solution)/shard_map/ppermute | solution.py:382
  72.8 11.2 %collective-permute-start.5 = (bf16[256,256]{1,0:T(8,128)(2,1)S(1)}, bf16[256,256]{1,0:T(8,128)(2,1)S(1)}, u32[]{:S(2)}, u32[]{:S(2)}) collective-permute-start(bf16[256,256]{1,0:T(8,128)(2,1)S(1)} %get-tuple-element.61.a_ref), channel_id=1, source_target_pairs={{0,3},{1,0},{2,1},{3,2},{4,7},{5,4},{6,5},{7,6},{8,11},{9,8},{10,9... | collective-permute-start | bytes 393224 | tf_op jit(solution)/shard_map/ppermute | solution.py:382
  85.3 15.3 %all-to-all-start.1 = ((bf16[32,16,512]{2,1,0:T(8,128)(2,1)}), bf16[32,16,512]{2,1,0:T(8,128)(2,1)S(1)}, u32[]{:S(2)}, u32[]{:S(2)}) async-start(bf16[32,16,512]{2,1,0:T(8,128)(2,1)} %bitcast.14), calls=%async_computation.1 | async-start | bytes 1048576 | tf_op jit(solution)/shard_map/all_to_all | solution.py:447

commit v9 on v8

--- a/solution.py
+++ b/solution.py
@@ -200,17 +200,28 @@
     return jnp.concatenate(parts, axis=1).reshape(len(values) * rows, columns)
 
 
-def expert_act(tokens, gain, w_gate, w_up, across, e, before, capacity):
+def expert_act(tokens, gain, w_gate, w_up, w_down, place_across, w_down_places, e, before, capacity):
     roles, slots, half = tokens.shape
     per_dev, width, quarter = w_gate.shape
-    columns = across.shape[1]
+    columns = w_down.shape[2] // w_down_places
+    piece = columns // roles
     chunk = 512
     rows = slots // per_dev
     done = e * rows
 
-    def body(x_ref, gain_ref, g_hbm, u_hbm, w_ref, *rest):
+    def body(place_ref, x_ref, gain_ref, g_hbm, u_hbm, w_hbm, *rest):
         before_ref = rest[0] if e else None
-        act_ref, far_ref, g_ref, u_ref, sums, sems = rest[1 if e else 0 :]
+        act_ref, far_ref, g_ref, u_ref, w_ref, sums, w_sems, sems = rest[1 if e else 0 :]
+        last = []
+        for s in range(roles):
+            start = pl.multiple_of(s * half + place_ref[0] * piece, piece)
+            last.append(
+                pltpu.make_async_copy(
+                    w_hbm.at[e, :, pl.ds(start, piece)],
+                    w_ref.at[:, pl.ds(s * piece, piece)],
+                    w_sems.at[s],
+                )
+            )
         copies = []
         for k in range(width // chunk):
             place = pl.ds(k * chunk, chunk)
@@ -223,6 +234,8 @@
         for pair in copies:
             for copy in pair:
                 copy.start()
+        for copy in last:
+            copy.start()
         square = jnp.zeros((rows, 1), F32)
         for k in range(width // chunk):
             s, place = divmod(k * chunk, half)
@@ -244,6 +257,8 @@
         if e:
             act_ref[:done] = before_ref[...]
         act_ref[done:] = act
+        for copy in last:
+            copy.wait()
         far_ref[...] = jnp.dot(act, w_ref[...], preferred_element_type=F32).astype(BF)
 
     return pl.pallas_call(
@@ -252,14 +267,17 @@
             jax.ShapeDtypeStruct((done + rows, quarter), BF),
             jax.ShapeDtypeStruct((rows, columns), BF),
         ],
-        in_specs=whole(2)
-        + [pl.BlockSpec(memory_space=pltpu.HBM)] * 2
-        + whole(2 if e else 1),
+        in_specs=[pl.BlockSpec(memory_space=pltpu.SMEM)]
+        + whole(2)
+        + [pl.BlockSpec(memory_space=pltpu.HBM)] * 3
+        + whole(1 if e else 0),
         out_specs=whole(2),
         scratch_shapes=[
             pltpu.VMEM((width, quarter), BF),
             pltpu.VMEM((width, quarter), BF),
+            pltpu.VMEM((quarter, columns), BF),
             pltpu.VMEM((2, rows, quarter), F32),
+            pltpu.SemaphoreType.DMA((roles,)),
             pltpu.SemaphoreType.DMA((2 * (width // chunk),)),
         ],
         compiler_params=pltpu.CompilerParams(vmem_limit_bytes=49 << 20),
@@ -267,7 +285,7 @@
             flops=4 * rows * width * quarter, bytes_accessed=6 << 20, transcendentals=0
         ),
         name=f"expert_act_{e}",
-    )(tokens, gain, w_gate, w_up, across, *([before] if e else []))
+    )(place_across.reshape(1), tokens, gain, w_gate, w_up, w_down, *([before] if e else []))
 
 
 def own_down(act, own, others, fars):
@@ -397,7 +415,7 @@
     chip = (mine + received.astype(F32)).astype(BF)
     chip, w_down = lax.optimization_barrier((chip, w_down))
     across, near = heads_count // 2, (0, 1, heads_count - 1)
-    pieces = [(step, e) for step in (*near, across) for e in range(per_dev)]
+    pieces = [(step, e) for step in near for e in range(per_dev)]
     rest = cut_down(w_down, head, heads_count, roles, pieces)
     total = chip.astype(F32)
     for step in range(1, heads_count):
@@ -432,10 +450,12 @@
     incoming = lax.all_to_all(outgoing, ("role", "rows"), 0, 0, tiled=True)
     tokens = incoming.reshape(roles, shards * per_dev * capacity, half)
     flat_gain = norm_gain.reshape(roles, 1, half)
+    opposite = lax.rem(head + across, heads_count)
     act, fars = None, []
     for e in range(per_dev):
-        opposite = rest[len(near) * per_dev + e]
-        act, far = expert_act(tokens, flat_gain, w_gate, w_up, opposite, e, act, capacity)
+        act, far = expert_act(
+            tokens, flat_gain, w_gate, w_up, w_down, opposite, heads_count, e, act, capacity
+        )
         fars.append(shift(far, across))
     acts = [shift(act, step) for step in near[1:]]
     others = [w for each in downs[1:] for w in each]

time: 102 us -> 101 us (level)
  local copies, waits for them, and re-layouts: 1.58 us -> 0.54 us
    unnamed x17 -> x13, local copies, waits for them, and re-layouts: 1.15 us -> 0.1 us
where the time goes in v9:
time: 101 us
  waiting for transfers between devices  44.9 us (44%)
  starting transfers between devices  30 us (30%)
  Pallas kernels  20.5 us (20%)
  matrix products  3.32 us (3%)
  other arithmetic  1.39 us (1%)
    all_to_all x1, waiting for transfers between devices, per_device(): incoming = lax.all_to_all(outgoing, ('role', 'rows'), 0, 0, tiled=True)  24.2 us
    ppermute x11, starting transfers between devices, shift(): lax.ppermute(x, 'heads', [(i, (i + step) % heads_count) for i in range(he...  15 us
    all_to_all x1, waiting for transfers between devices, per_device(): returned = lax.all_to_all(result, ('role', 'rows'), 0, 0, tiled=True)  10.7 us
    ppermute x11, waiting for transfers between devices, shift(): lax.ppermute(x, 'heads', [(i, (i + step) % heads_count) for i in range(he...  9.42 us
    all_to_all x1, starting transfers between devices, per_device(): incoming = lax.all_to_all(outgoing, ('role', 'rows'), 0, 0, tiled=True)  9.3 us
    pallas_call x1, Pallas kernels, attend(): pl.pallas_call(body, out_shape=[jax.ShapeDtypeStruct((rows, half), BF), j...  8.53 us
    pallas_call x2, Pallas kernels, expert_act(): pl.pallas_call(body, out_shape=[jax.ShapeDtypeStruct((done + rows, quarte...  5.83 us
    all_to_all x1, starting transfers between devices, per_device(): returned = lax.all_to_all(result, ('role', 'rows'), 0, 0, tiled=True)  4.2 us
  transfers between devices with their start and end apart: 14, of which 5 were waited for; matrix products, arithmetic and copies ran while one was open for 1% of the time, Pallas kernels for 11%

profile of v9, /device:TPU:1, one launch (start us, length us, event | category | flops | bytes accessed | tf_op | source)
XLA Modules:
  0.0 100.8 jit_solution(17757616155510197118)
XLA Ops:
  0.0 8.5 %attend.1 = (bf16[32,2048]{1,0:T(8,128)(2,1)}, f32[32,2048]{1,0:T(8,128)}) custom-call(s32[1]{0:T(128)} %bitcast.role_ref, s32[32]{0:T(128)} %len_ref.1, bf16[32,1024]{1,0:T(8,128)(2,1)} %bitcast.43, bf16[32,512,128]{2,1,0:T(8,128)(2,1)} %bitcast.41, bf16[32,512,128]{2,1,0:T(8,128)(2,1)} %bitcast.42, bf16[32,128]{1,0:T(8,128)(2,1)} %bitcast.44, ...), custom_call_target="tpu_custom_call" | custom-call | bytes 1048576 | tf_op jit(solution)/shard_map/attend/pallas_call | solution.py:154
  8.6 1.5 %collective-permute-start = (bf16[32,2048]{1,0:T(8,128)(2,1)}, bf16[32,2048]{1,0:T(8,128)(2,1)S(1)}, u32[]{:S(2)}, u32[]{:S(2)}) collective-permute-start(bf16[32,2048]{1,0:T(8,128)(2,1)} %get-tuple-element.37), channel_id=1, source_target_pairs={{0,64},{64,0},{1,65},{65,1},{2,66},{66,2},{3,67},{67,3},{4,68},{68... | collective-permute-start | bytes 393224 | tf_op jit(solution)/shard_map/ppermute | solution.py:414
  11.3 1.0 add_convert_fusion
  12.2 1.4 %collective-permute-start.1 = (bf16[32,2048]{1,0:T(8,128)(2,1)S(1)}, bf16[32,2048]{1,0:T(8,128)(2,1)S(1)}, u32[]{:S(2)}, u32[]{:S(2)}) collective-permute-start(bf16[32,2048]{1,0:T(8,128)(2,1)S(1)} %add_convert_fusion), channel_id=1, source_target_pairs={{0,1},{1,2},{2,3},{3,0},{4,5},{5,6},{6,7},{7,4},{8,9},{9,10},{10,1... | collective-permute-start | bytes 393224 | tf_op jit(solution)/shard_map/ppermute | solution.py:400
  13.6 2.5 %collective-permute-start.2 = (bf16[32,2048]{1,0:T(8,128)(2,1)S(1)}, bf16[32,2048]{1,0:T(8,128)(2,1)S(1)}, u32[]{:S(2)}, u32[]{:S(2)}) collective-permute-start(bf16[32,2048]{1,0:T(8,128)(2,1)S(1)} %add_convert_fusion), channel_id=1, source_target_pairs={{0,2},{1,3},{2,0},{3,1},{4,6},{5,7},{6,4},{7,5},{8,10},{9,11},{10,... | collective-permute-start | bytes 393224 | tf_op jit(solution)/shard_map/ppermute | solution.py:400
  16.1 1.2 %collective-permute-start.3 = (bf16[32,2048]{1,0:T(8,128)(2,1)S(1)}, bf16[32,2048]{1,0:T(8,128)(2,1)S(1)}, u32[]{:S(2)}, u32[]{:S(2)}) collective-permute-start(bf16[32,2048]{1,0:T(8,128)(2,1)S(1)} %add_convert_fusion), channel_id=1, source_target_pairs={{0,3},{1,0},{2,1},{3,2},{4,7},{5,4},{6,5},{7,6},{8,11},{9,8},{10,9... | collective-permute-start | bytes 393224 | tf_op jit(solution)/shard_map/ppermute | solution.py:400
  17.2 3.5 %cut_down.1 = (bf16[256,1024]{1,0:T(8,128)(2,1)}, bf16[256,1024]{1,0:T(8,128)(2,1)}, bf16[256,1024]{1,0:T(8,128)(2,1)}, bf16[256,1024]{1,0:T(8,128)(2,1)}, bf16[...) custom-call(s32[1]{0:T(128)} %bitcast.7.head_ref, bf16[2,256,4096]{2,1,0:T(8,128)(2,1)} %w_hbm.2), custom_call_target="tpu_custom_call" | custom-call | bytes 8388608 | tf_op jit(solution)/shard_map/cut_down/pallas_call | solution.py:61
  20.8 1.4 %collective-permute-done.2 = bf16[32,2048]{1,0:T(8,128)(2,1)S(1)} collective-permute-done((bf16[32,2048]{1,0:T(8,128)(2,1)S(1)}, bf16[32,2048]{1,0:T(8,128)(2,1)S(1)}, u32[]{:S(2)}, u32[]{:S(2)}) %collective-permute-start.2) | collective-permute-done | bytes 131104 | tf_op jit(solution)/shard_map/ppermute | solution.py:400
  22.2 2.1 %convolution_convert_fusion = bf16[512,2048]{1,0:T(8,128)(2,1)} fusion(f32[32,2048]{1,0:T(8,128)S(1)} %add_add_fusion, f32[2048]{0:T(1024)S(1)} %slice_select_fusion, s32[512]{0:T(512)S(1)} %eq.64, s32[32,64]{0,1:T(8,128)S(1)} %copy.22, pred[32,64]{0,1:T(8,128)(4,1)S(1)} %copy.21), kind=kOutput, calls=%fused_computation | convolution fusion | flops 68321280 | bytes 2379776 | tf_op jit(solution)/shard_map/dot_general | solution.py:446
  24.3 9.3 %all-to-all-start = ((bf16[32,16,2048]{2,1,0:T(8,128)(2,1)}), bf16[32,16,2048]{2,1,0:T(8,128)(2,1)S(1)}, u32[]{:S(2)}, u32[]{:S(2)}) async-start(bf16[32,16,2048]{2,1,0:T(8,128)(2,1)} %bitcast.38), calls=%async_computation | async-start | bytes 4194304 | tf_op jit(solution)/shard_map/all_to_all | solution.py:450
  33.6 1.1 %collective-permute-start.6 = (bf16[256,1024]{1,0:T(8,128)(2,1)}, bf16[256,1024]{1,0:T(8,128)(2,1)S(1)}, u32[]{:S(2)}, u32[]{:S(2)}) collective-permute-start(bf16[256,1024]{1,0:T(8,128)(2,1)} %get-tuple-element.49), channel_id=1, source_target_pairs={{0,1},{1,2},{2,3},{3,0},{4,5},{5,6},{6,7},{7,4},{8,9},{9,10},{10,1... | collective-permute-start | bytes 1572872 | tf_op jit(solution)/shard_map/ppermute | solution.py:400
  34.8 1.0 collective-permute-start.7
  35.8 1.7 %collective-permute-start.8 = (bf16[256,1024]{1,0:T(8,128)(2,1)}, bf16[256,1024]{1,0:T(8,128)(2,1)}, u32[]{:S(2)}, u32[]{:S(2)}) collective-permute-start(bf16[256,1024]{1,0:T(8,128)(2,1)} %get-tuple-element.51), channel_id=1, source_target_pairs={{0,3},{1,0},{2,1},{3,2},{4,7},{5,4},{6,5},{7,6},{8,11},{9,8},{10,9... | collective-permute-start | bytes 1572872 | tf_op jit(solution)/shard_map/ppermute | solution.py:400
  37.8 24.2 %all-to-all-done = bf16[32,16,2048]{2,1,0:T(8,128)(2,1)S(1)} async-done(((bf16[32,16,2048]{2,1,0:T(8,128)(2,1)}), bf16[32,16,2048]{2,1,0:T(8,128)(2,1)S(1)}, u32[]{:S(2)}, u32[]{:S(2)}) %all-to-all-start) | async-done | bytes 2097184 | tf_op jit(solution)/shard_map/all_to_all | solution.py:450
  62.0 2.9 %expert_act_0.1 = (bf16[128,256]{1,0:T(8,128)(2,1)S(1)}, bf16[128,1024]{1,0:T(8,128)(2,1)S(1)}) custom-call(s32[1]{0:T(128)} %bitcast.9.place_ref, bf16[2,256,2048]{2,1,0:T(8,128)(2,1)S(1)} %bitcast.33, f32[2,1,2048]{2,1,0:T(1,128)S(1)} %bitcast.35, bf16[2,4096,256]{2,1,0:T(8,128)(2,1)} %g_hbm.3, bf16[2,4096,256]{2,1,0:T(8,128)(2,1)} %u_hbm.3, ...), custom_call_target="tpu_custom_call" | custom-call | flops 536870912 | bytes 6291456 | tf_op jit(solution)/shard_map/expert_act_0/pallas_call | solution.py:264
  64.9 2.5 %collective-permute-start.10 = (bf16[128,1024]{1,0:T(8,128)(2,1)S(1)}, bf16[128,1024]{1,0:T(8,128)(2,1)S(1)}, u32[]{:S(2)}, u32[]{:S(2)}) collective-permute-start(bf16[128,1024]{1,0:T(8,128)(2,1)S(1)} %get-tuple-element.60), channel_id=1, source_target_pairs={{0,2},{1,3},{2,0},{3,1},{4,6},{5,7},{6,4},{7,5},{8,10},{9,11},{10,... | collective-permute-start | bytes 786440 | tf_op jit(solution)/shard_map/ppermute | solution.py:400
  67.4 3.0 %expert_act_1.1 = (bf16[256,256]{1,0:T(8,128)(2,1)S(1)}, bf16[128,1024]{1,0:T(8,128)(2,1)S(1)}) custom-call(s32[1]{0:T(128)} %bitcast.9.place_ref, bf16[2,256,2048]{2,1,0:T(8,128)(2,1)S(1)} %bitcast.34, f32[2,1,2048]{2,1,0:T(1,128)S(1)} %bitcast.36, bf16[2,4096,256]{2,1,0:T(8,128)(2,1)} %g_hbm.3, bf16[2,4096,256]{2,1,0:T(8,128)(2,1)} %u_hbm.3, ...), custom_call_target="tpu_custom_call" | custom-call | flops 536870912 | bytes 6291456 | tf_op jit(solution)/shard_map/expert_act_1/pallas_call | solution.py:264
  71.0 1.1 %collective-permute-start.4 = (bf16[256,256]{1,0:T(8,128)(2,1)S(1)}, bf16[256,256]{1,0:T(8,128)(2,1)S(1)}, u32[]{:S(2)}, u32[]{:S(2)}) collective-permute-start(bf16[256,256]{1,0:T(8,128)(2,1)S(1)} %get-tuple-element.53.a_ref), channel_id=1, source_target_pairs={{0,1},{1,2},{2,3},{3,0},{4,5},{5,6},{6,7},{7,4},{8,9},{9,10},{10,1... | collective-permute-start | bytes 393224 | tf_op jit(solution)/shard_map/ppermute | solution.py:400
  72.1 1.6 %collective-permute-start.5 = (bf16[256,256]{1,0:T(8,128)(2,1)S(1)}, bf16[256,256]{1,0:T(8,128)(2,1)S(1)}, u32[]{:S(2)}, u32[]{:S(2)}) collective-permute-start(bf16[256,256]{1,0:T(8,128)(2,1)S(1)} %get-tuple-element.53.a_ref), channel_id=1, source_target_pairs={{0,3},{1,0},{2,1},{3,2},{4,7},{5,4},{6,5},{7,6},{8,11},{9,8},{10,9... | collective-permute-start | bytes 393224 | tf_op jit(solution)/shard_map/ppermute | solution.py:400
  73.7 1.4 %own_down.1 = (f32[256,1024]{1,0:T(8,128)S(1)}, bf16[256,1024]{1,0:T(8,128)(2,1)S(1)}, bf16[256,1024]{1,0:T(8,128)(2,1)S(1)}, bf16[256,1024]{1,0:T(8,128)(2,1)S(1)}, bf16[256,1024]{1,0:T(8,128)(2,1)S(1)}) custom-call(bf16[256,256]{1,0:T(8,128)(2,1)S(1)} %get-tuple-element.53.a_ref, bf16[256,1024]{1,0:T(8,128)(2,1)S(1)} %copy-done, ...), custom_call_target="tpu_custom_call" | custom-call | bytes 8388608 | tf_op jit(solution)/shard_map/own_down/pallas_call | solution.py:316
  75.1 8.0 %collective-permute-done.4.refs_0_ = bf16[256,256]{1,0:T(8,128)(2,1)S(1)} collective-permute-done((bf16[256,256]{1,0:T(8,128)(2,1)S(1)}, bf16[256,256]{1,0:T(8,128)(2,1)S(1)}, u32[]{:S(2)}, u32[]{:S(2)}) %collective-permute-start.4) | collective-permute-done | bytes 131104 | tf_op jit(solution)/shard_map/ppermute | solution.py:400
  83.1 1.3 %experts_down.1 = bf16[512,512]{1,0:T(8,128)(2,1)} custom-call(bf16[256,256]{1,0:T(8,128)(2,1)S(1)} %collective-permute-done.4.refs_0_, bf16[256,256]{1,0:T(8,128)(2,1)S(1)} %collective-permute-done.5.refs_1_, bf16[256,1024]{1,0:T(8,128)(2,1)S(1)} %get-tuple-element.61.refs_2_, bf16[256,1024]{1,0:T(8,128)(2,1)S(1)} %get-tuple-element.62.refs_3_, ...), custom_call_target="tpu_custom_call" | custom-call | tf_op jit(solution)/shard_map/experts_down/pallas_call | solution.py:359
  84.4 4.2 %all-to-all-start.1 = ((bf16[32,16,512]{2,1,0:T(8,128)(2,1)}), bf16[32,16,512]{2,1,0:T(8,128)(2,1)S(1)}, u32[]{:S(2)}, u32[]{:S(2)}) async-start(bf16[32,16,512]{2,1,0:T(8,128)(2,1)} %bitcast.15), calls=%async_computation.1 | async-start | bytes 1048576 | tf_op jit(solution)/shard_map/all_to_all | solution.py:467
  89.0 10.7 %all-to-all-done.1 = bf16[32,16,512]{2,1,0:T(8,128)(2,1)S(1)} async-done(((bf16[32,16,512]{2,1,0:T(8,128)(2,1)}), bf16[32,16,512]{2,1,0:T(8,128)(2,1)S(1)}, u32[]{:S(2)}, u32[]{:S(2)}) %all-to-all-start.1) | async-done | bytes 524320 | tf_op jit(solution)/shard_map/all_to_all | solution.py:467
  (40 shorter events, 3.8 us)
Async XLA Ops:
  0.0 10.1 %copy-start.5 = (s32[32,8]{0,1:T(8,128)S(1)}, s32[32,8]{0,1:T(8,128)}, u32[]{:S(2)}) copy-start(s32[32,8]{0,1:T(8,128)} %param.23) | copy-start | bytes 3076
  0.0 17.2 %copy-start.2 = (f32[4096]{0:T(1024)S(1)}, f32[4096]{0:T(1024)}, u32[]{:S(2)}) copy-start(f32[4096]{0:T(1024)} %param.22) | copy-start | bytes 49156
  8.5 13.6 %copy-start.3 = (bf16[32,4096]{1,0:T(8,128)(2,1)S(1)}, bf16[32,4096]{1,0:T(8,128)(2,1)}, u32[]{:S(2)}) copy-start(bf16[32,4096]{1,0:T(8,128)(2,1)} %param.21) | copy-start | bytes 786436
  8.6 2.7 %collective-permute-start = (bf16[32,2048]{1,0:T(8,128)(2,1)}, bf16[32,2048]{1,0:T(8,128)(2,1)S(1)}, u32[]{:S(2)}, u32[]{:S(2)}) collective-permute-start(bf16[32,2048]{1,0:T(8,128)(2,1)} %get-tuple-element.37), channel_id=1, source_target_pairs={{0,64},{64,0},{1,65},{65,1},{2,66},{66,2},{3,67},{67,3},{4,68},{68... | collective-permute-start | bytes 393224 | tf_op jit(solution)/shard_map/ppermute | solution.py:414
  12.2 8.5 %collective-permute-start.1 = (bf16[32,2048]{1,0:T(8,128)(2,1)S(1)}, bf16[32,2048]{1,0:T(8,128)(2,1)S(1)}, u32[]{:S(2)}, u32[]{:S(2)}) collective-permute-start(bf16[32,2048]{1,0:T(8,128)(2,1)S(1)} %add_convert_fusion), channel_id=1, source_target_pairs={{0,1},{1,2},{2,3},{3,0},{4,5},{5,6},{6,7},{7,4},{8,9},{9,10},{10,1... | collective-permute-start | bytes 393224 | tf_op jit(solution)/shard_map/ppermute | solution.py:400
  13.6 8.5 %collective-permute-start.2 = (bf16[32,2048]{1,0:T(8,128)(2,1)S(1)}, bf16[32,2048]{1,0:T(8,128)(2,1)S(1)}, u32[]{:S(2)}, u32[]{:S(2)}) collective-permute-start(bf16[32,2048]{1,0:T(8,128)(2,1)S(1)} %add_convert_fusion), channel_id=1, source_target_pairs={{0,2},{1,3},{2,0},{3,1},{4,6},{5,7},{6,4},{7,5},{8,10},{9,11},{10,... | collective-permute-start | bytes 393224 | tf_op jit(solution)/shard_map/ppermute | solution.py:400
  16.1 6.1 %collective-permute-start.3 = (bf16[32,2048]{1,0:T(8,128)(2,1)S(1)}, bf16[32,2048]{1,0:T(8,128)(2,1)S(1)}, u32[]{:S(2)}, u32[]{:S(2)}) collective-permute-start(bf16[32,2048]{1,0:T(8,128)(2,1)S(1)} %add_convert_fusion), channel_id=1, source_target_pairs={{0,3},{1,0},{2,1},{3,2},{4,7},{5,4},{6,5},{7,6},{8,11},{9,8},{10,9... | collective-permute-start | bytes 393224 | tf_op jit(solution)/shard_map/ppermute | solution.py:400
  24.3 37.7 %all-to-all-start = ((bf16[32,16,2048]{2,1,0:T(8,128)(2,1)}), bf16[32,16,2048]{2,1,0:T(8,128)(2,1)S(1)}, u32[]{:S(2)}, u32[]{:S(2)}) async-start(bf16[32,16,2048]{2,1,0:T(8,128)(2,1)} %bitcast.38), calls=%async_computation | async-start | bytes 4194304 | tf_op jit(solution)/shard_map/all_to_all | solution.py:450
  33.6 36.7 %collective-permute-start.6 = (bf16[256,1024]{1,0:T(8,128)(2,1)}, bf16[256,1024]{1,0:T(8,128)(2,1)S(1)}, u32[]{:S(2)}, u32[]{:S(2)}) collective-permute-start(bf16[256,1024]{1,0:T(8,128)(2,1)} %get-tuple-element.49), channel_id=1, source_target_pairs={{0,1},{1,2},{2,3},{3,0},{4,5},{5,6},{6,7},{7,4},{8,9},{9,10},{10,1... | collective-permute-start | bytes 1572872 | tf_op jit(solution)/shard_map/ppermute | solution.py:400
  34.8 36.3 %collective-permute-start.7 = (bf16[256,1024]{1,0:T(8,128)(2,1)}, bf16[256,1024]{1,0:T(8,128)(2,1)S(1)}, u32[]{:S(2)}, u32[]{:S(2)}) collective-permute-start(bf16[256,1024]{1,0:T(8,128)(2,1)} %get-tuple-element.50), channel_id=1, source_target_pairs={{0,1},{1,2},{2,3},{3,0},{4,5},{5,6},{6,7},{7,4},{8,9},{9,10},{10,1... | collective-permute-start | bytes 1572872 | tf_op jit(solution)/shard_map/ppermute | solution.py:400
  35.8 36.3 %collective-permute-start.8 = (bf16[256,1024]{1,0:T(8,128)(2,1)}, bf16[256,1024]{1,0:T(8,128)(2,1)}, u32[]{:S(2)}, u32[]{:S(2)}) collective-permute-start(bf16[256,1024]{1,0:T(8,128)(2,1)} %get-tuple-element.51), channel_id=1, source_target_pairs={{0,3},{1,0},{2,1},{3,2},{4,7},{5,4},{6,5},{7,6},{8,11},{9,8},{10,9... | collective-permute-start | bytes 1572872 | tf_op jit(solution)/shard_map/ppermute | solution.py:400
  37.4 36.3 %collective-permute-start.9 = (bf16[256,1024]{1,0:T(8,128)(2,1)}, bf16[256,1024]{1,0:T(8,128)(2,1)}, u32[]{:S(2)}, u32[]{:S(2)}) collective-permute-start(bf16[256,1024]{1,0:T(8,128)(2,1)} %get-tuple-element.52), channel_id=1, source_target_pairs={{0,3},{1,0},{2,1},{3,2},{4,7},{5,4},{6,5},{7,6},{8,11},{9,8},{10,9... | collective-permute-start | bytes 1572872 | tf_op jit(solution)/shard_map/ppermute | solution.py:400
  64.9 8.8 %collective-permute-start.10 = (bf16[128,1024]{1,0:T(8,128)(2,1)S(1)}, bf16[128,1024]{1,0:T(8,128)(2,1)S(1)}, u32[]{:S(2)}, u32[]{:S(2)}) collective-permute-start(bf16[128,1024]{1,0:T(8,128)(2,1)S(1)} %get-tuple-element.60), channel_id=1, source_target_pairs={{0,2},{1,3},{2,0},{3,1},{4,6},{5,7},{6,4},{7,5},{8,10},{9,11},{10,... | collective-permute-start | bytes 786440 | tf_op jit(solution)/shard_map/ppermute | solution.py:400
  67.4 6.3 %copy-start = (bf16[256,1024]{1,0:T(8,128)(2,1)S(1)}, bf16[256,1024]{1,0:T(8,128)(2,1)}, u32[]{:S(2)}) copy-start(bf16[256,1024]{1,0:T(8,128)(2,1)} %get-tuple-element.54.refs_0_) | copy-start | bytes 1572868
  67.4 6.4 %copy-start.1 = (bf16[256,1024]{1,0:T(8,128)(2,1)S(1)}, bf16[256,1024]{1,0:T(8,128)(2,1)}, u32[]{:S(2)}) copy-start(bf16[256,1024]{1,0:T(8,128)(2,1)} %get-tuple-element.55.refs_1_) | copy-start | bytes 1572868
  70.3 12.8 %collective-permute-start.11 = (bf16[128,1024]{1,0:T(8,128)(2,1)S(1)}, bf16[128,1024]{1,0:T(8,128)(2,1)S(1)}, u32[]{:S(2)}, u32[]{:S(2)}) collective-permute-start(bf16[128,1024]{1,0:T(8,128)(2,1)S(1)} %get-tuple-element.66), channel_id=1, source_target_pairs={{0,2},{1,3},{2,0},{3,1},{4,6},{5,7},{6,4},{7,5},{8,10},{9,11},{10,... | collective-permute-start | bytes 786440 | tf_op jit(solution)/shard_map/ppermute | solution.py:400
  71.0 17.6 %copy-start.4 = (f32[32,8]{0,1:T(8,128)S(1)}, f32[32,8]{0,1:T(8,128)}, u32[]{:S(2)}) copy-start(f32[32,8]{0,1:T(8,128)} %param.24) | copy-start | bytes 3076
  71.0 12.1 %collective-permute-start.4 = (bf16[256,256]{1,0:T(8,128)(2,1)S(1)}, bf16[256,256]{1,0:T(8,128)(2,1)S(1)}, u32[]{:S(2)}, u32[]{:S(2)}) collective-permute-start(bf16[256,256]{1,0:T(8,128)(2,1)S(1)} %get-tuple-element.53.a_ref), channel_id=1, source_target_pairs={{0,1},{1,2},{2,3},{3,0},{4,5},{5,6},{6,7},{7,4},{8,9},{9,10},{10,1... | collective-permute-start | bytes 393224 | tf_op jit(solution)/shard_map/ppermute | solution.py:400
  72.1 11.1 %collective-permute-start.5 = (bf16[256,256]{1,0:T(8,128)(2,1)S(1)}, bf16[256,256]{1,0:T(8,128)(2,1)S(1)}, u32[]{:S(2)}, u32[]{:S(2)}) collective-permute-start(bf16[256,256]{1,0:T(8,128)(2,1)S(1)} %get-tuple-element.53.a_ref), channel_id=1, source_target_pairs={{0,3},{1,0},{2,1},{3,2},{4,7},{5,4},{6,5},{7,6},{8,11},{9,8},{10,9... | collective-permute-start | bytes 393224 | tf_op jit(solution)/shard_map/ppermute | solution.py:400
  84.4 15.3 %all-to-all-start.1 = ((bf16[32,16,512]{2,1,0:T(8,128)(2,1)}), bf16[32,16,512]{2,1,0:T(8,128)(2,1)S(1)}, u32[]{:S(2)}, u32[]{:S(2)}) async-start(bf16[32,16,512]{2,1,0:T(8,128)(2,1)} %bitcast.15), calls=%async_computation.1 | async-start | bytes 1048576 | tf_op jit(solution)/shard_map/all_to_all | solution.py:467
